TPU v7x, 128 devices: a whole 4x4x4 slice. The times are simulated.
128 devices in a mesh: dp: 16 (over y, x), seq: 8 (over z, core).
Axes of the slice: x: 4, y: 4, z: 4, core: 2. Of those that a mesh axis runs over, the one named last changes fastest.
Arguments:
- frames: bfloat16 [16, 6144, 1024], P('dp', 'seq'), may hold values from -6 to 6
- cotangent: bfloat16 [16, 6144, 1024], P('dp', 'seq'), may hold values from -6 to 6
- segments: int32 [16, 6144], P('dp', 'seq'), may hold values from 0 to 95, never falling along the last dimension, each value on 1 to 128 neighbouring positions
- w_in: bfloat16 [1024, 2048], P(('dp', 'seq')), may hold values from -0.1875 to 0.1875
- w_out: bfloat16 [1024, 1024], P(('dp', 'seq')), may hold values from -0.1875 to 0.1875
- kernel: bfloat16 [1024, 31], P(('dp', 'seq')), may hold values from -1 to 1
- gain_in: bfloat16 [1024], P(('dp', 'seq')), may hold values from 0.099609375 to 1.8984375
- gain_mid: bfloat16 [1024], P(('dp', 'seq')), may hold values from 0.099609375 to 1.8984375
Outputs:
- block_out: bfloat16 [16, 6144, 1024], P('dp', 'seq')
- input_grad: bfloat16 [16, 6144, 1024], P('dp', 'seq')
- grad_w_in: float32 [1024, 2048], P(('dp', 'seq'))
- grad_w_out: float32 [1024, 1024], P(('dp', 'seq'))
- grad_kernel: float32 [1024, 31], P(('dp', 'seq'))
- grad_gain_in: float32 [1024], P(('dp', 'seq'))
- grad_gain_mid: float32 [1024], P(('dp', 'seq'))
Inputs may be any that keep to these rules, and one draw needn't show every extreme that they name: `segments`: along each recording the ids never fall; each utterance holds 1 to 128 frames, and one holds exactly 128.
All inputs are finite; a program needn't handle non-finite values.
Results may differ from a plain program's by a relative error of at most 0.013.
Values may be sent and summed in bfloat16 or wider, within the bound.
A program may use at most 128 MiB of HBM per device.

v0:
```python
import math

import jax
import jax.numpy as jnp
from jax import lax
from jax.sharding import PartitionSpec as P

EPS = 1e-05
HALF = 15


def with_halo(array, sides, width):
    for axis, dim in sides:
        count, length = (lax.axis_size(axis), array.shape[dim])
        up = [(i, (i + 1) % count) for i in range(count - 1)]
        down = [(j, i) for i, j in up]
        last = lax.slice_in_dim(array, length - width, length, axis=dim)
        first = lax.slice_in_dim(array, 0, width, axis=dim)
        before = lax.ppermute(last, axis, up)
        after = lax.ppermute(first, axis, down)
        array = jnp.concatenate([before, array, after], axis=dim)
    return array


def norm_rows(values, gain):
    mean = jnp.mean(values, axis=-1, keepdims=True)
    centred = values - mean
    inv = lax.rsqrt(jnp.mean(centred * centred, axis=-1, keepdims=True) + EPS)
    normal = centred * inv
    return (normal, inv, normal * gain)


def norm_back(grad_out, normal, inv, gain):
    scaled = grad_out * gain
    return inv * (
        scaled
        - jnp.mean(scaled, -1, keepdims=True)
        - normal * jnp.mean(scaled * normal, -1, keepdims=True)
    )


def block_pass(
    frames, cotangent, seg_pad, widen_glu, widen_grad, w_in, w_out, kernel, gain_in, gain_mid, scale
):
    rows = frames.shape[0]
    width = frames.shape[1]
    taps = kernel.shape[1]
    kern = kernel.astype(jnp.float32)
    centre = seg_pad[HALF : HALF + rows]
    x_val = frames.astype(jnp.float32)
    normal_in, inv_in, scaled_in = norm_rows(x_val, gain_in.astype(jnp.float32))
    ln_in = scaled_in.astype(jnp.bfloat16)
    pre = jnp.dot(ln_in, w_in, preferred_element_type=jnp.float32)
    value = pre[:, :width]
    gate_sig = jax.nn.sigmoid(pre[:, width:])
    glu = (value * gate_sig).astype(jnp.bfloat16)
    glu_pad = widen_glu(glu)
    mixed = jnp.zeros((rows, width), jnp.float32)
    for tap in range(taps):
        same = (seg_pad[tap : tap + rows] == centre)[:, None]
        mixed = mixed + jnp.where(
            same, glu_pad[tap : tap + rows].astype(jnp.float32) * kern[:, tap], 0.0
        )
    gmid = gain_mid.astype(jnp.float32)
    normal_mid, inv_mid, ln_mid = norm_rows(mixed, gmid)
    sig_mid = jax.nn.sigmoid(ln_mid)
    act = (ln_mid * sig_mid).astype(jnp.bfloat16)
    block_out = (x_val + jnp.dot(act, w_out, preferred_element_type=jnp.float32)).astype(
        jnp.bfloat16
    )
    grad_w_out = jnp.dot(act.T, cotangent, preferred_element_type=jnp.float32) * scale
    d_act = jnp.dot(cotangent, w_out.T, preferred_element_type=jnp.float32)
    d_ln_mid = d_act * (sig_mid + ln_mid * sig_mid * (1.0 - sig_mid))
    grad_gain_mid = jnp.sum(d_ln_mid * normal_mid, axis=0) * scale
    d_mixed = norm_back(d_ln_mid, normal_mid, inv_mid, gmid)
    grad_pad = widen_grad(d_mixed)
    d_glu = jnp.zeros((rows, width), jnp.float32)
    kernel_terms = []
    for tap in range(taps):
        same = (seg_pad[tap : tap + rows] == centre)[:, None]
        kernel_terms.append(
            jnp.sum(
                jnp.where(same, glu_pad[tap : tap + rows].astype(jnp.float32) * d_mixed, 0.0),
                axis=0,
            )
        )
        start = 2 * HALF - tap
        back_same = (seg_pad[start : start + rows] == centre)[:, None]
        d_glu = d_glu + jnp.where(back_same, grad_pad[start : start + rows] * kern[:, tap], 0.0)
    grad_kernel = jnp.stack(kernel_terms, axis=1) * scale
    d_pre = jnp.concatenate(
        [d_glu * gate_sig, d_glu * value * gate_sig * (1.0 - gate_sig)], axis=-1
    ).astype(jnp.bfloat16)
    grad_w_in = jnp.dot(ln_in.T, d_pre, preferred_element_type=jnp.float32) * scale
    d_ln_in = jnp.dot(d_pre, w_in.T, preferred_element_type=jnp.float32)
    gin = gain_in.astype(jnp.float32)
    grad_gain_in = jnp.sum(d_ln_in * normal_in, axis=0) * scale
    input_grad = (
        cotangent.astype(jnp.float32) + norm_back(d_ln_in, normal_in, inv_in, gin)
    ).astype(jnp.bfloat16)
    return (
        block_out,
        input_grad,
        (grad_w_in, grad_w_out, grad_kernel, grad_gain_in, grad_gain_mid),
    )


def shards(frames, cotangent, segments, w_in, w_out, kernel, gain_in, gain_mid):
    full = (
        lax.all_gather(w_in, ("dp", "seq"), axis=0, tiled=True),
        lax.all_gather(w_out, ("dp", "seq"), axis=0, tiled=True),
        lax.all_gather(kernel, ("dp", "seq"), axis=0, tiled=True),
        lax.all_gather(gain_in, ("dp", "seq"), axis=0, tiled=True),
        lax.all_gather(gain_mid, ("dp", "seq"), axis=0, tiled=True),
    )
    frame_rows = frames[0]
    cot_rows = cotangent[0]
    rows = frame_rows.shape[0]
    scale = jnp.float32(1.0 / math.sqrt(rows * lax.axis_size("dp") * lax.axis_size("seq")))
    seg_pad = with_halo(segments[0], (("seq", 0),), HALF)
    block_out, input_grad, partial_grads = block_pass(
        frame_rows,
        cot_rows,
        seg_pad,
        lambda values: with_halo(values, (("seq", 0),), HALF),
        lambda values: with_halo(values, (("seq", 0),), HALF),
        full[0],
        full[1],
        full[2],
        full[3],
        full[4],
        scale,
    )
    grads = (
        lax.psum_scatter(partial_grads[0], ("dp", "seq"), scatter_dimension=0, tiled=True),
        lax.psum_scatter(partial_grads[1], ("dp", "seq"), scatter_dimension=0, tiled=True),
        lax.psum_scatter(partial_grads[2], ("dp", "seq"), scatter_dimension=0, tiled=True),
        lax.psum_scatter(partial_grads[3], ("dp", "seq"), scatter_dimension=0, tiled=True),
        lax.psum_scatter(partial_grads[4], ("dp", "seq"), scatter_dimension=0, tiled=True),
    )
    return (block_out[None], input_grad[None], grads[0], grads[1], grads[2], grads[3], grads[4])


def solution(mesh):
    in_specs = (
        P("dp", "seq", None),
        P("dp", "seq", None),
        P("dp", "seq"),
        P(("dp", "seq"), None),
        P(("dp", "seq"), None),
        P(("dp", "seq"), None),
        P(("dp", "seq")),
        P(("dp", "seq")),
    )
    out_specs = (
        P("dp", "seq", None),
        P("dp", "seq", None),
        P(("dp", "seq"), None),
        P(("dp", "seq"), None),
        P(("dp", "seq"), None),
        P(("dp", "seq")),
        P(("dp", "seq")),
    )
    return jax.shard_map(shards, mesh=mesh, in_specs=in_specs, out_specs=out_specs, check_vma=False)
```

profile of v0, /device:TPU:1, one launch (start us, length us, event | category | flops | bytes accessed | tf_op | source)
XLA Modules:
  0.0 1648.3 jit_solution(5624039842010378861)
XLA Ops:
  8.7 4.9 collective-permute-start
  15.6 37.5 %all_gather.17 = bf16[1024,31]{1,0:T(8,128)(2,1)S(1)} all-gather(bf16[8,31]{1,0:T(8,128)(2,1)} %param.13), channel_id=1, replica_groups=mesh['dp'=16,'seq'=8] {'dp','seq'}, dimensions={0}, use_global_device_ids=true | all-gather | bytes 63984 | tf_op jit(solution)/shard_map/all_gather | solution.py:112
  53.2 3.3 slice_reduce_fusion.29
  56.5 5.1 slice_reduce_fusion.30
  62.1 64.9 %all-reduce.6 = (bf16[1024]{0:T(1024)(128)(2,1)S(1)}, bf16[1024]{0:T(1024)(128)(2,1)S(1)}) all-reduce(bf16[1024]{0:T(1024)(128)(2,1)S(1)} %dynamic-update-slice, bf16[1024]{0:T(1024)(128)(2,1)S(1)} %dynamic-update-slice.1), channel_id=1, replica_groups=mesh['dp'=16,'seq'=8] {'dp','seq'}, use_global_device_ids=true, to_apply=%add | all-reduce | flops 2048 | bytes 8192
  128.3 5.3 fusion.296
  136.3 2.1 collective-permute-start.1
  138.3 2.3 collective-permute-start.3
  140.9 3.2 collective-permute-done.3
  144.1 28.9 %fusion.301 = (f32[768]{0:T(1024)S(1)}, f32[768,1024]{1,0:T(8,128)S(1)}) fusion(f32[1024]{0:T(1024)S(1)} %get-tuple-element.59, bf16[15,1024]{1,0:T(8,128)(2,1)S(1)} %collective-permute-done.3, bf16[768,1024]{1,0:T(8,128)(2,1)S(1)} %multiply_convert_fusion.2, pred[768]{0:T(1024)(128)(4,1)S(1)} %get-tuple-element.118, f32[1024]{0:T(1024)S(1)} %get-tuple-element.60, ...), kind=kLoop, calls=%fused_computation.536 | loop fusion | flops 167509248 | bytes 4933120 | tf_op jit(solution)/shard_map/reduce_sum | solution.py:26
  173.6 6.4 multiply_reduce_fusion
  180.0 7.8 fusion.134
  187.8 2.4 fusion.49
  190.2 5.2 fusion.95
  195.5 3.1 fusion.85
  198.6 6.7 fusion.107
  205.3 6.8 fusion.137
  212.2 3.0 fusion.73
  215.3 3.4 fusion.61
  219.7 6.5 convolution_multiply_fusion.1
  226.5 2.2 collective-permute-start.4
  228.7 3.8 collective-permute-start.5
  234.1 27.2 %multiply_convert_fusion.1 = (bf16[768,1024]{1,0:T(8,128)(2,1)}, f32[768,1024]{1,0:T(8,128)}) fusion(f32[768,2048]{1,0:T(8,128)} %copy-done.2, f32[1024]{0:T(1024)S(1)} %get-tuple-element.59, f32[768,1024]{1,0:T(8,128)S(1)} %get-tuple-element.93, f32[15,1024]{1,0:T(8,128)S(1)} %collective-permute-done.5, pred[768]{0:T(1024)(128)(4,1)S(1)} %copy-done.31, ...), kind=kLoop, calls=%fused_computation.408 | loop fusion | flops 99090432 | bytes 11282944 | tf_op jit(solution)/shard_map/convert
  261.3 3.3 multiply_convert_fusion
  265.7 6.4 convolution_multiply_fusion
  274.1 5.2 fusion.292
  279.4 5.4 fusion.14
  284.8 64.7 %all-reduce.5 = (f32[1024]{0:T(1024)S(1)}, f32[1024]{0:T(1024)S(1)}) all-reduce(f32[1024]{0:T(1024)S(1)} %broadcast_multiply_fusion.2, f32[1024]{0:T(1024)S(1)} %broadcast_multiply_fusion.1), channel_id=5, replica_groups=mesh['dp'=16,'seq'=8] {'dp','seq'}, use_global_device_ids=true, to_apply=%region_43.44.clone | all-reduce | flops 2048 | bytes 16384
  350.7 3.6 fusion.261
  354.3 2.6 all-reduce.9.cloned.1.call-done
  358.4 636.3 %reduce-scatter.6.cloned.1.call-done = f32[8,1024]{1,0:T(8,128)} async-done(((f32[1024,1024]{1,0:T(8,128)}), f32[8,1024]{1,0:T(8,128)}) %reduce-scatter.6.cloned.1.call-update) | async-done | bytes 32784 | tf_op jit(solution)/shard_map/reduce_scatter | solution.py:136
  994.8 646.6 %reduce-scatter.4.cloned.1.call-done = f32[8,2048]{1,0:T(8,128)} async-done(((f32[1024,2048]{1,0:T(8,128)}), f32[8,2048]{1,0:T(8,128)}) %reduce-scatter.4.cloned.1.call-update) | async-done | bytes 65552 | tf_op jit(solution)/shard_map/reduce_scatter | solution.py:135
  (234 shorter events, 16.6 us)
Async XLA Ops:
  7.2 121.1 %all-gather.3.cloned.1.call-start = ((), (), s32[]{:S(2)}) async-start(), calls=%async_computation.2 | async-start | bytes 4227072 | tf_op jit(solution)/shard_map/all_gather | solution.py:110
  7.9 165.7 %all-gather.5.cloned.1.call-start = ((), (), s32[]{:S(2)}) async-start(), calls=%async_computation.3 | async-start | bytes 2113536 | tf_op jit(solution)/shard_map/all_gather | solution.py:111
  8.7 119.2 %collective-permute-start = (s32[15]{0:T(128)S(1)}, s32[15]{0:T(128)S(1)}, u32[]{:S(2)}, u32[]{:S(2)}) collective-permute-start(s32[15]{0:T(128)S(1)} %get-tuple-element.134), channel_id=1, source_target_pairs={{0,1},{1,2},{2,3},{3,4},{4,5},{5,6},{6,7},{8,9},{9,10},{10,11},{11... | collective-permute-start | bytes 188 | tf_op jit(solution)/shard_map/ppermute | solution.py:19
  13.6 114.3 %collective-permute-start.2 = (s32[15]{0:T(128)S(1)}, s32[15]{0:T(128)S(1)}, u32[]{:S(2)}, u32[]{:S(2)}) collective-permute-start(s32[15]{0:T(128)S(1)} %get-tuple-element.135), channel_id=1, source_target_pairs={{1,0},{2,1},{3,2},{4,3},{5,4},{6,5},{7,6},{9,8},{10,9},{11,10},{12... | collective-permute-start | bytes 188 | tf_op jit(solution)/shard_map/ppermute | solution.py:20
  15.6 341.4 %all-reduce.9.cloned.1.call-start = ((), (), s32[]{:S(2)}) async-start(), calls=%async_computation.6 | async-start | bytes 262144
  56.5 70.5 %copy-start.5 = (bf16[1,768,1024]{2,1,0:T(8,128)(2,1)S(1)}, bf16[1,768,1024]{2,1,0:T(8,128)(2,1)}, u32[]{:S(2)}) copy-start(bf16[1,768,1024]{2,1,0:T(8,128)(2,1)} %param.8) | copy-start | bytes 4718596
  61.6 66.2 %copy-start.84 = (s32[1,768]{1,0:T(1,128)S(1)}, s32[1,768]{1,0:T(1,128)}, u32[]{:S(2)}) copy-start(s32[1,768]{1,0:T(1,128)} %param.10) | copy-start | bytes 9220
  128.1 59.7 %copy-start.30 = (pred[768]{0:T(1024)(128)(4,1)}, pred[768]{0:T(1024)(128)(4,1)S(1)}, u32[]{:S(2)}) copy-start(pred[768]{0:T(1024)(128)(4,1)S(1)} %get-tuple-element.102) | copy-start | bytes 2308
  128.1 59.7 %copy-start.60 = (pred[768]{0:T(1024)(128)(4,1)}, pred[768]{0:T(1024)(128)(4,1)S(1)}, u32[]{:S(2)}) copy-start(pred[768]{0:T(1024)(128)(4,1)S(1)} %get-tuple-element.115) | copy-start | bytes 2308
  128.1 59.7 %copy-start.62 = (pred[768]{0:T(1024)(128)(4,1)}, pred[768]{0:T(1024)(128)(4,1)S(1)}, u32[]{:S(2)}) copy-start(pred[768]{0:T(1024)(128)(4,1)S(1)} %get-tuple-element.116) | copy-start | bytes 2308
  128.1 67.3 %copy-start.32 = (pred[768]{0:T(1024)(128)(4,1)}, pred[768]{0:T(1024)(128)(4,1)S(1)}, u32[]{:S(2)}) copy-start(pred[768]{0:T(1024)(128)(4,1)S(1)} %get-tuple-element.103) | copy-start | bytes 2308
  128.2 67.3 %copy-start.34 = (pred[768]{0:T(1024)(128)(4,1)}, pred[768]{0:T(1024)(128)(4,1)S(1)}, u32[]{:S(2)}) copy-start(pred[768]{0:T(1024)(128)(4,1)S(1)} %get-tuple-element.104) | copy-start | bytes 2308
  128.2 67.3 %copy-start.36 = (pred[768]{0:T(1024)(128)(4,1)}, pred[768]{0:T(1024)(128)(4,1)S(1)}, u32[]{:S(2)}) copy-start(pred[768]{0:T(1024)(128)(4,1)S(1)} %get-tuple-element.105) | copy-start | bytes 2308
  128.2 67.3 %copy-start.38 = (pred[768]{0:T(1024)(128)(4,1)}, pred[768]{0:T(1024)(128)(4,1)S(1)}, u32[]{:S(2)}) copy-start(pred[768]{0:T(1024)(128)(4,1)S(1)} %get-tuple-element.106) | copy-start | bytes 2308
  128.2 84.0 %copy-start.40 = (pred[768]{0:T(1024)(128)(4,1)}, pred[768]{0:T(1024)(128)(4,1)S(1)}, u32[]{:S(2)}) copy-start(pred[768]{0:T(1024)(128)(4,1)S(1)} %get-tuple-element.107) | copy-start | bytes 2308
  128.2 84.0 %copy-start.42 = (pred[768]{0:T(1024)(128)(4,1)}, pred[768]{0:T(1024)(128)(4,1)S(1)}, u32[]{:S(2)}) copy-start(pred[768]{0:T(1024)(128)(4,1)S(1)} %get-tuple-element.108) | copy-start | bytes 2308
  128.2 84.0 %copy-start.44 = (pred[768]{0:T(1024)(128)(4,1)}, pred[768]{0:T(1024)(128)(4,1)S(1)}, u32[]{:S(2)}) copy-start(pred[768]{0:T(1024)(128)(4,1)S(1)} %get-tuple-element.109) | copy-start | bytes 2308
  128.2 84.0 %copy-start.46 = (pred[768]{0:T(1024)(128)(4,1)}, pred[768]{0:T(1024)(128)(4,1)S(1)}, u32[]{:S(2)}) copy-start(pred[768]{0:T(1024)(128)(4,1)S(1)} %get-tuple-element.110) | copy-start | bytes 2308
  136.3 4.6 collective-permute-start.1
  138.3 5.7 collective-permute-start.3
  140.8 39.2 %copy-start.16 = (pred[768]{0:T(1024)(128)(4,1)}, pred[768]{0:T(1024)(128)(4,1)S(1)}, u32[]{:S(2)}) copy-start(pred[768]{0:T(1024)(128)(4,1)S(1)} %get-tuple-element.119) | copy-start | bytes 2308
  140.8 49.4 %copy-start.64 = (pred[768]{0:T(1024)(128)(4,1)}, pred[768]{0:T(1024)(128)(4,1)S(1)}, u32[]{:S(2)}) copy-start(pred[768]{0:T(1024)(128)(4,1)S(1)} %get-tuple-element.117) | copy-start | bytes 2308
  140.8 64.5 %copy-start.14 = (pred[768]{0:T(1024)(128)(4,1)}, pred[768]{0:T(1024)(128)(4,1)S(1)}, u32[]{:S(2)}) copy-start(pred[768]{0:T(1024)(128)(4,1)S(1)} %get-tuple-element.118) | copy-start | bytes 2308
  140.8 64.5 %copy-start.18 = (pred[768]{0:T(1024)(128)(4,1)}, pred[768]{0:T(1024)(128)(4,1)S(1)}, u32[]{:S(2)}) copy-start(pred[768]{0:T(1024)(128)(4,1)S(1)} %get-tuple-element.120) | copy-start | bytes 2308
  140.8 64.5 %copy-start.20 = (pred[768]{0:T(1024)(128)(4,1)}, pred[768]{0:T(1024)(128)(4,1)S(1)}, u32[]{:S(2)}) copy-start(pred[768]{0:T(1024)(128)(4,1)S(1)} %get-tuple-element.121) | copy-start | bytes 2308
  140.8 64.5 %copy-start.22 = (pred[768]{0:T(1024)(128)(4,1)}, pred[768]{0:T(1024)(128)(4,1)S(1)}, u32[]{:S(2)}) copy-start(pred[768]{0:T(1024)(128)(4,1)S(1)} %get-tuple-element.122) | copy-start | bytes 2308
  219.6 775.2 %reduce-scatter.6.cloned.1.call-start = ((), (), s32[]{:S(2)}) async-start(), calls=%async_computation.5 | async-start | bytes 4227072 | tf_op jit(solution)/shard_map/reduce_scatter | solution.py:136
  226.4 1415.0 %reduce-scatter.4.cloned.1.call-start = ((), (), s32[]{:S(2)}) async-start(), calls=%async_computation.4 | async-start | bytes 8454144 | tf_op jit(solution)/shard_map/reduce_scatter | solution.py:135
  226.5 6.0 collective-permute-start.4
  228.7 5.1 collective-permute-start.5
  279.3 71.3 %copy-start.8 = (bf16[1,768,1024]{2,1,0:T(8,128)(2,1)S(1)}, bf16[1,768,1024]{2,1,0:T(8,128)(2,1)}, u32[]{:S(2)}) copy-start(bf16[1,768,1024]{2,1,0:T(8,128)(2,1)} %param.8) | copy-start | bytes 4718596
  279.4 71.3 %copy-start.9 = (bf16[1,768,1024]{2,1,0:T(8,128)(2,1)S(1)}, bf16[1,768,1024]{2,1,0:T(8,128)(2,1)}, u32[]{:S(2)}) copy-start(bf16[1,768,1024]{2,1,0:T(8,128)(2,1)} %param.9) | copy-start | bytes 4718596
  (70 other events, 802.8 us)
Sparse Core Ops, SparseCore 0:
  11.2 70.5 all-gather.2
  84.9 62.7 all-gather.4
  219.7 137.2 all-reduce.8
  359.9 634.8 reduce-scatter.5
  997.6 643.7 reduce-scatter.3
where the time goes:
time: 1660 us; the launch traced here: 1650 us
  waiting for transfers between devices  1290 us (78%)
  blocking collectives  167 us (10%)
  other arithmetic  104 us (6%)
  matrix products  35.3 us (2%)
  local copies, waits for them, and re-layouts  17.7 us (1%)
  starting transfers between devices  17.3 us (1%)
    reduce_scatter x1, waiting for transfers between devices, shards(): lax.psum_scatter(partial_grads[0], ('dp', 'seq'), scatter_dimension=0, ti...  647 us
    reduce_scatter x1, waiting for transfers between devices, shards(): lax.psum_scatter(partial_grads[1], ('dp', 'seq'), scatter_dimension=0, ti...  636 us
    unnamed x2, blocking collectives  130 us
    reduce_sum x8, other arithmetic, block_pass(): jnp.sum(jnp.where(same, glu_pad[tap:tap + rows].astype(jnp.float32) * d_m...  38.3 us
    all_gather x1, blocking collectives, shards(): lax.all_gather(kernel, ('dp', 'seq'), axis=0, tiled=True)  37.5 us
  transfers between devices with their start and end apart: 11, of which 5 were waited for; matrix products, arithmetic and copies ran while one was open for 6% of the time, Pallas kernels for 0%

commit v1 on v0

--- a/solution.py
+++ b/solution.py
@@ -3,7 +3,375 @@
 import jax
 import jax.numpy as jnp
 from jax import lax
+from jax.experimental import pallas as pl
+from jax.experimental.pallas import tpu as pltpu
 from jax.sharding import PartitionSpec as P
+
+MESH = pl.DeviceIdType.MESH
+HALFW = 1664
+WIDE = 2 * HALFW
+PARTS = ((0, 512, 256), (512, 512, 256), (1024, 640, 384))
+ORDERS = (("z", "x", "y"), ("x", "y", "z"), ("y", "z", "x"))
+HALO = 32
+
+
+def place():
+    d, s = lax.axis_index("dp"), lax.axis_index("seq")
+    return {"y": d // 4, "x": d % 4, "z": s // 2}, s % 2
+
+
+def dev(coords, core):
+    return (coords["y"] * 4 + coords["x"], coords["z"] * 2 + core)
+
+
+def moved(coords, axis, by):
+    out = dict(coords)
+    out[axis] = (coords[axis] + by + 4) % 4
+    return out
+
+
+def greet(targets):
+    barrier = pltpu.get_barrier_semaphore()
+    for t in targets:
+        pl.semaphore_signal(barrier, inc=1, device_id=t, device_id_type=MESH)
+    pl.semaphore_wait(barrier, len(targets))
+
+
+def block_index(coords, full, axis, value):
+    out = []
+    for a in ("y", "x", "z"):
+        if a == axis:
+            out.append(value)
+        elif a in full:
+            out.append(slice(None))
+        else:
+            out.append(coords[a])
+    return tuple(out)
+
+
+def gather_kernel(
+    shard_ref, frames_ref, cot_ref, seg_ref,
+    out_ref, hf_ref, hc_ref, hs_ref,
+    buf, sib, sib_sem, halo_send, halo_recv, a_send, a_recv, s_send, s_recv, out_sem,
+):
+    me, core = place()
+    sibling = dev(me, 1 - core)
+    right = (lax.axis_index("dp"), (lax.axis_index("seq") + 1) % 8)
+    left = (lax.axis_index("dp"), (lax.axis_index("seq") + 7) % 8)
+    cross = dev(moved(me, "z", 2 * core - 1), 1 - core)
+    targets = [dev(moved(me, a, b), core) for a in "yxz" for b in (1, -1)]
+    greet(targets + [sibling, cross])
+
+    first = pltpu.make_async_remote_copy(
+        src_ref=shard_ref, dst_ref=sib, send_sem=sib_sem.at[0], recv_sem=sib_sem.at[1],
+        device_id=sibling, device_id_type=MESH)
+    first.start()
+    halos = []
+    rows = frames_ref.shape[0]
+    for n, (src, dst, h) in enumerate(((frames_ref, hf_ref, HALO), (cot_ref, hc_ref, 16), (seg_ref, hs_ref, HALO))):
+        for m, (at, to, who) in enumerate(((rows - h, 0, right), (0, h, left))):
+            cp = pltpu.make_async_remote_copy(
+                src_ref=src.at[pl.ds(at, h)], dst_ref=dst.at[pl.ds(to, h)],
+                send_sem=halo_send.at[n, m], recv_sem=halo_recv.at[n, m],
+                device_id=who, device_id_type=MESH)
+            halos.append(cp)
+    first.wait()
+    mine, other = shard_ref[...], sib[...]
+    low = jnp.where(core == 0, mine[:, :HALFW], other[:, HALFW:])
+    high = jnp.where(core == 0, other[:, :HALFW], mine[:, HALFW:])
+    buf[me["y"], me["x"], me["z"], :, pl.ds(pl.multiple_of(core * HALFW, 128), HALFW)] = jnp.concatenate(
+        [low, high], axis=0).astype(jnp.bfloat16)
+    for cp in halos:
+        cp.start()
+
+    def cols(p, lo, width, c=core):
+        return pl.ds(pl.multiple_of(c * HALFW + PARTS[p][0] + lo, 128), width)
+
+    def send(p, ph, which, idx, lo, width, by):
+        axis = ORDERS[p][ph]
+        ref = buf.at[idx + (slice(None), cols(p, lo, width))]
+        return pltpu.make_async_remote_copy(
+            src_ref=ref, dst_ref=ref, send_sem=a_send.at[p, ph, which], recv_sem=a_recv.at[p, ph, which],
+            device_id=dev(moved(me, axis, by), core), device_id_type=MESH)
+
+    def to_sibling(p, which, idx, c=core):
+        start, width, _ = PARTS[p]
+        ref = buf.at[idx + (slice(None), cols(p, 0, width, c))]
+        return pltpu.make_async_remote_copy(
+            src_ref=ref, dst_ref=ref, send_sem=s_send.at[p, which], recv_sem=s_recv.at[p, which],
+            device_id=sibling, device_id_type=MESH)
+
+    def block(p, ph, by):
+        axis = ORDERS[p][ph]
+        return block_index(me, ORDERS[p][:ph], axis, (me[axis] + by + 4) % 4)
+
+    sends = []
+    for ph in range(3):
+        for p in range(3):
+            _, width, half = PARTS[p]
+            if ph > 0:
+                opp = block(p, ph - 1, 2)
+                send(p, ph - 1, 2, opp, 0, half, 1).wait_recv()
+                send(p, ph - 1, 3, opp, half, width - half, -1).wait_recv()
+            own = block(p, ph, 0)
+            for which, by in ((0, 1), (1, -1)):
+                cp = send(p, ph, which, own, 0, width, by)
+                cp.start()
+                sends.append(cp)
+            if ph == 2:
+                cp = to_sibling(p, 0, own)
+                cp.start()
+                sends.append(cp)
+        for p in range(3):
+            _, width, half = PARTS[p]
+            for which, by, lo, w in ((0, -1, 0, half), (1, 1, half, width - half)):
+                idx = block(p, ph, by)
+                send(p, ph, which, idx, 0, width, -by).wait_recv()
+                cp = send(p, ph, which + 2, idx, lo, w, -by)
+                cp.start()
+                sends.append(cp)
+                if ph == 2:
+                    cp = to_sibling(p, 1 + which, idx)
+                    cp.start()
+                    sends.append(cp)
+    for p in range(3):
+        _, width, half = PARTS[p]
+        opp = block(p, 2, 2)
+        send(p, 2, 2, opp, 0, half, 1).wait_recv()
+        send(p, 2, 3, opp, half, width - half, -1).wait_recv()
+        cp = to_sibling(p, 3, opp)
+        cp.start()
+        sends.append(cp)
+    for p in range(3):
+        for which, by in ((0, 0), (1, -1), (2, 1), (3, 2)):
+            to_sibling(p, which, block(p, 2, by), 1 - core).wait_recv()
+    out = pltpu.make_async_copy(buf, out_ref, out_sem)
+    out.start()
+    for cp in sends:
+        cp.wait_send()
+    for cp in halos:
+        cp.wait()
+    out.wait()
+
+
+def gather(shard, frames, cot, seg):
+    bf = jnp.bfloat16
+    vm = pl.BlockSpec(memory_space=pltpu.VMEM)
+    hbm = pl.BlockSpec(memory_space=pl.ANY)
+    return pl.pallas_call(
+        gather_kernel,
+        out_shape=(
+            jax.ShapeDtypeStruct((4, 4, 4, 16, WIDE), bf),
+            jax.ShapeDtypeStruct((2 * HALO, 1024), bf),
+            jax.ShapeDtypeStruct((32, 1024), bf),
+            jax.ShapeDtypeStruct((2 * HALO, 128), bf),
+        ),
+        in_specs=[vm, hbm, hbm, hbm],
+        out_specs=(hbm, vm, vm, vm),
+        scratch_shapes=[
+            pltpu.VMEM((4, 4, 4, 16, WIDE), bf),
+            pltpu.VMEM((8, WIDE), jnp.float32),
+            pltpu.SemaphoreType.DMA((2,)),
+            pltpu.SemaphoreType.DMA((3, 2)),
+            pltpu.SemaphoreType.DMA((3, 2)),
+            pltpu.SemaphoreType.DMA((3, 3, 4)),
+            pltpu.SemaphoreType.DMA((3, 3, 4)),
+            pltpu.SemaphoreType.DMA((3, 4)),
+            pltpu.SemaphoreType.DMA((3, 4)),
+            pltpu.SemaphoreType.DMA,
+        ],
+        compiler_params=pltpu.CompilerParams(
+            collective_id=0, has_side_effects=True, vmem_limit_bytes=24 << 20),
+        name="gather_weights",
+    )(shard, frames, cot, seg)
+
+
+def shapes_of(full):
+    return tuple(4 if a in full else 1 for a in "yxz")
+
+
+def scatter_kernel(
+    g_ref, out_ref,
+    acc, sibbuf, h0, h1, h2, f0, f1, f2, last, low, fin, own_sem, d_send, d_recv, a_send, a_recv, e_sem,
+):
+    me, core = place()
+    sibling = dev(me, 1 - core)
+    targets = [dev(moved(me, a, b), core) for a in "yxz" for b in (1, -1)]
+    greet(targets + [sibling])
+    hbufs, fbufs = (h0, h1, h2), (f0, f1, f2)
+
+    def cols(p, c):
+        return pl.ds(pl.multiple_of(c * HALFW + PARTS[p][0], 128), PARTS[p][1])
+
+    def lane(p, lo, w):
+        return pl.ds(PARTS[p][0] + lo, w)
+
+    full3 = (slice(None),) * 4
+    owns, gives, sends = [], [], []
+    for p in range(3):
+        give = pltpu.make_async_remote_copy(
+            src_ref=g_ref.at[full3 + (cols(p, 1 - core),)], dst_ref=sibbuf.at[full3 + (lane(p, 0, PARTS[p][1]),)],
+            send_sem=d_send.at[p], recv_sem=d_recv.at[p], device_id=sibling, device_id_type=MESH)
+        give.start()
+        own = pltpu.make_async_copy(
+            g_ref.at[full3 + (cols(p, core),)], acc.at[full3 + (lane(p, 0, PARTS[p][1]),)], own_sem.at[p])
+        own.start()
+        owns.append(own)
+        gives.append(give)
+
+    def axis_of(p, ph):
+        return ORDERS[p][2 - ph]
+
+    def rest(p, ph):
+        return ORDERS[p][: 2 - ph]
+
+    def block(p, ph, by):
+        axis = axis_of(p, ph)
+        return block_index(me, rest(p, ph), axis, (me[axis] + by + 4) % 4)
+
+    def hview(p, ph, lo, w):
+        nd = 2 - ph
+        return hbufs[ph].at[(slice(None),) * nd + (slice(None), lane(p, lo, w))]
+
+    def fview(p, ph, which, lo, w):
+        nd = 2 - ph
+        return fbufs[ph].at[(which,) + (slice(None),) * nd + (slice(None), lane(p, lo, w))]
+
+    def send_half(p, ph, which):
+        _, width, half = PARTS[p]
+        lo, w, by = ((0, half, 1), (half, width - half, -1))[which]
+        return pltpu.make_async_remote_copy(
+            src_ref=acc.at[block(p, ph, 2) + (slice(None), lane(p, lo, w))], dst_ref=hview(p, ph, lo, w),
+            send_sem=a_send.at[p, ph, which], recv_sem=a_recv.at[p, ph, which],
+            device_id=dev(moved(me, axis_of(p, ph), by), core), device_id_type=MESH)
+
+    def send_full(p, ph, which):
+        _, width, _ = PARTS[p]
+        by = (1, -1)[which]
+        return pltpu.make_async_remote_copy(
+            src_ref=acc.at[block(p, ph, by) + (slice(None), lane(p, 0, width))], dst_ref=fview(p, ph, which, 0, width),
+            send_sem=a_send.at[p, ph, 2 + which], recv_sem=a_recv.at[p, ph, 2 + which],
+            device_id=dev(moved(me, axis_of(p, ph), by), core), device_id_type=MESH)
+
+    def over(p, ph, value_axis_index, body):
+        names = rest(p, ph)
+        axis = axis_of(p, ph)
+        n = 4 ** len(names)
+
+        def index(k):
+            digits = [k // 4, k % 4][2 - len(names):] if names else []
+            by_name = dict(zip([a for a in "yxz" if a in names], digits))
+            at = []
+            for a in "yxz":
+                at.append(by_name[a] if a in by_name else (value_axis_index if a == axis else me[a]))
+            return tuple(at), tuple(digits)
+
+        if n == 1:
+            body(*index(0))
+        else:
+            def step(k, carry):
+                body(*index(k))
+                return carry
+            lax.fori_loop(0, n, step, 0)
+
+    f32 = jnp.float32
+    for p in range(3):
+        start, width, half = PARTS[p]
+        owns[p].wait()
+        gives[p].wait_recv()
+        sl = pl.ds(start, width)
+
+        def body(k, carry, sl=sl):
+            at = (k // 16, (k // 4) % 4, k % 4, slice(None), sl)
+            acc[at] = (acc[at].astype(f32) + sibbuf[at].astype(f32)).astype(jnp.bfloat16)
+            return carry
+        lax.fori_loop(0, 64, body, 0)
+        for which in (0, 1):
+            cp = send_half(p, 0, which)
+            cp.start()
+            sends.append(cp)
+    for ph in range(3):
+        for p in range(3):
+            start, width, half = PARTS[p]
+            axis = axis_of(p, ph)
+            for which, by, lo, w in ((0, 1, 0, half), (1, -1, half, width - half)):
+                send_half(p, ph, which).wait_recv()
+                sl = pl.ds(start + lo, w)
+
+                def body(at, dig, ph=ph, sl=sl):
+                    at = at + (slice(None), sl)
+                    hat = dig + (slice(None), sl)
+                    acc[at] = (acc[at].astype(f32) + hbufs[ph][hat].astype(f32)).astype(jnp.bfloat16)
+                over(p, ph, (me[axis] + by + 4) % 4, body)
+                cp = send_full(p, ph, which)
+                cp.start()
+                sends.append(cp)
+        for p in range(3):
+            start, width, half = PARTS[p]
+            axis = axis_of(p, ph)
+            for which in (0, 1):
+                send_full(p, ph, which).wait_recv()
+            sl = pl.ds(start, width)
+
+            def body(at, dig, ph=ph, sl=sl):
+                at = at + (slice(None), sl)
+                total = (acc[at].astype(f32) + fbufs[ph][(0,) + dig + (slice(None), sl)].astype(f32)
+                         + fbufs[ph][(1,) + dig + (slice(None), sl)].astype(f32))
+                if ph < 2:
+                    acc[at] = total.astype(jnp.bfloat16)
+                else:
+                    last[:, sl] = total
+            over(p, ph, me[axis], body)
+            if ph < 2:
+                for which in (0, 1):
+                    cp = send_half(p, ph + 1, which)
+                    cp.start()
+                    sends.append(cp)
+    top, bottom = last[0:8, :], last[8:16, :]
+    low[...] = jnp.where(core == 0, bottom, top)
+    swap = pltpu.make_async_remote_copy(
+        src_ref=low, dst_ref=fin, send_sem=e_sem.at[0], recv_sem=e_sem.at[1], device_id=sibling, device_id_type=MESH)
+    swap.start()
+    mine = jnp.where(core == 0, top, bottom)
+    swap.wait()
+    theirs = fin[...]
+    out_ref[:, :HALFW] = jnp.where(core == 0, mine, theirs)
+    out_ref[:, HALFW:] = jnp.where(core == 0, theirs, mine)
+    for cp in sends + gives:
+        cp.wait_send()
+
+
+def scatter(g):
+    bf = jnp.bfloat16
+    return pl.pallas_call(
+        scatter_kernel,
+        out_shape=jax.ShapeDtypeStruct((8, WIDE), jnp.float32),
+        in_specs=[pl.BlockSpec(memory_space=pl.ANY)],
+        out_specs=pl.BlockSpec(memory_space=pltpu.VMEM),
+        scratch_shapes=[
+            pltpu.VMEM((4, 4, 4, 16, HALFW), bf),
+            pltpu.VMEM((4, 4, 4, 16, HALFW), bf),
+            pltpu.VMEM((4, 4, 16, HALFW), bf),
+            pltpu.VMEM((4, 16, HALFW), bf),
+            pltpu.VMEM((16, HALFW), bf),
+            pltpu.VMEM((2, 4, 4, 16, HALFW), bf),
+            pltpu.VMEM((2, 4, 16, HALFW), bf),
+            pltpu.VMEM((2, 16, HALFW), bf),
+            pltpu.VMEM((16, HALFW), jnp.float32),
+            pltpu.VMEM((8, HALFW), jnp.float32),
+            pltpu.VMEM((8, HALFW), jnp.float32),
+            pltpu.SemaphoreType.DMA((3,)),
+            pltpu.SemaphoreType.DMA((3,)),
+            pltpu.SemaphoreType.DMA((3,)),
+            pltpu.SemaphoreType.DMA((3, 3, 4)),
+            pltpu.SemaphoreType.DMA((3, 3, 4)),
+            pltpu.SemaphoreType.DMA((2,)),
+        ],
+        compiler_params=pltpu.CompilerParams(
+            collective_id=1, has_side_effects=True, vmem_limit_bytes=32 << 20),
+        name="scatter_grads",
+    )(g)
+
 
 EPS = 1e-05
 HALF = 15
@@ -106,39 +474,42 @@
 
 
 def shards(frames, cotangent, segments, w_in, w_out, kernel, gain_in, gain_mid):
-    full = (
-        lax.all_gather(w_in, ("dp", "seq"), axis=0, tiled=True),
-        lax.all_gather(w_out, ("dp", "seq"), axis=0, tiled=True),
-        lax.all_gather(kernel, ("dp", "seq"), axis=0, tiled=True),
-        lax.all_gather(gain_in, ("dp", "seq"), axis=0, tiled=True),
-        lax.all_gather(gain_mid, ("dp", "seq"), axis=0, tiled=True),
-    )
     frame_rows = frames[0]
     cot_rows = cotangent[0]
     rows = frame_rows.shape[0]
-    scale = jnp.float32(1.0 / math.sqrt(rows * lax.axis_size("dp") * lax.axis_size("seq")))
-    seg_pad = with_halo(segments[0], (("seq", 0),), HALF)
+    f32 = jnp.float32
+    packed = jnp.concatenate(
+        [w_in.astype(f32), w_out.astype(f32), kernel.astype(f32), gain_in.astype(f32)[:, None],
+         gain_mid.astype(f32)[:, None], jnp.zeros((8, WIDE - 3072 - 33), f32)], axis=1)
+    seg_rows = jnp.broadcast_to(segments[0].astype(jnp.bfloat16)[:, None], (rows, 128))
+    full, _, _, seg_halo = gather(packed, frame_rows, cot_rows, seg_rows)
+    full = full.reshape(1024, WIDE)
+    scale = jnp.float32(1.0 / math.sqrt(rows * 128))
+    at = lax.axis_index("seq")
+    halo = seg_halo[:, 0].astype(jnp.int32)
+    seg_pad = jnp.concatenate([
+        jnp.where(at == 0, -1, halo[HALO - HALF : HALO]), segments[0],
+        jnp.where(at == 7, -1, halo[HALO : HALO + HALF])])
     block_out, input_grad, partial_grads = block_pass(
         frame_rows,
         cot_rows,
         seg_pad,
         lambda values: with_halo(values, (("seq", 0),), HALF),
         lambda values: with_halo(values, (("seq", 0),), HALF),
-        full[0],
-        full[1],
-        full[2],
-        full[3],
-        full[4],
+        full[:, :2048],
+        full[:, 2048:3072],
+        full[:, 3072:3103],
+        full[:, 3103],
+        full[:, 3104],
         scale,
     )
-    grads = (
-        lax.psum_scatter(partial_grads[0], ("dp", "seq"), scatter_dimension=0, tiled=True),
-        lax.psum_scatter(partial_grads[1], ("dp", "seq"), scatter_dimension=0, tiled=True),
-        lax.psum_scatter(partial_grads[2], ("dp", "seq"), scatter_dimension=0, tiled=True),
-        lax.psum_scatter(partial_grads[3], ("dp", "seq"), scatter_dimension=0, tiled=True),
-        lax.psum_scatter(partial_grads[4], ("dp", "seq"), scatter_dimension=0, tiled=True),
-    )
-    return (block_out[None], input_grad[None], grads[0], grads[1], grads[2], grads[3], grads[4])
+    bf = jnp.bfloat16
+    g = jnp.concatenate([
+        partial_grads[0].astype(bf), partial_grads[1].astype(bf), partial_grads[2].astype(bf),
+        partial_grads[3].astype(bf)[:, None], partial_grads[4].astype(bf)[:, None],
+        jnp.zeros((1024, WIDE - 3072 - 33), bf)], axis=1).reshape(4, 4, 4, 16, WIDE)
+    r = scatter(g)
+    return (block_out[None], input_grad[None], r[:, :2048], r[:, 2048:3072], r[:, 3072:3103], r[:, 3103], r[:, 3104])
 
 
 def solution(mesh):

time: 1660 us -> 417 us (0.25)
  waiting for transfers between devices: 1290 us -> 0.01 us
  blocking collectives: 167 us -> 0 us
  other arithmetic: 104 us -> 209 us
  Pallas kernels: 0 us -> 80.7 us
  local copies, waits for them, and re-layouts: 17.7 us -> 78 us
    reduce_scatter x2 -> x0, waiting for transfers between devices: 1280 us -> none  [the longest x1 647 us: shards(): lax.psum_scatter(partial_grads[0], ('dp', 'seq'), scatter_dimension=0, ti...]
    unnamed x2 -> x0, blocking collectives: 130 us -> none
    pallas_call x0 -> x2, Pallas kernels: none -> 80.7 us  [the longest x1 40.6 us: scatter(): pl.pallas_call(scatter_kernel, out_shape=jax.ShapeDtypeStruct((8, WIDE),...]
    another operation x2, other arithmetic: 30.5 us -> 81.3 us
    another operation x1 -> x32, local copies, waits for them, and re-layouts: 0.24 us -> 45.6 us  [block_pass(): grad_kernel = jnp.stack(kernel_terms, axis=1) * scale]
    all_gather x1 -> x0, blocking collectives: 37.5 us -> none  [shards(): lax.all_gather(kernel, ('dp', 'seq'), axis=0, tiled=True)]
    reduce_sum x2, other arithmetic: 29.2 us -> 55.5 us  [norm_rows(): mean = jnp.mean(values, axis=-1, keepdims=True)]
    reduce_sum x8, other arithmetic: 38.3 us -> 61.3 us  [block_pass(): jnp.sum(jnp.where(same, glu_pad[tap:tap + rows].astype(jnp.float32) * d_m...]
  transfers between devices with their start and end apart: 11 -> 4, of which waited for: 5 -> 0; matrix products, arithmetic and copies ran while one was open for 6% -> 26% of each run, Pallas kernels for 0% -> 0%
where the time goes in v1:
time: 417 us; the launch traced here: 411 us
  other arithmetic  209 us (50%)
  Pallas kernels  80.7 us (19%)
  local copies, waits for them, and re-layouts  78 us (19%)
  matrix products  31.9 us (8%)
  starting transfers between devices  10.4 us (2%)
    another operation x2, other arithmetic  81.3 us
    reduce_sum x8, other arithmetic, block_pass(): jnp.sum(jnp.where(same, glu_pad[tap:tap + rows].astype(jnp.float32) * d_m...  61.3 us
    reduce_sum x2, other arithmetic, norm_rows(): mean = jnp.mean(values, axis=-1, keepdims=True)  55.5 us
    another operation x32, local copies, waits for them, and re-layouts, block_pass(): grad_kernel = jnp.stack(kernel_terms, axis=1) * scale  45.6 us
    pallas_call x1, Pallas kernels, scatter(): pl.pallas_call(scatter_kernel, out_shape=jax.ShapeDtypeStruct((8, WIDE),...  40.6 us
    pallas_call x1, Pallas kernels, gather(): pl.pallas_call(gather_kernel, out_shape=(jax.ShapeDtypeStruct((4, 4, 4, 1...  40.1 us
    unnamed x109, local copies, waits for them, and re-layouts  12.1 us
    concatenate x1, local copies, waits for them, and re-layouts, shards(): jnp.concatenate([partial_grads[0].astype(bf), partial_grads[1].astype(bf)...  11 us
  transfers between devices with their start and end apart: 4, of which 0 were waited for; matrix products, arithmetic and copies ran while one was open for 26% of the time, Pallas kernels for 0%

profile of v1, /device:TPU:1, one launch (start us, length us, event | category | flops | bytes accessed | tf_op | source)
XLA Modules:
  0.0 411.3 jit_solution(9293507963357578045)
XLA Ops:
  2.8 1.8 convert_reduce_fusion
  7.1 1.4 copy-done.3
  8.5 40.1 %gather_weights.1 = (bf16[4,4,4,16,3328]{4,3,2,1,0:T(8,128)(2,1)S(1)}, bf16[64,1024]{1,0:T(8,128)(2,1)}, bf16[32,1024]{1,0:T(8,128)(2,1)}, bf16[64,128]{1,0:T(8,128)(2,1)S(1)}) custom-call(f32[8,3328]{1,0:T(8,128)S(1)} %concatenate.121.shard_ref, bf16[768,1024]{1,0:T(8,128)(2,1)S(1)} %bitcast.68, bf16[768,1024]{1,0:T(8,128)(2,1)S(1)} %bitcast.69, ...), custom_call_target="tpu_custom_call" | custom-call | tf_op jit(solution)/shard_map/gather_weights/pallas_call | solution.py:161
  48.6 2.8 copy-done.5
  52.3 5.3 %fusion.8 = f32[768,2048]{1,0:T(8,128)S(1)} fusion(bf16[1024,3328]{1,0:T(8,128)(2,1)} %bitcast.71, f32[1024]{0:T(1024)S(1)} %bitcast.140, f32[768]{0:T(1024)S(1)} %add_rsqrt_fusion.1, f32[768]{0:T(1024)S(1)} %broadcast_multiply_fusion.5, bf16[1,768,1024]{2,1,0:T(8,128)(2,1)S(1)} %copy-done.2), kind=kOutput, calls=%fused_computation.131 | convolution fusion | flops 3225157632 | bytes 12068864 | tf_op jit(solution)/shard_map/dot_general | solution.py:421
  58.6 1.7 copy-done.9
  61.5 1.9 collective-permute-start.1
  63.4 4.2 %collective-permute-start = (bf16[15,1024]{1,0:T(8,128)(2,1)S(1)}, bf16[15,1024]{1,0:T(8,128)(2,1)S(1)}, u32[]{:S(2)}, u32[]{:S(2)}) collective-permute-start(bf16[15,1024]{1,0:T(8,128)(2,1)S(1)} %get-tuple-element.62), channel_id=1, source_target_pairs={{0,1},{1,2},{2,3},{3,4},{4,5},{5,6},{6,7},{8,9},{9,10},{10,11},{11... | collective-permute-start | bytes 92168 | tf_op jit(solution)/shard_map/ppermute | solution.py:387
  71.0 53.7 %fusion.306 = (f32[768]{0:T(1024)S(1)}, f32[768,1024]{1,0:T(8,128)S(1)}) fusion(f32[1024]{0:T(1024)S(1)} %bitcast.100, bf16[15,1024]{1,0:T(8,128)(2,1)S(1)} %collective-permute-done.1, bf16[768,1024]{1,0:T(8,128)(2,1)} %copy-done.7, pred[768]{0:T(1024)(128)(4,1)S(1)} %get-tuple-element.111, f32[1024]{0:T(1024)S(1)} %bitcast.98, ...), kind=kLoop, calls=%fused_computation.517 | loop fusion | flops 167509248 | bytes 4933120 | tf_op jit(solution)/shard_map/reduce_sum | solution.py:394
  125.5 5.4 %multiply_reduce_fusion = (f32[1024]{0:T(1024)}, f32[768]{0:T(1024)S(1)}, f32[768]{0:T(1024)S(1)}, bf16[768,1024]{1,0:T(8,128)(2,1)S(1)}, f32[768,1024]{1,0:T(8,128)S(1)}) fusion(f32[768,1024]{1,0:T(8,128)S(1)} %get-tuple-element.56, f32[768]{0:T(1024)S(1)} %add_rsqrt_fusion, f32[768]{0:T(1024)S(1)} %broadcast_multiply_fusion.4, f32[1024]{0:T(1024)S(1)} %bitcast.144, ...), kind=kOutput, calls=%fused_computation.411 | convolution fusion | flops 1624765952 | bytes 11554816 | tf_op jit(solution)/shard_map/dot_general | solution.py:440
  130.9 4.5 %fusion.265 = bf16[1,768,1024]{2,1,0:T(8,128)(2,1)} fusion(bf16[768,1024]{1,0:T(8,128)(2,1)S(1)} %get-tuple-element.59, bf16[1024,3328]{1,0:T(8,128)(2,1)} %bitcast.74, bf16[1,768,1024]{2,1,0:T(8,128)(2,1)S(1)} %copy-done.2), kind=kOutput, calls=%fused_computation.427 | convolution fusion | flops 1612972032 | bytes 6815744 | tf_op jit(solution)/shard_map/dot_general | solution.py:436
  135.4 3.2 multiply_convert_fusion.1
  138.6 5.7 %fusion.135 = (f32[1024]{0:T(1024)S(1)}, f32[1024]{0:T(1024)S(1)}, f32[1024]{0:T(1024)S(1)}, f32[1024]{0:T(1024)S(1)}, f32[768,1024]{1,0:T(8,128)S(1)}) fusion(pred[768]{0:T(1024)(128)(4,1)S(1)} %get-tuple-element.112, bf16[15,1024]{1,0:T(8,128)(2,1)S(1)} %collective-permute-done.1, bf16[768,1024]{1,0:T(8,128)(2,1)S(1)} %copy-done.8, ...), kind=kLoop, calls=%fused_computation.258 | loop fusion | flops 27521024 | bytes 11076608 | tf_op jit(solution)/shard_map/reduce_sum | solution.py:450
  145.0 1.9 collective-permute-start.3
  146.9 2.4 collective-permute-start.2
  149.4 3.3 fusion.50
  156.1 7.8 %fusion.62 = (f32[1024]{0:T(1024)S(1)}, f32[1024]{0:T(1024)S(1)}, f32[1024]{0:T(1024)S(1)}, f32[1024]{0:T(1024)S(1)}) fusion(f32[768,1024]{1,0:T(8,128)} %copy-done.6, pred[768]{0:T(1024)(128)(4,1)} %get-tuple-element.104, bf16[15,1024]{1,0:T(8,128)(2,1)S(1)} %collective-permute-done, bf16[768,1024]{1,0:T(8,128)(2,1)} %copy-done.7, ...), kind=kLoop, calls=%fused_computation.185 | loop fusion | flops 22016000 | bytes 4768768 | tf_op jit(solution)/shard_map/reduce_sum | solution.py:450
  168.5 7.4 %fusion.74 = (f32[1024]{0:T(1024)S(1)}, f32[1024]{0:T(1024)S(1)}, f32[1024]{0:T(1024)S(1)}, f32[1024]{0:T(1024)S(1)}) fusion(f32[768,1024]{1,0:T(8,128)} %copy-done.6, pred[768]{0:T(1024)(128)(4,1)} %get-tuple-element.100, bf16[15,1024]{1,0:T(8,128)(2,1)S(1)} %collective-permute-done, bf16[768,1024]{1,0:T(8,128)(2,1)} %copy-done.7, ...), kind=kLoop, calls=%fused_computation.197 | loop fusion | flops 22016000 | bytes 4768768 | tf_op jit(solution)/shard_map/reduce_sum | solution.py:450
  180.5 7.8 %fusion.86 = (f32[1024]{0:T(1024)S(1)}, f32[1024]{0:T(1024)S(1)}, f32[1024]{0:T(1024)S(1)}, f32[1024]{0:T(1024)S(1)}) fusion(f32[768,1024]{1,0:T(8,128)} %copy-done.6, bf16[768,1024]{1,0:T(8,128)(2,1)} %copy-done.7, bf16[15,1024]{1,0:T(8,128)(2,1)S(1)} %collective-permute-done, pred[768]{0:T(1024)(128)(4,1)} %get-tuple-element.96, ...), kind=kLoop, calls=%fused_computation.209 | loop fusion | flops 22016000 | bytes 4768768 | tf_op jit(solution)/shard_map/reduce_sum | solution.py:450
  192.9 10.6 %fusion.138 = (f32[1024]{0:T(1024)S(1)}, f32[1024]{0:T(1024)S(1)}, f32[1024]{0:T(1024)S(1)}, f32[1024]{0:T(1024)S(1)}, f32[1024]{0:T(1024)S(1)}) fusion(f32[768,1024]{1,0:T(8,128)} %copy-done.6, bf16[15,1024]{1,0:T(8,128)(2,1)S(1)} %collective-permute-done.1, bf16[768,1024]{1,0:T(8,128)(2,1)} %copy-done.7, pred[768]{0:T(1024)(128)(4,1)S(1)} %get-tuple-element.111, ...), kind=kLoop, calls=%fused_computation.261 | loop fusion | flops 24374272 | bytes 4772864 | tf_op jit(solution)/shard_map/reduce_sum | solution.py:450
  204.7 8.7 %fusion.96 = (f32[1024]{0:T(1024)S(1)}, f32[1024]{0:T(1024)S(1)}, f32[1024]{0:T(1024)S(1)}) fusion(f32[768,1024]{1,0:T(8,128)} %copy-done.6, pred[768]{0:T(1024)(128)(4,1)} %get-tuple-element.123, bf16[15,1024]{1,0:T(8,128)(2,1)S(1)} %collective-permute-done.1, bf16[768,1024]{1,0:T(8,128)(2,1)} %copy-done.7, pred[768]{0:T(1024)(128)(4,1)} %get-tuple-element.124, ...), kind=kLoop, calls=%fused_computation.219 | loop fusion | flops 16512000 | bytes 4763904 | tf_op jit(solution)/shard_map/reduce_sum | solution.py:450
  216.9 10.0 %fusion.108 = (f32[1024]{0:T(1024)S(1)}, f32[1024]{0:T(1024)S(1)}, f32[1024]{0:T(1024)S(1)}, f32[1024]{0:T(1024)S(1)}) fusion(f32[768,1024]{1,0:T(8,128)} %copy-done.6, pred[768]{0:T(1024)(128)(4,1)S(1)} %get-tuple-element.119, bf16[15,1024]{1,0:T(8,128)(2,1)S(1)} %collective-permute-done.1, bf16[768,1024]{1,0:T(8,128)(2,1)} %copy-done.7, ...), kind=kLoop, calls=%fused_computation.231 | loop fusion | flops 22016000 | bytes 4768768 | tf_op jit(solution)/shard_map/reduce_sum | solution.py:450
  240.6 10.0 %stack.127 = f32[4,4,4,16,31]{4,3,2,1,0:T(8,128)} concatenate(f32[4,4,4,16,1]{4,3,2,1,0:T(8,128)} %stack.128, f32[4,4,4,16,1]{4,3,2,1,0:T(8,128)} %stack.129, f32[4,4,4,16,1]{4,3,2,1,0:T(8,128)} %stack.130, f32[4,4,4,16,1]{4,3,2,1,0:T(8,128)} %stack.131, f32[4,4,4,16,1]{4,3,2,1,0:T(8,128)} %stack.132, f32[4,4,4,16,1]{4,3,2,1,0:T(8,128)} %stack.133, f32[4,4,4,16,1]{4,3,2,1,0:T(8,128)} %stack.134, ...), dimensions={4} | concatenate | bytes 253952 | tf_op jit(solution)/shard_map/stack | solution.py:458
  253.0 1.8 convert_element_type.288
  254.9 77.2 %multiply_convert_fusion.3 = (bf16[768,1024]{1,0:T(8,128)(2,1)S(1)}, f32[768,1024]{1,0:T(8,128)S(1)}) fusion(f32[768,2048]{1,0:T(8,128)} %copy-done.9, f32[1024]{0:T(1024)} %bitcast.101, f32[768,1024]{1,0:T(8,128)} %copy-done.6, f32[15,1024]{1,0:T(8,128)S(1)} %collective-permute-done.3, pred[768]{0:T(1024)(128)(4,1)} %get-tuple-element.95, ...), kind=kLoop, calls=%fused_computation.413 | loop fusion | flops 99090432 | bytes 11282944 | tf_op jit(solution)/shard_map/convert.4
  332.1 4.1 multiply_convert_fusion.2
  336.2 7.6 %fusion.16 = (f32[1024]{0:T(1024)S(1)}, f32[768]{0:T(1024)S(1)}, f32[768]{0:T(1024)S(1)}, f32[768,1024]{1,0:T(8,128)}) fusion(f32[768]{0:T(1024)S(1)} %copy-done.42, f32[768]{0:T(1024)S(1)} %broadcast_multiply_fusion.5, bf16[1,768,1024]{2,1,0:T(8,128)(2,1)S(1)} %copy-done.2, f32[1024]{0:T(1024)S(1)} %bitcast.141, bf16[1024,3328]{1,0:T(8,128)(2,1)} %bitcast.75, ...), kind=kOutput, calls=%fused_computation.139 | convolution fusion | flops 3234592256 | bytes 12079104 | tf_op jit(solution)/shard_map/dot_general | solution.py:463
  343.8 5.8 %multiply_convert_fusion = bf16[1024,2048]{1,0:T(8,128)(2,1)} fusion(bf16[768,1024]{1,0:T(8,128)(2,1)S(1)} %multiply_convert_fusion.2, bf16[768,1024]{1,0:T(8,128)(2,1)S(1)} %get-tuple-element.53, f32[1024]{0:T(1024)S(1)} %bitcast.142, f32[768]{0:T(1024)S(1)} %copy-done.42, f32[768]{0:T(1024)S(1)} %broadcast_multiply_fusion.5, ...), kind=kOutput, calls=%fused_computation.56 | convolution fusion | flops 3235643392 | bytes 8923136 | tf_op jit(solution)/shard_map/dot_general | solution.py:462
  351.7 11.0 %concatenate.131.g_ref = bf16[4,4,4,16,3328]{4,3,2,1,0:T(8,128)(2,1)} concatenate(bf16[4,4,4,16,2048]{4,3,2,1,0:T(8,128)(2,1)} %bitcast.76, bf16[4,4,4,16,1024]{4,3,2,1,0:T(8,128)(2,1)} %bitcast.77, bf16[4,4,4,16,31]{4,3,2,1,0:T(8,128)(2,1)S(1)} %multiply_convert_fusion.5, bf16[4,4,4,16,1]{4,3,2,1,0:T(8,128)(2,1)} %convert_element_type.287, ...), dimensions={4} | concatenate | bytes 13631488 | tf_op jit(solution)/shard_map/concatenate | solution.py:507
  362.6 2.9 copy-done
  365.6 40.6 %scatter_grads.1 = f32[8,3328]{1,0:T(8,128)S(1)} custom-call(bf16[4,4,4,16,3328]{4,3,2,1,0:T(8,128)(2,1)S(1)} %copy-done), custom_call_target="tpu_custom_call" | custom-call | tf_op jit(solution)/shard_map/scatter_grads/pallas_call | solution.py:346
  408.8 2.4 fusion.266
  (179 shorter events, 54.5 us)
Async XLA Ops:
  61.5 9.5 %collective-permute-start.1 = (bf16[15,1024]{1,0:T(8,128)(2,1)S(1)}, bf16[15,1024]{1,0:T(8,128)(2,1)S(1)}, u32[]{:S(2)}, u32[]{:S(2)}) collective-permute-start(bf16[15,1024]{1,0:T(8,128)(2,1)S(1)} %get-tuple-element.63), channel_id=1, source_target_pairs={{1,0},{2,1},{3,2},{4,3},{5,4},{6,5},{7,6},{9,8},{10,9},{11,10},{12... | collective-permute-start | bytes 92168 | tf_op jit(solution)/shard_map/ppermute | solution.py:388
  63.4 7.6 %collective-permute-start = (bf16[15,1024]{1,0:T(8,128)(2,1)S(1)}, bf16[15,1024]{1,0:T(8,128)(2,1)S(1)}, u32[]{:S(2)}, u32[]{:S(2)}) collective-permute-start(bf16[15,1024]{1,0:T(8,128)(2,1)S(1)} %get-tuple-element.62), channel_id=1, source_target_pairs={{0,1},{1,2},{2,3},{3,4},{4,5},{5,6},{6,7},{8,9},{9,10},{10,11},{11... | collective-permute-start | bytes 92168 | tf_op jit(solution)/shard_map/ppermute | solution.py:387
  68.8 56.4 %copy-start.12 = (f32[1024,1]{0,1:T(1,128)}, f32[1024,1]{0,1:T(1,128)S(1)}, u32[]{:S(2)}) copy-start(f32[1024,1]{0,1:T(1,128)S(1)} %get-tuple-element.87) | copy-start | bytes 12292
  68.8 56.4 %copy-start.13 = (f32[1024,1]{0,1:T(1,128)}, f32[1024,1]{0,1:T(1,128)S(1)}, u32[]{:S(2)}) copy-start(f32[1024,1]{0,1:T(1,128)S(1)} %get-tuple-element.88) | copy-start | bytes 12292
  68.8 56.4 %copy-start.14 = (f32[1024,1]{0,1:T(1,128)}, f32[1024,1]{0,1:T(1,128)S(1)}, u32[]{:S(2)}) copy-start(f32[1024,1]{0,1:T(1,128)S(1)} %get-tuple-element.89) | copy-start | bytes 12292
  68.8 56.4 %copy-start.15 = (f32[1024,1]{0,1:T(1,128)}, f32[1024,1]{0,1:T(1,128)S(1)}, u32[]{:S(2)}) copy-start(f32[1024,1]{0,1:T(1,128)S(1)} %get-tuple-element.90) | copy-start | bytes 12292
  68.8 56.4 %copy-start.16 = (f32[1024,1]{0,1:T(1,128)}, f32[1024,1]{0,1:T(1,128)S(1)}, u32[]{:S(2)}) copy-start(f32[1024,1]{0,1:T(1,128)S(1)} %get-tuple-element.91) | copy-start | bytes 12292
  68.8 56.4 %copy-start.17 = (f32[1024,1]{0,1:T(1,128)}, f32[1024,1]{0,1:T(1,128)S(1)}, u32[]{:S(2)}) copy-start(f32[1024,1]{0,1:T(1,128)S(1)} %get-tuple-element.92) | copy-start | bytes 12292
  68.8 56.4 %copy-start.18 = (f32[1024,1]{0,1:T(1,128)}, f32[1024,1]{0,1:T(1,128)S(1)}, u32[]{:S(2)}) copy-start(f32[1024,1]{0,1:T(1,128)S(1)} %get-tuple-element.93) | copy-start | bytes 12292
  68.8 56.4 %copy-start.19 = (f32[1024,1]{0,1:T(1,128)}, f32[1024,1]{0,1:T(1,128)S(1)}, u32[]{:S(2)}) copy-start(f32[1024,1]{0,1:T(1,128)S(1)} %get-tuple-element.94) | copy-start | bytes 12292
  68.9 56.4 %copy-start.20 = (f32[1024,1]{0,1:T(1,128)}, f32[1024,1]{0,1:T(1,128)S(1)}, u32[]{:S(2)}) copy-start(f32[1024,1]{0,1:T(1,128)S(1)} %get-tuple-element.64) | copy-start | bytes 12292
  68.9 56.4 %copy-start.21 = (f32[1024,1]{0,1:T(1,128)}, f32[1024,1]{0,1:T(1,128)S(1)}, u32[]{:S(2)}) copy-start(f32[1024,1]{0,1:T(1,128)S(1)} %get-tuple-element.65) | copy-start | bytes 12292
  68.9 56.4 %copy-start.22 = (f32[1024,1]{0,1:T(1,128)}, f32[1024,1]{0,1:T(1,128)S(1)}, u32[]{:S(2)}) copy-start(f32[1024,1]{0,1:T(1,128)S(1)} %get-tuple-element.66) | copy-start | bytes 12292
  68.9 56.4 %copy-start.23 = (f32[1024,1]{0,1:T(1,128)}, f32[1024,1]{0,1:T(1,128)S(1)}, u32[]{:S(2)}) copy-start(f32[1024,1]{0,1:T(1,128)S(1)} %get-tuple-element.67) | copy-start | bytes 12292
  68.9 56.4 %copy-start.24 = (f32[1024,1]{0,1:T(1,128)}, f32[1024,1]{0,1:T(1,128)S(1)}, u32[]{:S(2)}) copy-start(f32[1024,1]{0,1:T(1,128)S(1)} %get-tuple-element.68) | copy-start | bytes 12292
  69.0 56.4 %copy-start.25 = (f32[1024,1]{0,1:T(1,128)}, f32[1024,1]{0,1:T(1,128)S(1)}, u32[]{:S(2)}) copy-start(f32[1024,1]{0,1:T(1,128)S(1)} %get-tuple-element.69) | copy-start | bytes 12292
  69.0 56.4 %copy-start.26 = (f32[1024,1]{0,1:T(1,128)}, f32[1024,1]{0,1:T(1,128)S(1)}, u32[]{:S(2)}) copy-start(f32[1024,1]{0,1:T(1,128)S(1)} %get-tuple-element.70) | copy-start | bytes 12292
  69.0 56.4 %copy-start.27 = (f32[1024,1]{0,1:T(1,128)}, f32[1024,1]{0,1:T(1,128)S(1)}, u32[]{:S(2)}) copy-start(f32[1024,1]{0,1:T(1,128)S(1)} %get-tuple-element.71) | copy-start | bytes 12292
  69.0 56.4 %copy-start.28 = (f32[1024,1]{0,1:T(1,128)}, f32[1024,1]{0,1:T(1,128)S(1)}, u32[]{:S(2)}) copy-start(f32[1024,1]{0,1:T(1,128)S(1)} %get-tuple-element.72) | copy-start | bytes 12292
  69.0 56.4 %copy-start.29 = (f32[1024,1]{0,1:T(1,128)}, f32[1024,1]{0,1:T(1,128)S(1)}, u32[]{:S(2)}) copy-start(f32[1024,1]{0,1:T(1,128)S(1)} %get-tuple-element.73) | copy-start | bytes 12292
  70.0 68.6 %copy-start.44 = (pred[768]{0:T(1024)(128)(4,1)}, pred[768]{0:T(1024)(128)(4,1)S(1)}, u32[]{:S(2)}) copy-start(pred[768]{0:T(1024)(128)(4,1)S(1)} %get-tuple-element.112) | copy-start | bytes 2308
  70.0 68.6 %copy-start.48 = (pred[768]{0:T(1024)(128)(4,1)}, pred[768]{0:T(1024)(128)(4,1)S(1)}, u32[]{:S(2)}) copy-start(pred[768]{0:T(1024)(128)(4,1)S(1)} %get-tuple-element.116) | copy-start | bytes 2308
  70.0 68.6 %copy-start.49 = (pred[768]{0:T(1024)(128)(4,1)}, pred[768]{0:T(1024)(128)(4,1)S(1)}, u32[]{:S(2)}) copy-start(pred[768]{0:T(1024)(128)(4,1)S(1)} %get-tuple-element.117) | copy-start | bytes 2308
  70.0 68.6 %copy-start.50 = (pred[768]{0:T(1024)(128)(4,1)}, pred[768]{0:T(1024)(128)(4,1)S(1)}, u32[]{:S(2)}) copy-start(pred[768]{0:T(1024)(128)(4,1)S(1)} %get-tuple-element.118) | copy-start | bytes 2308
  70.0 122.9 %copy-start.43 = (pred[768]{0:T(1024)(128)(4,1)}, pred[768]{0:T(1024)(128)(4,1)S(1)}, u32[]{:S(2)}) copy-start(pred[768]{0:T(1024)(128)(4,1)S(1)} %get-tuple-element.111) | copy-start | bytes 2308
  70.0 122.9 %copy-start.45 = (pred[768]{0:T(1024)(128)(4,1)}, pred[768]{0:T(1024)(128)(4,1)S(1)}, u32[]{:S(2)}) copy-start(pred[768]{0:T(1024)(128)(4,1)S(1)} %get-tuple-element.113) | copy-start | bytes 2308
  70.0 122.9 %copy-start.46 = (pred[768]{0:T(1024)(128)(4,1)}, pred[768]{0:T(1024)(128)(4,1)S(1)}, u32[]{:S(2)}) copy-start(pred[768]{0:T(1024)(128)(4,1)S(1)} %get-tuple-element.114) | copy-start | bytes 2308
  70.0 122.9 %copy-start.47 = (pred[768]{0:T(1024)(128)(4,1)}, pred[768]{0:T(1024)(128)(4,1)S(1)}, u32[]{:S(2)}) copy-start(pred[768]{0:T(1024)(128)(4,1)S(1)} %get-tuple-element.115) | copy-start | bytes 2308
  70.0 134.7 %copy-start.51 = (pred[768]{0:T(1024)(128)(4,1)}, pred[768]{0:T(1024)(128)(4,1)S(1)}, u32[]{:S(2)}) copy-start(pred[768]{0:T(1024)(128)(4,1)S(1)} %get-tuple-element.110) | copy-start | bytes 2308
  70.1 146.8 %copy-start.52 = (pred[768]{0:T(1024)(128)(4,1)}, pred[768]{0:T(1024)(128)(4,1)S(1)}, u32[]{:S(2)}) copy-start(pred[768]{0:T(1024)(128)(4,1)S(1)} %get-tuple-element.119) | copy-start | bytes 2308
  145.0 109.8 %collective-permute-start.3 = (f32[15,1024]{1,0:T(8,128)}, f32[15,1024]{1,0:T(8,128)S(1)}, u32[]{:S(2)}, u32[]{:S(2)}) collective-permute-start(f32[15,1024]{1,0:T(8,128)} %get-tuple-element.61), channel_id=1, source_target_pairs={{0,1},{1,2},{2,3},{3,4},{4,5},{5,6},{6,7},{8,9},{9,10},{10,11},{11... | collective-permute-start | bytes 184328 | tf_op jit(solution)/shard_map/ppermute | solution.py:387
  146.9 107.9 %collective-permute-start.2 = (f32[15,1024]{1,0:T(8,128)}, f32[15,1024]{1,0:T(8,128)S(1)}, u32[]{:S(2)}, u32[]{:S(2)}) collective-permute-start(f32[15,1024]{1,0:T(8,128)} %get-tuple-element.60), channel_id=1, source_target_pairs={{1,0},{2,1},{3,2},{4,3},{5,4},{6,5},{7,6},{9,8},{10,9},{11,10},{12... | collective-permute-start | bytes 184328 | tf_op jit(solution)/shard_map/ppermute | solution.py:388
  (25 other events, 750.1 us)

commit v2 on v1

--- a/solution.py
+++ b/solution.py
@@ -2,6 +2,7 @@
 
 import jax
 import jax.numpy as jnp
+import numpy as np
 from jax import lax
 from jax.experimental import pallas as pl
 from jax.experimental.pallas import tpu as pltpu
@@ -375,161 +376,295 @@
 
 EPS = 1e-05
 HALF = 15
-
-
-def with_halo(array, sides, width):
-    for axis, dim in sides:
-        count, length = (lax.axis_size(axis), array.shape[dim])
-        up = [(i, (i + 1) % count) for i in range(count - 1)]
-        down = [(j, i) for i, j in up]
-        last = lax.slice_in_dim(array, length - width, length, axis=dim)
-        first = lax.slice_in_dim(array, 0, width, axis=dim)
-        before = lax.ppermute(last, axis, up)
-        after = lax.ppermute(first, axis, down)
-        array = jnp.concatenate([before, array, after], axis=dim)
-    return array
-
-
-def norm_rows(values, gain):
-    mean = jnp.mean(values, axis=-1, keepdims=True)
-    centred = values - mean
-    inv = lax.rsqrt(jnp.mean(centred * centred, axis=-1, keepdims=True) + EPS)
-    normal = centred * inv
-    return (normal, inv, normal * gain)
-
-
-def norm_back(grad_out, normal, inv, gain):
-    scaled = grad_out * gain
-    return inv * (
-        scaled
-        - jnp.mean(scaled, -1, keepdims=True)
-        - normal * jnp.mean(scaled * normal, -1, keepdims=True)
-    )
-
-
-def block_pass(
-    frames, cotangent, seg_pad, widen_glu, widen_grad, w_in, w_out, kernel, gain_in, gain_mid, scale
+ROWS = 768
+D = 1024
+NFFT = 256
+
+
+def tables():
+    omega = 2 * np.pi * (np.arange(128) + 0.5) / NFFT
+    phase = omega[:, None] * np.arange(NFFT)[None]
+    basis = np.concatenate([np.cos(phase), -np.sin(phase)], axis=0)
+    lag = omega[:, None] * (np.arange(31) - HALF)[None]
+    spread = np.zeros((NFFT, 128))
+    spread[:, :31] = np.concatenate([np.cos(lag), np.sin(lag)], axis=0) * (2 / NFFT)
+    back = np.zeros((128, NFFT))
+    back[:31] = np.concatenate([np.cos(lag), -np.sin(lag)], axis=0).T * (2 / NFFT)
+    return (jnp.asarray(basis, jnp.bfloat16), jnp.asarray(spread, jnp.float32), jnp.asarray(back, jnp.float32))
+
+
+def colours(ids):
+    step = ids[HALF:] - ids[:-HALF]
+    fwd_at, bwd_at = (0, 208, 416, 592), (16, 208, 400, 592)
+    counts, rows = [], []
+    for starts, length in ((fwd_at, 240), (bwd_at, 224)):
+        for at in starts:
+            count = jnp.max(step[at : at + length - HALF]) + 1
+            counts.append(count)
+            own = jnp.pad(ids[at : at + length] % count, (0, NFFT - length), constant_values=-1)
+            rows.append(own)
+    inner = jnp.arange(NFFT)
+    for w in range(4):
+        rows.append(jnp.where((inner >= 16) & (inner < 208), rows[4 + w], -1))
+    table = jnp.stack(rows).astype(jnp.float32)
+    return jnp.stack(counts).astype(jnp.int32), jnp.broadcast_to(table[:, None, :], (12, 8, NFFT))
+
+
+def sigmoid(v):
+    return 0.5 * jnp.tanh(0.5 * v) + 0.5
+
+
+NT = (((1,), (1,)), ((), ()))
+TN = (((0,), (0,)), ((), ()))
+F32 = jnp.float32
+BF = jnp.bfloat16
+
+
+def nt(a, b):
+    return lax.dot_general(a, b, NT, preferred_element_type=F32)
+
+
+def mm(a, b):
+    return jnp.dot(a, b, preferred_element_type=F32)
+
+
+def row_mean(v):
+    return jnp.sum(v, axis=-1, keepdims=True) * (1.0 / D)
+
+
+def mid_kernel(
+    counts, table, basis, spread, back, frames, cot, hf, hc, w_hbm,
+    out_ref, igrad_ref, g_hbm,
+    xe, ce, w, ln, glu, sig, mixed, work, act, dm, dpre, g, spec, prod, gains, extra, inv_in, mean_in, sems,
 ):
-    rows = frames.shape[0]
-    width = frames.shape[1]
-    taps = kernel.shape[1]
-    kern = kernel.astype(jnp.float32)
-    centre = seg_pad[HALF : HALF + rows]
-    x_val = frames.astype(jnp.float32)
-    normal_in, inv_in, scaled_in = norm_rows(x_val, gain_in.astype(jnp.float32))
-    ln_in = scaled_in.astype(jnp.bfloat16)
-    pre = jnp.dot(ln_in, w_in, preferred_element_type=jnp.float32)
-    value = pre[:, :width]
-    gate_sig = jax.nn.sigmoid(pre[:, width:])
-    glu = (value * gate_sig).astype(jnp.bfloat16)
-    glu_pad = widen_glu(glu)
-    mixed = jnp.zeros((rows, width), jnp.float32)
-    for tap in range(taps):
-        same = (seg_pad[tap : tap + rows] == centre)[:, None]
-        mixed = mixed + jnp.where(
-            same, glu_pad[tap : tap + rows].astype(jnp.float32) * kern[:, tap], 0.0
-        )
-    gmid = gain_mid.astype(jnp.float32)
-    normal_mid, inv_mid, ln_mid = norm_rows(mixed, gmid)
-    sig_mid = jax.nn.sigmoid(ln_mid)
-    act = (ln_mid * sig_mid).astype(jnp.bfloat16)
-    block_out = (x_val + jnp.dot(act, w_out, preferred_element_type=jnp.float32)).astype(
-        jnp.bfloat16
-    )
-    grad_w_out = jnp.dot(act.T, cotangent, preferred_element_type=jnp.float32) * scale
-    d_act = jnp.dot(cotangent, w_out.T, preferred_element_type=jnp.float32)
-    d_ln_mid = d_act * (sig_mid + ln_mid * sig_mid * (1.0 - sig_mid))
-    grad_gain_mid = jnp.sum(d_ln_mid * normal_mid, axis=0) * scale
-    d_mixed = norm_back(d_ln_mid, normal_mid, inv_mid, gmid)
-    grad_pad = widen_grad(d_mixed)
-    d_glu = jnp.zeros((rows, width), jnp.float32)
-    kernel_terms = []
-    for tap in range(taps):
-        same = (seg_pad[tap : tap + rows] == centre)[:, None]
-        kernel_terms.append(
-            jnp.sum(
-                jnp.where(same, glu_pad[tap : tap + rows].astype(jnp.float32) * d_mixed, 0.0),
-                axis=0,
-            )
-        )
-        start = 2 * HALF - tap
-        back_same = (seg_pad[start : start + rows] == centre)[:, None]
-        d_glu = d_glu + jnp.where(back_same, grad_pad[start : start + rows] * kern[:, tap], 0.0)
-    grad_kernel = jnp.stack(kernel_terms, axis=1) * scale
-    d_pre = jnp.concatenate(
-        [d_glu * gate_sig, d_glu * value * gate_sig * (1.0 - gate_sig)], axis=-1
-    ).astype(jnp.bfloat16)
-    grad_w_in = jnp.dot(ln_in.T, d_pre, preferred_element_type=jnp.float32) * scale
-    d_ln_in = jnp.dot(d_pre, w_in.T, preferred_element_type=jnp.float32)
-    gin = gain_in.astype(jnp.float32)
-    grad_gain_in = jnp.sum(d_ln_in * normal_in, axis=0) * scale
-    input_grad = (
-        cotangent.astype(jnp.float32) + norm_back(d_ln_in, normal_in, inv_in, gin)
-    ).astype(jnp.bfloat16)
-    return (
-        block_out,
-        input_grad,
-        (grad_w_in, grad_w_out, grad_kernel, grad_gain_in, grad_gain_mid),
-    )
+    scale = 1.0 / math.sqrt(98304.0)
+
+    def cp(src, dst, n):
+        c = pltpu.make_async_copy(src, dst, sems.at[n])
+        c.start()
+        return c
+
+    loads = [
+        cp(frames, xe.at[pl.ds(32, ROWS)], 0),
+        cp(hf.at[pl.ds(0, 32)], xe.at[pl.ds(0, 32)], 1),
+        cp(hf.at[pl.ds(32, 32)], xe.at[pl.ds(800, 32)], 2),
+        cp(w_hbm, w, 3),
+        cp(cot, ce.at[pl.ds(16, ROWS)], 4),
+        cp(hc.at[pl.ds(0, 16)], ce.at[pl.ds(0, 16)], 5),
+        cp(hc.at[pl.ds(16, 16)], ce.at[pl.ds(784, 16)], 6),
+    ]
+    loads[3].wait()
+    taps = w[:, 3072:3200].astype(F32).T
+    gains[0:8, :] = jnp.broadcast_to(taps[31:32, :], (8, D))
+    gains[8:16, :] = jnp.broadcast_to(taps[32:33, :], (8, D))
+    spec[...] = jnp.dot(spread[...], taps, precision=lax.Precision.HIGHEST, preferred_element_type=F32)
+    glu[pl.ds(832, 16), :] = jnp.zeros((16, D), BF)
+    dm[pl.ds(800, 32), :] = jnp.zeros((32, D), BF)
+    prod[...] = jnp.zeros((NFFT, D), F32)
+    extra[...] = jnp.zeros((128, D), F32)
+    for n in (0, 1, 2):
+        loads[n].wait()
+
+    @pl.loop(0, 52)
+    def _(i):
+        at = pl.ds(pl.multiple_of(i * 16, 16), 16)
+        x = xe[at, :].astype(F32)
+        mean = row_mean(x)
+        cen = x - mean
+        inv = lax.rsqrt(row_mean(cen * cen) + EPS)
+        ln[at, :] = (cen * inv * gains[0:1, :]).astype(BF)
+        inv_in[at, :] = jnp.broadcast_to(inv, (16, 128))
+        mean_in[at, :] = jnp.broadcast_to(mean, (16, 128))
+
+    @pl.loop(0, 8)
+    def _(i):
+        j, r = i // 2, i % 2
+        rows = pl.ds(pl.multiple_of(r * 416, 16), 416)
+        c0 = pl.ds(pl.multiple_of(j * 256, 256), 256)
+        c1 = pl.ds(pl.multiple_of(j * 256 + 1024, 256), 256)
+        lhs = ln[rows, :]
+        value = mm(lhs, w[:, c0])
+        s = sigmoid(mm(lhs, w[:, c1]))
+        glu[rows, c0] = (value * s).astype(BF)
+        sig[rows, c0] = s
+
+    for n in (4, 5, 6):
+        loads[n].wait()
+
+    def masked(row, c):
+        hit = table[row, 0:1, :] == c.astype(F32)
+        return jnp.where(hit, basis[...].astype(F32), 0.0).astype(BF)
+
+    @pl.loop(0, 4)
+    def _(wi):
+        base = pl.multiple_of(jnp.minimum(wi * 208, 592), 16)
+        mixed[pl.ds(base, 208), :] = jnp.zeros((208, D), F32)
+
+        @pl.loop(0, counts[wi])
+        def _(c):
+            cm = masked(wi, c)
+            inv = cm.T[16:224, :]
+            for j in range(4):
+                col = slice(j * 256, j * 256 + 256)
+                x = mm(cm, glu[pl.ds(base, 256), col])
+                xr, xi = x[:128], x[128:]
+                hr, hi = spec[:128, col], spec[128:, col]
+                y = jnp.concatenate([xr * hr - xi * hi, xr * hi + xi * hr], axis=0).astype(BF)
+                mixed[pl.ds(base, 208), col] += mm(inv, y)
+
+    @pl.loop(0, 4)
+    def _(j):
+        col = pl.ds(pl.multiple_of(j * 256, 256), 256)
+        work[:, col] = nt(ce[...], w[col, 2048:3072])
+
+    def mid_rows(i, central):
+        at = pl.ds(pl.multiple_of(i * 16, 16), 16)
+        gain = gains[8:9, :]
+        m = mixed[at, :]
+        cen = m - row_mean(m)
+        inv = lax.rsqrt(row_mean(cen * cen) + EPS)
+        normal = cen * inv
+        y = normal * gain
+        s = sigmoid(y)
+        ys = y * s
+        act[at, :] = ys.astype(BF)
+        d_ln = work[at, :] * (s + ys * (1.0 - s))
+        if central:
+            dn = d_ln * normal
+            extra[40:48, :] += dn[:8] + dn[8:]
+        u = d_ln * gain
+        dm[at, :] = (inv * (u - row_mean(u) - normal * row_mean(u * normal))).astype(BF)
+
+    mid_rows(0, False)
+    mid_rows(49, False)
+
+    @pl.loop(1, 49)
+    def _(i):
+        mid_rows(i, True)
+
+    @pl.loop(0, 4)
+    def _(j):
+        col = pl.ds(pl.multiple_of(j * 256, 256), 256)
+        y = mm(act[16:784, :], w[:, pl.ds(pl.multiple_of(2048 + j * 256, 256), 256)])
+        out_ref[:, col] = (xe[32:800, col].astype(F32) + y).astype(BF)
+        lhs = act[16:784, col].T
+        g[col, 2048:3072] = (mm(lhs, ce[16:784, :]) * scale).astype(BF)
+
+    @pl.loop(0, 4)
+    def _(wi):
+        base = pl.multiple_of(wi * 192, 16)
+        mixed[pl.ds(base, 192), :] = jnp.zeros((192, D), F32)
+
+        @pl.loop(0, counts[4 + wi])
+        def _(c):
+            cm = masked(4 + wi, c)
+            cg = masked(8 + wi, c)
+            inv = cm.T[16:208, :]
+            for j in range(4):
+                col = slice(j * 256, j * 256 + 256)
+                d = mm(cm, dm[pl.ds(base, 256), col])
+                q = mm(cg, glu[pl.ds(base + 16, 256), col])
+                dr, di, qr, qi = d[:128], d[128:], q[:128], q[128:]
+                hr, hi = spec[:128, col], spec[128:, col]
+                y = jnp.concatenate([dr * hr + di * hi, di * hr - dr * hi], axis=0).astype(BF)
+                prod[:128, col] += qr * dr + qi * di
+                prod[128:, col] += qi * dr - qr * di
+                mixed[pl.ds(base, 192), col] += mm(inv, y)
+
+    @pl.loop(0, 48)
+    def _(i):
+        at = pl.ds(pl.multiple_of(i * 16, 16), 16)
+        ext = pl.ds(pl.multiple_of(i * 16 + 32, 16), 16)
+        d = mixed[at, :]
+        s = sig[ext, :]
+        ds = d * s
+        dpre[at, :1024] = ds.astype(BF)
+        dpre[at, 1024:] = (d * glu[ext, :].astype(F32) * (1.0 - s)).astype(BF)
+
+    @pl.loop(0, 4)
+    def _(j):
+        col = pl.ds(pl.multiple_of(j * 256, 256), 256)
+        lhs = ln[32:800, col].T
+        for n in range(4):
+            cols = slice(n * 512, n * 512 + 512)
+            g[col, cols] = (mm(lhs, dpre[:, cols]) * scale).astype(BF)
+        work[0:768, col] = nt(dpre[...], w[col, 0:2048])
+
+    @pl.loop(0, 48)
+    def _(i):
+        at = pl.ds(pl.multiple_of(i * 16, 16), 16)
+        ext = pl.ds(pl.multiple_of(i * 16 + 32, 16), 16)
+        inv = inv_in[ext, 0:1]
+        normal = (xe[ext, :].astype(F32) - mean_in[ext, 0:1]) * inv
+        d = work[at, :]
+        dn = d * normal
+        extra[48:56, :] += dn[:8] + dn[8:]
+        u = d * gains[0:1, :]
+        back_in = inv * (u - row_mean(u) - normal * row_mean(u * normal))
+        c = ce[pl.ds(pl.multiple_of(i * 16 + 16, 16), 16), :].astype(F32)
+        igrad_ref[at, :] = (c + back_in).astype(BF)
+
+    gk = jnp.dot(back[...], prod[...], precision=lax.Precision.HIGHEST, preferred_element_type=F32)
+    extra[0:31, :] = gk[0:31]
+    g_mid = jnp.sum(extra[40:48, :], axis=0, keepdims=True)
+    g_in = jnp.sum(extra[48:56, :], axis=0, keepdims=True)
+    extra[31:32, :] = g_in
+    extra[32:33, :] = g_mid
+    g[:, 3072:3200] = (extra[...].T * scale).astype(BF)
+    g[:, 3200:3328] = jnp.zeros((D, 128), BF)
+    cp(g, g_hbm, 7).wait()
+
+
+def mid(counts, table, consts, frames, cot, hf, hc, w):
+    vm = pl.BlockSpec(memory_space=pltpu.VMEM)
+    hbm = pl.BlockSpec(memory_space=pl.ANY)
+    V = pltpu.VMEM
+    return pl.pallas_call(
+        mid_kernel,
+        out_shape=(
+            jax.ShapeDtypeStruct((ROWS, D), BF),
+            jax.ShapeDtypeStruct((ROWS, D), BF),
+            jax.ShapeDtypeStruct((D, WIDE), BF),
+        ),
+        in_specs=[pl.BlockSpec(memory_space=pltpu.SMEM), vm, vm, vm, vm, hbm, hbm, hbm, hbm, hbm],
+        out_specs=(vm, vm, hbm),
+        scratch_shapes=[
+            V((832, D), BF), V((800, D), BF), V((D, WIDE), BF),
+            V((832, D), BF), V((848, D), BF), V((832, D), F32),
+            V((800, D), F32), V((800, D), F32), V((800, D), BF), V((832, D), BF),
+            V((768, 2 * D), BF), V((D, WIDE), BF), V((NFFT, D), F32), V((NFFT, D), F32),
+            V((16, D), F32), V((128, D), F32), V((832, 128), F32), V((832, 128), F32),
+            pltpu.SemaphoreType.DMA((8,)),
+        ],
+        compiler_params=pltpu.CompilerParams(vmem_limit_bytes=60 << 20),
+        name="block_pass",
+    )(counts, table, *consts, frames, cot, hf, hc, w)
 
 
 def shards(frames, cotangent, segments, w_in, w_out, kernel, gain_in, gain_mid):
     frame_rows = frames[0]
     cot_rows = cotangent[0]
-    rows = frame_rows.shape[0]
-    f32 = jnp.float32
     packed = jnp.concatenate(
-        [w_in.astype(f32), w_out.astype(f32), kernel.astype(f32), gain_in.astype(f32)[:, None],
-         gain_mid.astype(f32)[:, None], jnp.zeros((8, WIDE - 3072 - 33), f32)], axis=1)
-    seg_rows = jnp.broadcast_to(segments[0].astype(jnp.bfloat16)[:, None], (rows, 128))
-    full, _, _, seg_halo = gather(packed, frame_rows, cot_rows, seg_rows)
-    full = full.reshape(1024, WIDE)
-    scale = jnp.float32(1.0 / math.sqrt(rows * 128))
+        [w_in.astype(F32), w_out.astype(F32), kernel.astype(F32), gain_in.astype(F32)[:, None],
+         gain_mid.astype(F32)[:, None], jnp.zeros((8, WIDE - 3072 - 33), F32)], axis=1)
+    seg_rows = jnp.broadcast_to(segments[0].astype(BF)[:, None], (ROWS, 128))
+    full, f_halo, c_halo, seg_halo = gather(packed, frame_rows, cot_rows, seg_rows)
     at = lax.axis_index("seq")
     halo = seg_halo[:, 0].astype(jnp.int32)
-    seg_pad = jnp.concatenate([
-        jnp.where(at == 0, -1, halo[HALO - HALF : HALO]), segments[0],
-        jnp.where(at == 7, -1, halo[HALO : HALO + HALF])])
-    block_out, input_grad, partial_grads = block_pass(
-        frame_rows,
-        cot_rows,
-        seg_pad,
-        lambda values: with_halo(values, (("seq", 0),), HALF),
-        lambda values: with_halo(values, (("seq", 0),), HALF),
-        full[:, :2048],
-        full[:, 2048:3072],
-        full[:, 3072:3103],
-        full[:, 3103],
-        full[:, 3104],
-        scale,
-    )
-    bf = jnp.bfloat16
-    g = jnp.concatenate([
-        partial_grads[0].astype(bf), partial_grads[1].astype(bf), partial_grads[2].astype(bf),
-        partial_grads[3].astype(bf)[:, None], partial_grads[4].astype(bf)[:, None],
-        jnp.zeros((1024, WIDE - 3072 - 33), bf)], axis=1).reshape(4, 4, 4, 16, WIDE)
-    r = scatter(g)
+    own = segments[0]
+    ids = jnp.concatenate([
+        jnp.where(at == 0, own[0] - 1, halo[:HALO]), own, jnp.where(at == 7, own[-1] + 1, halo[HALO:])])
+    counts, table = colours(ids)
+    block_out, input_grad, g = mid(
+        counts, table, tables(), frame_rows, cot_rows, f_halo, c_halo, full.reshape(1024, WIDE))
+    r = scatter(g.reshape(4, 4, 4, 16, WIDE))
     return (block_out[None], input_grad[None], r[:, :2048], r[:, 2048:3072], r[:, 3072:3103], r[:, 3103], r[:, 3104])
 
 
 def solution(mesh):
-    in_specs = (
-        P("dp", "seq", None),
-        P("dp", "seq", None),
-        P("dp", "seq"),
-        P(("dp", "seq"), None),
-        P(("dp", "seq"), None),
-        P(("dp", "seq"), None),
-        P(("dp", "seq")),
-        P(("dp", "seq")),
-    )
-    out_specs = (
-        P("dp", "seq", None),
-        P("dp", "seq", None),
-        P(("dp", "seq"), None),
-        P(("dp", "seq"), None),
-        P(("dp", "seq"), None),
-        P(("dp", "seq")),
-        P(("dp", "seq")),
-    )
-    return jax.shard_map(shards, mesh=mesh, in_specs=in_specs, out_specs=out_specs, check_vma=False)
+    rows = P("dp", "seq", None)
+    mat = P(("dp", "seq"), None)
+    vec = P(("dp", "seq"))
+    return jax.shard_map(
+        shards, mesh=mesh, in_specs=(rows, rows, P("dp", "seq"), mat, mat, mat, vec, vec),
+        out_specs=(rows, rows, mat, mat, mat, vec, vec), check_vma=False)

time: 417 us -> 196 us (0.47); the launches traced: 411 us -> 195 us
  other arithmetic: 209 us -> 4.88 us
  Pallas kernels: 80.7 us -> 167 us
  local copies, waits for them, and re-layouts: 78 us -> 16.1 us
  matrix products: 31.9 us -> 0 us
  starting transfers between devices: 10.4 us -> 0 us
  between operations: 1.78 us -> 7.32 us
    reduce_sum x12 -> x0, other arithmetic: 118 us -> none  [the longest x8 61.3 us: block_pass(): jnp.sum(jnp.where(same, glu_pad[tap:tap + rows].astype(jnp.float32) * d_m...]
    pallas_call x0 -> x1, Pallas kernels: none -> 88.4 us  [mid(): pl.pallas_call(mid_kernel, out_shape=(jax.ShapeDtypeStruct((ROWS, D), BF)...]
    another operation x2 -> x0, other arithmetic: 81.3 us -> none
    another operation x32 -> x2, local copies, waits for them, and re-layouts: 45.6 us -> 0.66 us  [the longest x1 0.61 us: colours(): jnp.stack(counts).astype(jnp.int32)]
    dot_general x6 -> x0, matrix products: 31.9 us -> none  [the longest x1 7.63 us: block_pass(): d_ln_in = jnp.dot(d_pre, w_in.T, preferred_element_type=jnp.float32)]
    concatenate x2 -> x1, local copies, waits for them, and re-layouts: 11.8 us -> 0.86 us  [shards(): jnp.concatenate([w_in.astype(F32), w_out.astype(F32), kernel.astype(F32),...]
    ppermute x4 -> x0, starting transfers between devices: 10.4 us -> none  [the longest x2 6.07 us: with_halo(): before = lax.ppermute(last, axis, up)]
    unnamed x109 -> x14, local copies, waits for them, and re-layouts: 12.1 us -> 9.8 us
  transfers between devices with their start and end apart: 4 -> 0, of which waited for: 0 -> 0; matrix products, arithmetic and copies ran while one was open for 26% -> 0% of each run, Pallas kernels for 0% -> 0%
where the time goes in v2:
time: 196 us; the launch traced here: 195 us
  Pallas kernels  167 us (85%)
  local copies, waits for them, and re-layouts  16.1 us (8%)
  between operations  7.32 us (4%)
  other arithmetic  4.88 us (2%)
    pallas_call x1, Pallas kernels, mid(): pl.pallas_call(mid_kernel, out_shape=(jax.ShapeDtypeStruct((ROWS, D), BF)...  88.4 us
    pallas_call x1, Pallas kernels, gather(): pl.pallas_call(gather_kernel, out_shape=(jax.ShapeDtypeStruct((4, 4, 4, 1...  39.4 us
    pallas_call x1, Pallas kernels, scatter(): pl.pallas_call(scatter_kernel, out_shape=jax.ShapeDtypeStruct((8, WIDE),...  39 us
    unnamed x14, local copies, waits for them, and re-layouts  9.8 us

profile of v2, /device:TPU:1, one launch (start us, length us, event | category | flops | bytes accessed | tf_op | source)
XLA Modules:
  0.0 195.2 jit_solution(9924871105841276595)
XLA Ops:
  0.6 0.7 bitcast_convert_fusion.1
  1.3 0.7 bitcast_convert_fusion
  2.0 1.3 fusion.2
  4.5 0.1 copy.21
  4.6 0.1 copy.20
  4.7 0.7 reduce
  5.4 0.9 concatenate.18.shard_ref
  6.3 0.2 broadcast_in_dim.53.seg_ref
  6.4 1.4 copy-done.2
  7.8 1.4 copy-done.3
  9.2 39.4 %gather_weights.1 = (bf16[4,4,4,16,3328]{4,3,2,1,0:T(8,128)(2,1)S(1)}, bf16[64,1024]{1,0:T(8,128)(2,1)S(1)}, bf16[32,1024]{1,0:T(8,128)(2,1)S(1)}, bf16[64,128]{1,0:T(8,128)(2,1)S(1)}) custom-call(f32[8,3328]{1,0:T(8,128)S(1)} %concatenate.18.shard_ref, bf16[768,1024]{1,0:T(8,128)(2,1)S(1)} %bitcast.41, bf16[768,1024]{1,0:T(8,128)(2,1)S(1)} %bitcast.43, ...), custom_call_target="tpu_custom_call" | custom-call | tf_op jit(solution)/shard_map/gather_weights/pallas_call | solution.py:162
  48.7 2.8 %copy-done = bf16[4,4,4,16,3328]{4,3,2,1,0:T(8,128)(2,1)} copy-done((bf16[4,4,4,16,3328]{4,3,2,1,0:T(8,128)(2,1)}, bf16[4,4,4,16,3328]{4,3,2,1,0:T(8,128)(2,1)S(1)}, u32[]{:S(2)}) %copy-start) | copy-done | bytes 6815768
  51.4 0.7 copy-done.4
  52.1 0.6 copy-done.5
  52.7 0.1 fusion.1
  52.8 0.1 pad_add_fusion
  53.0 0.8 slice_reduce_fusion.6
  56.4 0.8 slice_reduce_fusion.2
  59.8 0.6 stack.74.counts
  60.4 0.3 slice_remainder_fusion
  60.7 0.2 slice_remainder_fusion.2
  61.0 0.1 pad_add_fusion.2
  61.1 0.2 and_select_fusion
  61.3 0.2 and_select_fusion.4
  61.6 0.6 broadcast_in_dim.56.table
  62.2 88.4 %block_pass.1 = (bf16[768,1024]{1,0:T(8,128)(2,1)}, bf16[768,1024]{1,0:T(8,128)(2,1)}, bf16[1024,3328]{1,0:T(8,128)(2,1)}) custom-call(s32[8]{0:T(128)} %stack.74.counts, f32[12,8,256]{2,1,0:T(8,128)} %broadcast_in_dim.56.table, bf16[256,256]{1,0:T(8,128)(2,1)} %constant.61.clone.basis, f32[256,128]{1,0:T(8,128)} %constant.62.clone.spread, ...), custom_call_target="tpu_custom_call" | custom-call | tf_op jit(solution)/shard_map/block_pass/pallas_call | solution.py:622
  150.7 2.9 %copy-done.1 = bf16[1024,3328]{1,0:T(8,128)(2,1)S(1)} copy-done((bf16[1024,3328]{1,0:T(8,128)(2,1)S(1)}, bf16[1024,3328]{1,0:T(8,128)(2,1)}, u32[]{:S(2)}) %copy-start.1) | copy-done | bytes 6815768
  153.6 39.0 %scatter_grads.1 = f32[8,3328]{1,0:T(8,128)S(1)} custom-call(bf16[4,4,4,16,3328]{4,3,2,1,0:T(8,128)(2,1)S(1)} %bitcast.39), custom_call_target="tpu_custom_call" | custom-call | tf_op jit(solution)/shard_map/scatter_grads/pallas_call | solution.py:347
  192.6 0.7 slice_reduce_fusion
  193.3 0.6 slice.121
  193.9 0.6 slice.120
  194.6 0.6 slice.119
  (25 shorter events, 0.2 us)
Async XLA Ops:
  6.4 1.4 copy-start.2
  7.8 1.4 copy-start.3
  9.2 51.1 %copy-start.6 = (s32[1,768]{1,0:T(1,128)S(1)}, s32[1,768]{1,0:T(1,128)}, u32[]{:S(2)}) copy-start(s32[1,768]{1,0:T(1,128)} %param.13) | copy-start | bytes 9220
  48.6 2.8 %copy-start = (bf16[4,4,4,16,3328]{4,3,2,1,0:T(8,128)(2,1)}, bf16[4,4,4,16,3328]{4,3,2,1,0:T(8,128)(2,1)S(1)}, u32[]{:S(2)}) copy-start(bf16[4,4,4,16,3328]{4,3,2,1,0:T(8,128)(2,1)S(1)} %get-tuple-element.17) | copy-start | bytes 20447236
  51.4 0.7 copy-start.4
  52.1 0.6 copy-start.5
  150.7 2.9 %copy-start.1 = (bf16[1024,3328]{1,0:T(8,128)(2,1)S(1)}, bf16[1024,3328]{1,0:T(8,128)(2,1)}, u32[]{:S(2)}) copy-start(bf16[1024,3328]{1,0:T(8,128)(2,1)} %get-tuple-element.20) | copy-start | bytes 20447236

commit v3 on v2

--- a/solution.py
+++ b/solution.py
@@ -51,33 +51,40 @@
 
 
 def gather_kernel(
-    shard_ref, frames_ref, cot_ref, seg_ref,
-    out_ref, hf_ref, hc_ref, hs_ref,
-    buf, sib, sib_sem, halo_send, halo_recv, a_send, a_recv, s_send, s_recv, out_sem,
+    w_in_ref, w_out_ref, small_ref, seg_ref, frames_ref, cot_ref,
+    out_ref, hf_ref, hc_ref, ids_ref,
+    buf, shard, sib, segs, sib_sem, halo_send, halo_recv, a_send, a_recv, s_send, s_recv, out_sem,
 ):
     me, core = place()
     sibling = dev(me, 1 - core)
-    right = (lax.axis_index("dp"), (lax.axis_index("seq") + 1) % 8)
-    left = (lax.axis_index("dp"), (lax.axis_index("seq") + 7) % 8)
+    seq = lax.axis_index("seq")
+    right = (lax.axis_index("dp"), (seq + 1) % 8)
+    left = (lax.axis_index("dp"), (seq + 7) % 8)
     cross = dev(moved(me, "z", 2 * core - 1), 1 - core)
     targets = [dev(moved(me, a, b), core) for a in "yxz" for b in (1, -1)]
+    shard[:, 0:2048] = w_in_ref[...].astype(jnp.float32)
+    shard[:, 2048:3072] = w_out_ref[...].astype(jnp.float32)
+    shard[:, 3072:] = small_ref[...]
     greet(targets + [sibling, cross])
 
     first = pltpu.make_async_remote_copy(
-        src_ref=shard_ref, dst_ref=sib, send_sem=sib_sem.at[0], recv_sem=sib_sem.at[1],
+        src_ref=shard, dst_ref=sib, send_sem=sib_sem.at[0], recv_sem=sib_sem.at[1],
         device_id=sibling, device_id_type=MESH)
     first.start()
     halos = []
     rows = frames_ref.shape[0]
-    for n, (src, dst, h) in enumerate(((frames_ref, hf_ref, HALO), (cot_ref, hc_ref, 16), (seg_ref, hs_ref, HALO))):
+    for n, (src, dst, h) in enumerate(((frames_ref, hf_ref, HALO), (cot_ref, hc_ref, 16))):
         for m, (at, to, who) in enumerate(((rows - h, 0, right), (0, h, left))):
-            cp = pltpu.make_async_remote_copy(
+            halos.append(pltpu.make_async_remote_copy(
                 src_ref=src.at[pl.ds(at, h)], dst_ref=dst.at[pl.ds(to, h)],
                 send_sem=halo_send.at[n, m], recv_sem=halo_recv.at[n, m],
-                device_id=who, device_id_type=MESH)
-            halos.append(cp)
+                device_id=who, device_id_type=MESH))
+    for m, who in enumerate((right, left)):
+        halos.append(pltpu.make_async_remote_copy(
+            src_ref=seg_ref, dst_ref=segs.at[m], send_sem=halo_send.at[2, m], recv_sem=halo_recv.at[2, m],
+            device_id=who, device_id_type=MESH))
     first.wait()
-    mine, other = shard_ref[...], sib[...]
+    mine, other = shard[...], sib[...]
     low = jnp.where(core == 0, mine[:, :HALFW], other[:, HALFW:])
     high = jnp.where(core == 0, other[:, :HALFW], mine[:, HALFW:])
     buf[me["y"], me["x"], me["z"], :, pl.ds(pl.multiple_of(core * HALFW, 128), HALFW)] = jnp.concatenate(
@@ -135,6 +142,14 @@
                     cp = to_sibling(p, 1 + which, idx)
                     cp.start()
                     sends.append(cp)
+    outs = []
+
+    def flush(p, c, n):
+        at = (slice(None),) * 4 + (cols(p, 0, PARTS[p][1], c),)
+        cp = pltpu.make_async_copy(buf.at[at], out_ref.at[at], out_sem.at[p, n])
+        cp.start()
+        outs.append(cp)
+
     for p in range(3):
         _, width, half = PARTS[p]
         opp = block(p, 2, 2)
@@ -143,35 +158,42 @@
         cp = to_sibling(p, 3, opp)
         cp.start()
         sends.append(cp)
+        flush(p, core, 0)
+    for cp in halos:
+        cp.wait()
+    own = seg_ref[...]
+    before = jnp.where(seq == 0, jnp.broadcast_to(own[0:1, 0:1] - 1, (1, 128)), segs[0, 5:6, :])
+    after = jnp.where(seq == 7, jnp.broadcast_to(own[5:6, 127:128] + 1, (1, 128)), segs[1, 0:1, :])
+    ids_ref[...] = jnp.concatenate([before, own, after], axis=0).astype(jnp.float32)
     for p in range(3):
         for which, by in ((0, 0), (1, -1), (2, 1), (3, 2)):
             to_sibling(p, which, block(p, 2, by), 1 - core).wait_recv()
-    out = pltpu.make_async_copy(buf, out_ref, out_sem)
-    out.start()
+        flush(p, 1 - core, 1)
     for cp in sends:
         cp.wait_send()
-    for cp in halos:
+    for cp in outs:
         cp.wait()
-    out.wait()
-
-
-def gather(shard, frames, cot, seg):
+
+
+def gather(w_in, w_out, small, seg, frames, cot):
     bf = jnp.bfloat16
     vm = pl.BlockSpec(memory_space=pltpu.VMEM)
-    hbm = pl.BlockSpec(memory_space=pl.ANY)
+    hbm = pl.BlockSpec(memory_space=pltpu.HBM)
     return pl.pallas_call(
         gather_kernel,
         out_shape=(
             jax.ShapeDtypeStruct((4, 4, 4, 16, WIDE), bf),
             jax.ShapeDtypeStruct((2 * HALO, 1024), bf),
             jax.ShapeDtypeStruct((32, 1024), bf),
-            jax.ShapeDtypeStruct((2 * HALO, 128), bf),
+            jax.ShapeDtypeStruct((8, 128), jnp.float32),
         ),
-        in_specs=[vm, hbm, hbm, hbm],
+        in_specs=[vm, vm, vm, vm, hbm, hbm],
         out_specs=(hbm, vm, vm, vm),
         scratch_shapes=[
             pltpu.VMEM((4, 4, 4, 16, WIDE), bf),
             pltpu.VMEM((8, WIDE), jnp.float32),
+            pltpu.VMEM((8, WIDE), jnp.float32),
+            pltpu.VMEM((2, 6, 128), jnp.int32),
             pltpu.SemaphoreType.DMA((2,)),
             pltpu.SemaphoreType.DMA((3, 2)),
             pltpu.SemaphoreType.DMA((3, 2)),
@@ -179,16 +201,12 @@
             pltpu.SemaphoreType.DMA((3, 3, 4)),
             pltpu.SemaphoreType.DMA((3, 4)),
             pltpu.SemaphoreType.DMA((3, 4)),
-            pltpu.SemaphoreType.DMA,
+            pltpu.SemaphoreType.DMA((3, 2)),
         ],
         compiler_params=pltpu.CompilerParams(
-            collective_id=0, has_side_effects=True, vmem_limit_bytes=24 << 20),
+            collective_id=0, has_side_effects=True, vmem_limit_bytes=48 << 20),
         name="gather_weights",
-    )(shard, frames, cot, seg)
-
-
-def shapes_of(full):
-    return tuple(4 if a in full else 1 for a in "yxz")
+    )(w_in, w_out, small, seg, frames, cot)
 
 
 def scatter_kernel(
@@ -347,7 +365,7 @@
     return pl.pallas_call(
         scatter_kernel,
         out_shape=jax.ShapeDtypeStruct((8, WIDE), jnp.float32),
-        in_specs=[pl.BlockSpec(memory_space=pl.ANY)],
+        in_specs=[pl.BlockSpec(memory_space=pltpu.HBM)],
         out_specs=pl.BlockSpec(memory_space=pltpu.VMEM),
         scratch_shapes=[
             pltpu.VMEM((4, 4, 4, 16, HALFW), bf),
@@ -369,7 +387,7 @@
             pltpu.SemaphoreType.DMA((2,)),
         ],
         compiler_params=pltpu.CompilerParams(
-            collective_id=1, has_side_effects=True, vmem_limit_bytes=32 << 20),
+            collective_id=1, has_side_effects=True, vmem_limit_bytes=48 << 20),
         name="scatter_grads",
     )(g)
 
@@ -390,24 +408,8 @@
     spread[:, :31] = np.concatenate([np.cos(lag), np.sin(lag)], axis=0) * (2 / NFFT)
     back = np.zeros((128, NFFT))
     back[:31] = np.concatenate([np.cos(lag), -np.sin(lag)], axis=0).T * (2 / NFFT)
-    return (jnp.asarray(basis, jnp.bfloat16), jnp.asarray(spread, jnp.float32), jnp.asarray(back, jnp.float32))
-
-
-def colours(ids):
-    step = ids[HALF:] - ids[:-HALF]
-    fwd_at, bwd_at = (0, 208, 416, 592), (16, 208, 400, 592)
-    counts, rows = [], []
-    for starts, length in ((fwd_at, 240), (bwd_at, 224)):
-        for at in starts:
-            count = jnp.max(step[at : at + length - HALF]) + 1
-            counts.append(count)
-            own = jnp.pad(ids[at : at + length] % count, (0, NFFT - length), constant_values=-1)
-            rows.append(own)
-    inner = jnp.arange(NFFT)
-    for w in range(4):
-        rows.append(jnp.where((inner >= 16) & (inner < 208), rows[4 + w], -1))
-    table = jnp.stack(rows).astype(jnp.float32)
-    return jnp.stack(counts).astype(jnp.int32), jnp.broadcast_to(table[:, None, :], (12, 8, NFFT))
+    f32 = jnp.float32
+    return (jnp.asarray(basis, f32), jnp.asarray(basis.T, f32), jnp.asarray(spread, f32), jnp.asarray(back, f32))
 
 
 def sigmoid(v):
@@ -432,10 +434,43 @@
     return jnp.sum(v, axis=-1, keepdims=True) * (1.0 / D)
 
 
+FWD_AT, BWD_AT = (0, 208, 416, 592), (16, 208, 400, 592)
+
+
+def colours(ids, table, across):
+    lane = lax.broadcasted_iota(jnp.int32, (1, 128), 1)
+    wide = lax.broadcasted_iota(jnp.int32, (1, NFFT), 1)
+    counts = []
+    for n, at in enumerate(FWD_AT + BWD_AT):
+        length = 240 if n < 4 else 224
+        r, o = divmod(at + 96, 128)
+
+        def piece(k, o=o):
+            if o == 0:
+                return ids[k : k + 1, :]
+            first = pltpu.roll(ids[k : k + 1, :], 128 - o, 1)
+            return jnp.where(lane < 128 - o, first, pltpu.roll(ids[min(k + 1, 7) : min(k + 1, 7) + 1, :], 128 - o, 1))
+
+        own = jnp.concatenate([piece(r), piece(r + 1)], axis=1)
+        step = jnp.where(wide < length - HALF, pltpu.roll(own, NFFT - HALF, 1) - own, 0.0)
+        count = jnp.max(step) + 1.0
+        own = own + 1.0
+        own = own - count * jnp.floor((own + 0.5) / count)
+        own = jnp.where(wide < length, own, -1.0)
+        rows = jnp.broadcast_to(own, (8, NFFT))
+        table[n] = rows
+        across[n] = jnp.broadcast_to(rows.T[:, 0:1], (NFFT, 128))
+        if n >= 4:
+            table[n + 4] = jnp.where((wide >= 16) & (wide < 208), rows, -1.0)
+        counts.append(count.astype(jnp.int32))
+    return counts
+
+
 def mid_kernel(
-    counts, table, basis, spread, back, frames, cot, hf, hc, w_hbm,
-    out_ref, igrad_ref, g_hbm,
-    xe, ce, w, ln, glu, sig, mixed, work, act, dm, dpre, g, spec, prod, gains, extra, inv_in, mean_in, sems,
+    ids, basis, turned, spread, back, frames, cot, hf, hc, w_hbm,
+    out_hbm, igrad_hbm, g_hbm,
+    xe, ce, w, ln, glu, sig, mixed, work, act, dm, dpre, g, spec, prod, gains, extra, inv_in, mean_in,
+    table, across, counts, out, sems,
 ):
     scale = 1.0 / math.sqrt(98304.0)
 
@@ -444,16 +479,21 @@
         c.start()
         return c
 
+    cols = lambda lo, n: (slice(None), pl.ds(lo, n))
     loads = [
-        cp(frames, xe.at[pl.ds(32, ROWS)], 0),
+        cp(w_hbm.at[cols(3072, 256)], w.at[cols(3072, 256)], 0),
         cp(hf.at[pl.ds(0, 32)], xe.at[pl.ds(0, 32)], 1),
         cp(hf.at[pl.ds(32, 32)], xe.at[pl.ds(800, 32)], 2),
-        cp(w_hbm, w, 3),
-        cp(cot, ce.at[pl.ds(16, ROWS)], 4),
-        cp(hc.at[pl.ds(0, 16)], ce.at[pl.ds(0, 16)], 5),
-        cp(hc.at[pl.ds(16, 16)], ce.at[pl.ds(784, 16)], 6),
+        cp(frames, xe.at[pl.ds(32, ROWS)], 3),
+        cp(w_hbm.at[cols(0, 2048)], w.at[cols(0, 2048)], 4),
+        cp(w_hbm.at[cols(2048, 1024)], w.at[cols(2048, 1024)], 5),
+        cp(cot, ce.at[pl.ds(16, ROWS)], 6),
+        cp(hc.at[pl.ds(0, 16)], ce.at[pl.ds(0, 16)], 7),
+        cp(hc.at[pl.ds(16, 16)], ce.at[pl.ds(784, 16)], 8),
     ]
-    loads[3].wait()
+    for n, count in enumerate(colours(ids, table, across)):
+        counts[n] = count
+    loads[0].wait()
     taps = w[:, 3072:3200].astype(F32).T
     gains[0:8, :] = jnp.broadcast_to(taps[31:32, :], (8, D))
     gains[8:16, :] = jnp.broadcast_to(taps[32:33, :], (8, D))
@@ -462,19 +502,26 @@
     dm[pl.ds(800, 32), :] = jnp.zeros((32, D), BF)
     prod[...] = jnp.zeros((NFFT, D), F32)
     extra[...] = jnp.zeros((128, D), F32)
-    for n in (0, 1, 2):
+    for n in (1, 2, 3):
         loads[n].wait()
 
-    @pl.loop(0, 52)
+    def strips(i, n, off=0):
+        return [pl.ds(pl.multiple_of(i * (16 * n) + off + 16 * u, 16), 16) for u in range(n)]
+
+    @pl.loop(0, 13)
     def _(i):
-        at = pl.ds(pl.multiple_of(i * 16, 16), 16)
-        x = xe[at, :].astype(F32)
-        mean = row_mean(x)
-        cen = x - mean
-        inv = lax.rsqrt(row_mean(cen * cen) + EPS)
-        ln[at, :] = (cen * inv * gains[0:1, :]).astype(BF)
-        inv_in[at, :] = jnp.broadcast_to(inv, (16, 128))
-        mean_in[at, :] = jnp.broadcast_to(mean, (16, 128))
+        ats = strips(i, 4)
+        gain = gains[0:1, :]
+        xs = [xe[at, :].astype(F32) for at in ats]
+        means = [row_mean(x) for x in xs]
+        cens = [x - m for x, m in zip(xs, means)]
+        invs = [lax.rsqrt(row_mean(c * c) + EPS) for c in cens]
+        for at, c, inv, m in zip(ats, cens, invs, means):
+            ln[at, :] = (c * inv * gain).astype(BF)
+            inv_in[at, :] = jnp.broadcast_to(inv, (16, 128))
+            mean_in[at, :] = jnp.broadcast_to(m, (16, 128))
+
+    loads[4].wait()
 
     @pl.loop(0, 8)
     def _(i):
@@ -488,88 +535,134 @@
         glu[rows, c0] = (value * s).astype(BF)
         sig[rows, c0] = s
 
-    for n in (4, 5, 6):
+    for n in (5, 6, 7, 8):
         loads[n].wait()
 
-    def masked(row, c):
-        hit = table[row, 0:1, :] == c.astype(F32)
-        return jnp.where(hit, basis[...].astype(F32), 0.0).astype(BF)
+    def picked(row, first, k):
+        return jnp.concatenate(
+            [jnp.where(table[row, 0:1, :] == (first + c).astype(F32), basis[...], 0.0) for c in range(k)],
+            axis=0).astype(BF)
+
+    def placed(row, first, k, lo, hi):
+        own = across[row, lo:hi, :]
+        own = jnp.concatenate([own, own], axis=1)
+        return jnp.concatenate(
+            [jnp.where(own == (first + c).astype(F32), turned[lo:hi, :], 0.0) for c in range(k)], axis=1).astype(BF)
+
+    def forward(wi, first, k, add):
+        base = pl.multiple_of(jnp.minimum(wi * 208, 592), 16)
+        to = picked(wi, first, k)
+        fro = placed(wi, first, k, 16, 224)
+        for j in range(4):
+            col = slice(j * 256, j * 256 + 256)
+            x = mm(to, glu[pl.ds(base, 256), col])
+            hr, hi = spec[:128, col], spec[128:, col]
+            ys = []
+            for c in range(k):
+                xr, xi = x[256 * c : 256 * c + 128], x[256 * c + 128 : 256 * c + 256]
+                ys += [(xr * hr - xi * hi).astype(BF), (xr * hi + xi * hr).astype(BF)]
+            y = mm(fro, jnp.concatenate(ys, axis=0))
+            if add:
+                mixed[pl.ds(base, 208), col] += y
+            else:
+                mixed[pl.ds(base, 208), col] = y
+
+    def backward(wi, first, k, add):
+        base = pl.multiple_of(wi * 192, 16)
+        to = picked(4 + wi, first, k)
+        mid_to = picked(8 + wi, first, k)
+        fro = placed(4 + wi, first, k, 16, 208)
+        for j in range(4):
+            col = slice(j * 256, j * 256 + 256)
+            d = mm(to, dm[pl.ds(base, 256), col])
+            q = mm(mid_to, glu[pl.ds(base + 16, 256), col])
+            hr, hi = spec[:128, col], spec[128:, col]
+            ys = []
+            pr, pi = prod[:128, col], prod[128:, col]
+            for c in range(k):
+                lo, mi, up = 256 * c, 256 * c + 128, 256 * c + 256
+                dr, di, qr, qi = d[lo:mi], d[mi:up], q[lo:mi], q[mi:up]
+                ys += [(dr * hr + di * hi).astype(BF), (di * hr - dr * hi).astype(BF)]
+                pr = pr + (qr * dr + qi * di)
+                pi = pi + (qi * dr - qr * di)
+            prod[:128, col] = pr
+            prod[128:, col] = pi
+            y = mm(fro, jnp.concatenate(ys, axis=0))
+            if add:
+                mixed[pl.ds(base, 192), col] += y
+            else:
+                mixed[pl.ds(base, 192), col] = y
+
+    def by_class(run, wi, count, length, step):
+        zero = jnp.int32(0)
+
+        @pl.when(count <= 2)
+        def _():
+            run(wi, zero, 2, False)
+
+        @pl.when(count == 3)
+        def _():
+            run(wi, zero, 3, False)
+
+        @pl.when(count > 3)
+        def _():
+            base = pl.multiple_of(jnp.minimum(wi * step, 592), 16)
+            mixed[pl.ds(base, length), :] = jnp.zeros((length, D), F32)
+
+            @pl.loop(0, (count + 3) // 4)
+            def _(n):
+                run(wi, n * 4, 4, True)
 
     @pl.loop(0, 4)
     def _(wi):
-        base = pl.multiple_of(jnp.minimum(wi * 208, 592), 16)
-        mixed[pl.ds(base, 208), :] = jnp.zeros((208, D), F32)
-
-        @pl.loop(0, counts[wi])
-        def _(c):
-            cm = masked(wi, c)
-            inv = cm.T[16:224, :]
-            for j in range(4):
-                col = slice(j * 256, j * 256 + 256)
-                x = mm(cm, glu[pl.ds(base, 256), col])
-                xr, xi = x[:128], x[128:]
-                hr, hi = spec[:128, col], spec[128:, col]
-                y = jnp.concatenate([xr * hr - xi * hi, xr * hi + xi * hr], axis=0).astype(BF)
-                mixed[pl.ds(base, 208), col] += mm(inv, y)
+        by_class(forward, wi, counts[wi], 208, 208)
 
     @pl.loop(0, 4)
     def _(j):
         col = pl.ds(pl.multiple_of(j * 256, 256), 256)
         work[:, col] = nt(ce[...], w[col, 2048:3072])
 
-    def mid_rows(i, central):
-        at = pl.ds(pl.multiple_of(i * 16, 16), 16)
+    def mid_rows(ats, central):
         gain = gains[8:9, :]
-        m = mixed[at, :]
-        cen = m - row_mean(m)
-        inv = lax.rsqrt(row_mean(cen * cen) + EPS)
-        normal = cen * inv
-        y = normal * gain
-        s = sigmoid(y)
-        ys = y * s
-        act[at, :] = ys.astype(BF)
-        d_ln = work[at, :] * (s + ys * (1.0 - s))
-        if central:
-            dn = d_ln * normal
-            extra[40:48, :] += dn[:8] + dn[8:]
-        u = d_ln * gain
-        dm[at, :] = (inv * (u - row_mean(u) - normal * row_mean(u * normal))).astype(BF)
-
-    mid_rows(0, False)
-    mid_rows(49, False)
-
-    @pl.loop(1, 49)
+        cens = [mixed[at, :] for at in ats]
+        cens = [m - row_mean(m) for m in cens]
+        invs = [lax.rsqrt(row_mean(c * c) + EPS) for c in cens]
+        normals = [c * inv for c, inv in zip(cens, invs)]
+        us = []
+        for at, normal in zip(ats, normals):
+            y = normal * gain
+            s = sigmoid(y)
+            ys = y * s
+            act[at, :] = ys.astype(BF)
+            d_ln = work[at, :] * (s + ys * (1.0 - s))
+            if central:
+                dn = d_ln * normal
+                extra[40:48, :] += dn[:8] + dn[8:]
+            us.append(d_ln * gain)
+        m1 = [row_mean(u) for u in us]
+        m2 = [row_mean(u * n) for u, n in zip(us, normals)]
+        for at, inv, u, n, a, b in zip(ats, invs, us, normals, m1, m2):
+            dm[at, :] = (inv * (u - a - n * b)).astype(BF)
+
+    mid_rows([pl.ds(0, 16), pl.ds(784, 16)], False)
+
+    @pl.loop(0, 24)
     def _(i):
-        mid_rows(i, True)
+        mid_rows(strips(i, 2, 16), True)
 
     @pl.loop(0, 4)
     def _(j):
         col = pl.ds(pl.multiple_of(j * 256, 256), 256)
         y = mm(act[16:784, :], w[:, pl.ds(pl.multiple_of(2048 + j * 256, 256), 256)])
-        out_ref[:, col] = (xe[32:800, col].astype(F32) + y).astype(BF)
+        out[:, col] = (xe[32:800, col].astype(F32) + y).astype(BF)
         lhs = act[16:784, col].T
         g[col, 2048:3072] = (mm(lhs, ce[16:784, :]) * scale).astype(BF)
 
+    stores = [cp(out, out_hbm, 9), cp(g.at[cols(2048, 1024)], g_hbm.at[cols(2048, 1024)], 10)]
+
     @pl.loop(0, 4)
     def _(wi):
-        base = pl.multiple_of(wi * 192, 16)
-        mixed[pl.ds(base, 192), :] = jnp.zeros((192, D), F32)
-
-        @pl.loop(0, counts[4 + wi])
-        def _(c):
-            cm = masked(4 + wi, c)
-            cg = masked(8 + wi, c)
-            inv = cm.T[16:208, :]
-            for j in range(4):
-                col = slice(j * 256, j * 256 + 256)
-                d = mm(cm, dm[pl.ds(base, 256), col])
-                q = mm(cg, glu[pl.ds(base + 16, 256), col])
-                dr, di, qr, qi = d[:128], d[128:], q[:128], q[128:]
-                hr, hi = spec[:128, col], spec[128:, col]
-                y = jnp.concatenate([dr * hr + di * hi, di * hr - dr * hi], axis=0).astype(BF)
-                prod[:128, col] += qr * dr + qi * di
-                prod[128:, col] += qi * dr - qr * di
-                mixed[pl.ds(base, 192), col] += mm(inv, y)
+        by_class(backward, wi, counts[4 + wi], 192, 192)
 
     @pl.loop(0, 48)
     def _(i):
@@ -586,38 +679,55 @@
         col = pl.ds(pl.multiple_of(j * 256, 256), 256)
         lhs = ln[32:800, col].T
         for n in range(4):
-            cols = slice(n * 512, n * 512 + 512)
-            g[col, cols] = (mm(lhs, dpre[:, cols]) * scale).astype(BF)
-        work[0:768, col] = nt(dpre[...], w[col, 0:2048])
-
-    @pl.loop(0, 48)
-    def _(i):
-        at = pl.ds(pl.multiple_of(i * 16, 16), 16)
-        ext = pl.ds(pl.multiple_of(i * 16 + 32, 16), 16)
-        inv = inv_in[ext, 0:1]
-        normal = (xe[ext, :].astype(F32) - mean_in[ext, 0:1]) * inv
-        d = work[at, :]
-        dn = d * normal
-        extra[48:56, :] += dn[:8] + dn[8:]
-        u = d * gains[0:1, :]
-        back_in = inv * (u - row_mean(u) - normal * row_mean(u * normal))
-        c = ce[pl.ds(pl.multiple_of(i * 16 + 16, 16), 16), :].astype(F32)
-        igrad_ref[at, :] = (c + back_in).astype(BF)
-
+            c = slice(n * 512, n * 512 + 512)
+            g[col, c] = (mm(lhs, dpre[:, c]) * scale).astype(BF)
+
+    stores.append(cp(g.at[cols(0, 2048)], g_hbm.at[cols(0, 2048)], 11))
     gk = jnp.dot(back[...], prod[...], precision=lax.Precision.HIGHEST, preferred_element_type=F32)
     extra[0:31, :] = gk[0:31]
+
+    @pl.loop(0, 4)
+    def _(j):
+        col = pl.ds(pl.multiple_of(j * 256, 256), 256)
+        work[0:768, col] = nt(dpre[...], w[col, 0:2048])
+
+    stores[0].wait()
+
+    @pl.loop(0, 12)
+    def _(i):
+        ats, exts, ces = strips(i, 4), strips(i, 4, 32), strips(i, 4, 16)
+        invs = [inv_in[e, 0:1] for e in exts]
+        normals = [(xe[e, :].astype(F32) - mean_in[e, 0:1]) * inv for e, inv in zip(exts, invs)]
+        us = []
+        gain = gains[0:1, :]
+        total = None
+        for at, normal in zip(ats, normals):
+            d = work[at, :]
+            dn = d * normal
+            dn = dn[:8] + dn[8:]
+            total = dn if total is None else total + dn
+            us.append(d * gain)
+        extra[48:56, :] += total
+        m1 = [row_mean(u) for u in us]
+        m2 = [row_mean(u * n) for u, n in zip(us, normals)]
+        for at, c, inv, u, n, a, b in zip(ats, ces, invs, us, normals, m1, m2):
+            out[at, :] = (ce[c, :].astype(F32) + inv * (u - a - n * b)).astype(BF)
+
+    stores.append(cp(out, igrad_hbm, 12))
     g_mid = jnp.sum(extra[40:48, :], axis=0, keepdims=True)
     g_in = jnp.sum(extra[48:56, :], axis=0, keepdims=True)
     extra[31:32, :] = g_in
     extra[32:33, :] = g_mid
     g[:, 3072:3200] = (extra[...].T * scale).astype(BF)
     g[:, 3200:3328] = jnp.zeros((D, 128), BF)
-    cp(g, g_hbm, 7).wait()
-
-
-def mid(counts, table, consts, frames, cot, hf, hc, w):
+    stores.append(cp(g.at[cols(3072, 256)], g_hbm.at[cols(3072, 256)], 13))
+    for s in stores[1:]:
+        s.wait()
+
+
+def mid(ids, consts, frames, cot, hf, hc, w):
     vm = pl.BlockSpec(memory_space=pltpu.VMEM)
-    hbm = pl.BlockSpec(memory_space=pl.ANY)
+    hbm = pl.BlockSpec(memory_space=pltpu.HBM)
     V = pltpu.VMEM
     return pl.pallas_call(
         mid_kernel,
@@ -626,37 +736,28 @@
             jax.ShapeDtypeStruct((ROWS, D), BF),
             jax.ShapeDtypeStruct((D, WIDE), BF),
         ),
-        in_specs=[pl.BlockSpec(memory_space=pltpu.SMEM), vm, vm, vm, vm, hbm, hbm, hbm, hbm, hbm],
-        out_specs=(vm, vm, hbm),
+        in_specs=[vm, vm, vm, vm, vm, hbm, hbm, hbm, hbm, hbm],
+        out_specs=(hbm, hbm, hbm),
         scratch_shapes=[
             V((832, D), BF), V((800, D), BF), V((D, WIDE), BF),
             V((832, D), BF), V((848, D), BF), V((832, D), F32),
             V((800, D), F32), V((800, D), F32), V((800, D), BF), V((832, D), BF),
             V((768, 2 * D), BF), V((D, WIDE), BF), V((NFFT, D), F32), V((NFFT, D), F32),
             V((16, D), F32), V((128, D), F32), V((832, 128), F32), V((832, 128), F32),
-            pltpu.SemaphoreType.DMA((8,)),
+            V((12, 8, NFFT), F32), V((8, NFFT, 128), F32), pltpu.SMEM((8,), jnp.int32), V((ROWS, D), BF),
+            pltpu.SemaphoreType.DMA((14,)),
         ],
         compiler_params=pltpu.CompilerParams(vmem_limit_bytes=60 << 20),
         name="block_pass",
-    )(counts, table, *consts, frames, cot, hf, hc, w)
+    )(ids, *consts, frames, cot, hf, hc, w)
 
 
 def shards(frames, cotangent, segments, w_in, w_out, kernel, gain_in, gain_mid):
-    frame_rows = frames[0]
-    cot_rows = cotangent[0]
-    packed = jnp.concatenate(
-        [w_in.astype(F32), w_out.astype(F32), kernel.astype(F32), gain_in.astype(F32)[:, None],
-         gain_mid.astype(F32)[:, None], jnp.zeros((8, WIDE - 3072 - 33), F32)], axis=1)
-    seg_rows = jnp.broadcast_to(segments[0].astype(BF)[:, None], (ROWS, 128))
-    full, f_halo, c_halo, seg_halo = gather(packed, frame_rows, cot_rows, seg_rows)
-    at = lax.axis_index("seq")
-    halo = seg_halo[:, 0].astype(jnp.int32)
-    own = segments[0]
-    ids = jnp.concatenate([
-        jnp.where(at == 0, own[0] - 1, halo[:HALO]), own, jnp.where(at == 7, own[-1] + 1, halo[HALO:])])
-    counts, table = colours(ids)
+    small = jnp.concatenate(
+        [kernel.astype(F32), gain_in.astype(F32)[:, None], gain_mid.astype(F32)[:, None], jnp.zeros((8, 223), F32)], axis=1)
+    full, f_halo, c_halo, ids = gather(w_in, w_out, small, segments.reshape(6, 128), frames[0], cotangent[0])
     block_out, input_grad, g = mid(
-        counts, table, tables(), frame_rows, cot_rows, f_halo, c_halo, full.reshape(1024, WIDE))
+        ids, tables(), frames[0], cotangent[0], f_halo, c_halo, full.reshape(D, WIDE))
     r = scatter(g.reshape(4, 4, 4, 16, WIDE))
     return (block_out[None], input_grad[None], r[:, :2048], r[:, 2048:3072], r[:, 3072:3103], r[:, 3103], r[:, 3104])
 

time: 196 us -> 147 us (0.75)
  Pallas kernels: 167 us -> 134 us
  local copies, waits for them, and re-layouts: 16.1 us -> 8.96 us
  between operations: 7.32 us -> 0.68 us
  other arithmetic: 4.88 us -> 2.78 us
    pallas_call x1, Pallas kernels: 88.4 us -> 52.1 us  [mid(): pl.pallas_call(mid_kernel, out_shape=(jax.ShapeDtypeStruct((ROWS, D), BF)...]
    unnamed x14, local copies, waits for them, and re-layouts: 9.8 us -> 6.15 us
    pallas_call x1, Pallas kernels: 39 us -> 41.6 us  [scatter(): pl.pallas_call(scatter_kernel, out_shape=jax.ShapeDtypeStruct((8, WIDE),...]
where the time goes in v3:
time: 147 us; the launch traced here: 146 us
  Pallas kernels  134 us (91%)
  local copies, waits for them, and re-layouts  8.96 us (6%)
  other arithmetic  2.78 us (2%)
    pallas_call x1, Pallas kernels, mid(): pl.pallas_call(mid_kernel, out_shape=(jax.ShapeDtypeStruct((ROWS, D), BF)...  52.1 us
    pallas_call x1, Pallas kernels, scatter(): pl.pallas_call(scatter_kernel, out_shape=jax.ShapeDtypeStruct((8, WIDE),...  41.6 us
    pallas_call x1, Pallas kernels, gather(): pl.pallas_call(gather_kernel, out_shape=(jax.ShapeDtypeStruct((4, 4, 4, 1...  39.9 us
    unnamed x14, local copies, waits for them, and re-layouts  6.15 us

profile of v3, /device:TPU:1, one launch (start us, length us, event | category | flops | bytes accessed | tf_op | source)
XLA Modules:
  0.0 146.1 jit_solution(15614073735006768367)
XLA Ops:
  0.6 0.7 bitcast_convert_fusion.1
  1.3 0.7 bitcast_convert_fusion
  1.9 0.1 pad.3.clone
  2.0 0.1 copy.22
  2.1 0.1 copy.21
  2.2 0.7 reduce
  2.9 0.7 convert_element_type.2
  3.6 0.1 maximum_maximum_fusion.small_ref
  3.7 0.0 copy-start
  3.7 1.4 copy-done
  5.1 0.0 copy-start.1
  5.1 1.4 copy-done.1
  6.5 0.0 copy-start.4
  6.5 0.8 copy-done.4
  7.2 0.0 copy-start.5
  7.2 0.7 copy-done.5
  7.9 39.9 %gather_weights.1 = (bf16[4,4,4,16,3328]{4,3,2,1,0:T(8,128)(2,1)}, bf16[64,1024]{1,0:T(8,128)(2,1)S(1)}, bf16[32,1024]{1,0:T(8,128)(2,1)S(1)}, f32[8,128]{1,0:T(8,128)S(1)}) custom-call(bf16[8,2048]{1,0:T(8,128)(2,1)S(1)} %copy-done.4, bf16[8,1024]{1,0:T(8,128)(2,1)S(1)} %copy-done.5, f32[8,256]{1,0:T(8,128)S(1)} %maximum_maximum_fusion.small_ref, ...), custom_call_target="tpu_custom_call" | custom-call | tf_op jit(solution)/shard_map/gather_weights/pallas_call | solution.py:182
  47.9 0.0 copy-start.2
  47.9 0.6 copy-done.2
  48.5 0.0 copy-start.3
  48.5 0.6 copy-done.3
  49.2 0.0 copy-start.6
  49.2 0.6 copy-done.6
  49.8 52.1 %block_pass.1 = (bf16[768,1024]{1,0:T(8,128)(2,1)}, bf16[768,1024]{1,0:T(8,128)(2,1)}, bf16[1024,3328]{1,0:T(8,128)(2,1)}) custom-call(f32[8,128]{1,0:T(8,128)} %copy-done.6, f32[256,256]{1,0:T(8,128)} %constant.10.clone.basis, f32[256,256]{1,0:T(8,128)} %constant.11.clone.turned, f32[256,128]{1,0:T(8,128)} %constant.12.clone.spread, ...), custom_call_target="tpu_custom_call" | custom-call | tf_op jit(solution)/shard_map/block_pass/pallas_call | solution.py:732
  101.9 41.6 %scatter_grads.1 = f32[8,3328]{1,0:T(8,128)S(1)} custom-call(bf16[4,4,4,16,3328]{4,3,2,1,0:T(8,128)(2,1)} %bitcast.19), custom_call_target="tpu_custom_call" | custom-call | tf_op jit(solution)/shard_map/scatter_grads/pallas_call | solution.py:365
  143.5 0.7 slice_reduce_fusion
  144.2 0.6 slice.17
  144.8 0.6 slice.16
  145.4 0.6 slice.15
  (1 shorter events, 0.0 us)
Async XLA Ops:
  3.7 1.4 copy-start
  5.1 1.4 copy-start.1
  6.5 0.8 copy-start.4
  7.2 0.7 copy-start.5
  47.9 0.6 copy-start.2
  48.5 0.6 copy-start.3
  49.2 0.6 copy-start.6

commit v4 on v3

--- a/solution.py
+++ b/solution.py
@@ -61,10 +61,12 @@
     right = (lax.axis_index("dp"), (seq + 1) % 8)
     left = (lax.axis_index("dp"), (seq + 7) % 8)
     cross = dev(moved(me, "z", 2 * core - 1), 1 - core)
-    targets = [dev(moved(me, a, b), core) for a in "yxz" for b in (1, -1)]
-    shard[:, 0:2048] = w_in_ref[...].astype(jnp.float32)
-    shard[:, 2048:3072] = w_out_ref[...].astype(jnp.float32)
-    shard[:, 3072:] = small_ref[...]
+    targets = [dev(moved(me, a, b), core) for a in "yxz" for b in (1, -1, 2)]
+    for c in (0, 1):
+        at = c * HALFW
+        shard[:, at : at + 1024] = w_in_ref[:, c * 1024 : c * 1024 + 1024].astype(jnp.float32)
+        shard[:, at + 1024 : at + 1536] = w_out_ref[:, c * 512 : c * 512 + 512].astype(jnp.float32)
+        shard[:, at + 1536 : at + HALFW] = small_ref[...] if c == 0 else jnp.zeros((8, 128), jnp.float32)
     greet(targets + [sibling, cross])
 
     first = pltpu.make_async_remote_copy(
@@ -114,34 +116,34 @@
         return block_index(me, ORDERS[p][:ph], axis, (me[axis] + by + 4) % 4)
 
     sends = []
-    for ph in range(3):
+
+    def go(cp):
+        cp.start()
+        sends.append(cp)
+
+    for ph in range(2):
         for p in range(3):
-            _, width, half = PARTS[p]
+            width = PARTS[p][1]
             if ph > 0:
-                opp = block(p, ph - 1, 2)
-                send(p, ph - 1, 2, opp, 0, half, 1).wait_recv()
-                send(p, ph - 1, 3, opp, half, width - half, -1).wait_recv()
-            own = block(p, ph, 0)
-            for which, by in ((0, 1), (1, -1)):
-                cp = send(p, ph, which, own, 0, width, by)
-                cp.start()
-                sends.append(cp)
-            if ph == 2:
-                cp = to_sibling(p, 0, own)
-                cp.start()
-                sends.append(cp)
-        for p in range(3):
-            _, width, half = PARTS[p]
-            for which, by, lo, w in ((0, -1, 0, half), (1, 1, half, width - half)):
-                idx = block(p, ph, by)
-                send(p, ph, which, idx, 0, width, -by).wait_recv()
-                cp = send(p, ph, which + 2, idx, lo, w, -by)
-                cp.start()
-                sends.append(cp)
-                if ph == 2:
-                    cp = to_sibling(p, 1 + which, idx)
-                    cp.start()
-                    sends.append(cp)
+                for which, by in ((0, -1), (1, 1), (2, 2)):
+                    send(p, 0, which, block(p, 0, by), 0, width, by).wait_recv()
+            for which, by in ((0, 1), (1, -1), (2, 2)):
+                go(send(p, ph, which, block(p, ph, 0), 0, width, by))
+    for p in range(3):
+        width = PARTS[p][1]
+        for which, by in ((0, -1), (1, 1), (2, 2)):
+            send(p, 1, which, block(p, 1, by), 0, width, by).wait_recv()
+        own = block(p, 2, 0)
+        for which, by in ((0, 1), (1, -1)):
+            go(send(p, 2, which, own, 0, width, by))
+        go(to_sibling(p, 0, own))
+    for p in range(3):
+        _, width, half = PARTS[p]
+        for which, by, lo, w in ((0, -1, 0, half), (1, 1, half, width - half)):
+            idx = block(p, 2, by)
+            send(p, 2, which, idx, 0, width, -by).wait_recv()
+            go(send(p, 2, which + 2, idx, lo, w, -by))
+            go(to_sibling(p, 1 + which, idx))
     outs = []
 
     def flush(p, c, n):
@@ -204,148 +206,228 @@
             pltpu.SemaphoreType.DMA((3, 2)),
         ],
         compiler_params=pltpu.CompilerParams(
-            collective_id=0, has_side_effects=True, vmem_limit_bytes=48 << 20),
+            collective_id=0, has_side_effects=True, vmem_limit_bytes=60 << 20),
         name="gather_weights",
     )(w_in, w_out, small, seg, frames, cot)
 
 
-def scatter_kernel(
-    g_ref, out_ref,
-    acc, sibbuf, h0, h1, h2, f0, f1, f2, last, low, fin, own_sem, d_send, d_recv, a_send, a_recv, e_sem,
+def back_kernel(
+    early, ln_hbm, dpre_hbm, w_hbm, frames, cot, inv_hbm, mean_hbm, gains, w_rows, small,
+    o_in, o_out, o_small, igrad_hbm,
+    acc, sibbuf, gsend, h0, f0, f1, f2, last, low, fin,
+    ln, turned, dpre, w, xe, ce, inv_in, mean_in, work, out,
+    load_sem, d_send, d_recv, a_send, a_recv, e_sem,
 ):
+    scale = 1.0 / math.sqrt(98304.0)
+    f32, bf = jnp.float32, jnp.bfloat16
     me, core = place()
     sibling = dev(me, 1 - core)
-    targets = [dev(moved(me, a, b), core) for a in "yxz" for b in (1, -1)]
-    greet(targets + [sibling])
-    hbufs, fbufs = (h0, h1, h2), (f0, f1, f2)
-
-    def cols(p, c):
-        return pl.ds(pl.multiple_of(c * HALFW + PARTS[p][0], 128), PARTS[p][1])
+    full4 = (slice(None),) * 4
+
+    def cp(src, dst, n):
+        c = pltpu.make_async_copy(src, dst, load_sem.at[n])
+        c.start()
+        return c
+
+    def early_cols(c):
+        return full4 + (pl.ds(pl.multiple_of(c * 640, 128), 640),)
 
     def lane(p, lo, w):
         return pl.ds(PARTS[p][0] + lo, w)
 
-    full3 = (slice(None),) * 4
-    owns, gives, sends = [], [], []
-    for p in range(3):
-        give = pltpu.make_async_remote_copy(
-            src_ref=g_ref.at[full3 + (cols(p, 1 - core),)], dst_ref=sibbuf.at[full3 + (lane(p, 0, PARTS[p][1]),)],
+    loads = [
+        cp(ln_hbm, ln, 0),
+        cp(dpre_hbm, dpre, 1),
+        cp(early.at[early_cols(core)], acc.at[full4 + (lane(2, 0, 640),)], 2),
+        cp(w_hbm.at[:, pl.ds(0, 1024)], w.at[:, pl.ds(0, 1024)], 3),
+        cp(w_hbm.at[:, pl.ds(HALFW, 1024)], w.at[:, pl.ds(1024, 1024)], 4),
+        cp(frames, xe, 5),
+        cp(cot, ce, 6),
+        cp(inv_hbm, inv_in, 7),
+        cp(mean_hbm, mean_in, 8),
+    ]
+    targets = [dev(moved(me, a, b), core) for a in "yxz" for b in (1, -1, 2)]
+    greet(targets + [sibling])
+
+    def give(p):
+        src = early.at[early_cols(1 - core)] if p == 2 else gsend.at[full4 + (lane(p, 0, 512),)]
+        return pltpu.make_async_remote_copy(
+            src_ref=src, dst_ref=sibbuf.at[full4 + (lane(p, 0, PARTS[p][1]),)],
             send_sem=d_send.at[p], recv_sem=d_recv.at[p], device_id=sibling, device_id_type=MESH)
-        give.start()
-        own = pltpu.make_async_copy(
-            g_ref.at[full3 + (cols(p, core),)], acc.at[full3 + (lane(p, 0, PARTS[p][1]),)], own_sem.at[p])
-        own.start()
-        owns.append(own)
-        gives.append(give)
+
+    sends = []
+
+    def go(c):
+        c.start()
+        sends.append(c)
 
     def axis_of(p, ph):
         return ORDERS[p][2 - ph]
 
-    def rest(p, ph):
-        return ORDERS[p][: 2 - ph]
-
     def block(p, ph, by):
         axis = axis_of(p, ph)
-        return block_index(me, rest(p, ph), axis, (me[axis] + by + 4) % 4)
-
-    def hview(p, ph, lo, w):
-        nd = 2 - ph
-        return hbufs[ph].at[(slice(None),) * nd + (slice(None), lane(p, lo, w))]
-
-    def fview(p, ph, which, lo, w):
-        nd = 2 - ph
-        return fbufs[ph].at[(which,) + (slice(None),) * nd + (slice(None), lane(p, lo, w))]
-
-    def send_half(p, ph, which):
+        return block_index(me, ORDERS[p][: 2 - ph], axis, (me[axis] + by + 4) % 4)
+
+    def landing(p, ph, which, lo, w):
+        ref = (f0, f1, f2)[ph]
+        return ref.at[(which,) + (slice(None),) * (2 - ph) + (slice(None), lane(p, lo, w))]
+
+    def send_half(p, which):
         _, width, half = PARTS[p]
         lo, w, by = ((0, half, 1), (half, width - half, -1))[which]
         return pltpu.make_async_remote_copy(
-            src_ref=acc.at[block(p, ph, 2) + (slice(None), lane(p, lo, w))], dst_ref=hview(p, ph, lo, w),
-            send_sem=a_send.at[p, ph, which], recv_sem=a_recv.at[p, ph, which],
-            device_id=dev(moved(me, axis_of(p, ph), by), core), device_id_type=MESH)
+            src_ref=acc.at[block(p, 0, 2) + (slice(None), lane(p, lo, w))],
+            dst_ref=h0.at[(slice(None),) * 3 + (lane(p, lo, w),)],
+            send_sem=a_send.at[p, 0, which], recv_sem=a_recv.at[p, 0, which],
+            device_id=dev(moved(me, axis_of(p, 0), by), core), device_id_type=MESH)
 
     def send_full(p, ph, which):
-        _, width, _ = PARTS[p]
-        by = (1, -1)[which]
+        width = PARTS[p][1]
+        by = (1, -1, 2)[which]
         return pltpu.make_async_remote_copy(
-            src_ref=acc.at[block(p, ph, by) + (slice(None), lane(p, 0, width))], dst_ref=fview(p, ph, which, 0, width),
+            src_ref=acc.at[block(p, ph, by) + (slice(None), lane(p, 0, width))], dst_ref=landing(p, ph, which, 0, width),
             send_sem=a_send.at[p, ph, 2 + which], recv_sem=a_recv.at[p, ph, 2 + which],
             device_id=dev(moved(me, axis_of(p, ph), by), core), device_id_type=MESH)
 
-    def over(p, ph, value_axis_index, body):
-        names = rest(p, ph)
-        axis = axis_of(p, ph)
-        n = 4 ** len(names)
-
-        def index(k):
-            digits = [k // 4, k % 4][2 - len(names):] if names else []
-            by_name = dict(zip([a for a in "yxz" if a in names], digits))
-            at = []
-            for a in "yxz":
-                at.append(by_name[a] if a in by_name else (value_axis_index if a == axis else me[a]))
-            return tuple(at), tuple(digits)
-
-        if n == 1:
-            body(*index(0))
+    def over(p, ph, value, body):
+        axis, full = axis_of(p, ph), ORDERS[p][: 2 - ph]
+        names = [a for a in "yxz" if a in full]
+
+        def at(k):
+            by_name = {axis: value}
+            if len(names) == 2:
+                by_name[names[0]] = k
+                by_name[names[1]] = slice(None)
+            elif len(names) == 1:
+                by_name[names[0]] = slice(None)
+            return tuple(by_name[a] if a in by_name else me[a] for a in "yxz")
+
+        if len(names) == 2:
+            @pl.loop(0, 4)
+            def _(k):
+                body(at(k), (k, slice(None)))
         else:
-            def step(k, carry):
-                body(*index(k))
-                return carry
-            lax.fori_loop(0, n, step, 0)
-
-    f32 = jnp.float32
-    for p in range(3):
+            body(at(0), (slice(None),) * len(names))
+
+    def start_halves(p):
+        for which in (0, 1):
+            go(send_half(p, which))
+
+    def pass_on(p):
         start, width, half = PARTS[p]
-        owns[p].wait()
-        gives[p].wait_recv()
+        axis = axis_of(p, 0)
+        for which, by, lo, w in ((0, 1, 0, half), (1, -1, half, width - half)):
+            send_half(p, which).wait_recv()
+            sl = pl.ds(start + lo, w)
+
+            def body(at, dig, sl=sl):
+                at = at + (slice(None), sl)
+                acc[at] = (acc[at].astype(f32) + h0[dig + (slice(None), sl)].astype(f32)).astype(bf)
+            over(p, 0, (me[axis] + by + 4) % 4, body)
+            go(send_full(p, 0, which))
+
+    def take(p, ph):
+        start, width, _ = PARTS[p]
+        count = 2 if ph == 0 else 3
+        ref = (f0, f1, f2)[ph]
+        for which in range(count):
+            send_full(p, ph, which).wait_recv()
         sl = pl.ds(start, width)
 
-        def body(k, carry, sl=sl):
-            at = (k // 16, (k // 4) % 4, k % 4, slice(None), sl)
-            acc[at] = (acc[at].astype(f32) + sibbuf[at].astype(f32)).astype(jnp.bfloat16)
-            return carry
-        lax.fori_loop(0, 64, body, 0)
-        for which in (0, 1):
-            cp = send_half(p, 0, which)
-            cp.start()
-            sends.append(cp)
-    for ph in range(3):
-        for p in range(3):
-            start, width, half = PARTS[p]
-            axis = axis_of(p, ph)
-            for which, by, lo, w in ((0, 1, 0, half), (1, -1, half, width - half)):
-                send_half(p, ph, which).wait_recv()
-                sl = pl.ds(start + lo, w)
-
-                def body(at, dig, ph=ph, sl=sl):
-                    at = at + (slice(None), sl)
-                    hat = dig + (slice(None), sl)
-                    acc[at] = (acc[at].astype(f32) + hbufs[ph][hat].astype(f32)).astype(jnp.bfloat16)
-                over(p, ph, (me[axis] + by + 4) % 4, body)
-                cp = send_full(p, ph, which)
-                cp.start()
-                sends.append(cp)
-        for p in range(3):
-            start, width, half = PARTS[p]
-            axis = axis_of(p, ph)
-            for which in (0, 1):
-                send_full(p, ph, which).wait_recv()
-            sl = pl.ds(start, width)
-
-            def body(at, dig, ph=ph, sl=sl):
-                at = at + (slice(None), sl)
-                total = (acc[at].astype(f32) + fbufs[ph][(0,) + dig + (slice(None), sl)].astype(f32)
-                         + fbufs[ph][(1,) + dig + (slice(None), sl)].astype(f32))
-                if ph < 2:
-                    acc[at] = total.astype(jnp.bfloat16)
-                else:
-                    last[:, sl] = total
-            over(p, ph, me[axis], body)
+        def body(at, dig):
+            at = at + (slice(None), sl)
+            total = acc[at].astype(f32)
+            for which in range(count):
+                total = total + ref[(which,) + dig + (slice(None), sl)].astype(f32)
             if ph < 2:
-                for which in (0, 1):
-                    cp = send_half(p, ph + 1, which)
-                    cp.start()
-                    sends.append(cp)
+                acc[at] = total.astype(bf)
+            else:
+                last[:, sl] = total
+        over(p, ph, me[axis_of(p, ph)], body)
+        if ph < 2:
+            for which in range(3):
+                go(send_full(p, ph + 1, which))
+
+    def product(p, half, store):
+        @pl.loop(0, 4)
+        def _(y):
+            lhs = turned[pl.ds(pl.multiple_of(y * 256, 256), 256), :]
+            rhs = dpre[:, pl.ds(pl.multiple_of(half * 1024 + p * 512, 512), 512)]
+            r = jnp.dot(lhs, rhs, preferred_element_type=f32) * scale
+            store(y, r.reshape(4, 4, 16, 512))
+
+    def for_sibling(p):
+        def store(y, r):
+            gsend[y, :, :, :, lane(p, 0, 512)] = r.astype(bf)
+        product(p, 1 - core, store)
+        go(give(p))
+
+    def for_own(p):
+        give(p).wait_recv()
+
+        def store(y, r):
+            acc[y, :, :, :, lane(p, 0, 512)] = (r + sibbuf[y, :, :, :, lane(p, 0, 512)].astype(f32)).astype(bf)
+        product(p, core, store)
+        start_halves(p)
+
+    def input_product(j):
+        col = slice(j * 256, j * 256 + 256)
+        work[:, col] = lax.dot_general(dpre[...], w[col, :], (((1,), (1,)), ((), ())), preferred_element_type=f32)
+
+    def input_rows(n):
+        @pl.loop(3 * n, 3 * n + 3)
+        def _(i):
+            ats = [pl.ds(pl.multiple_of(i * 64 + 16 * u, 16), 16) for u in range(4)]
+            gain = gains[0:1, :]
+            invs = [inv_in[at, 0:1] for at in ats]
+            normals = [(xe[at, :].astype(f32) - mean_in[at, 0:1]) * inv for at, inv in zip(ats, invs)]
+            us = [work[at, :] * gain for at in ats]
+            m1 = [row_mean(u) for u in us]
+            m2 = [row_mean(u * n) for u, n in zip(us, normals)]
+            for at, inv, u, n, a, b in zip(ats, invs, us, normals, m1, m2):
+                out[at, :] = (ce[at, :].astype(f32) + inv * (u - a - n * b)).astype(bf)
+
+    go(give(2))
+    loads[0].wait()
+    turned[...] = ln[...].T
+    loads[1].wait()
+    for_sibling(0)
+    loads[2].wait()
+    give(2).wait_recv()
+
+    @pl.loop(0, 4)
+    def _(y):
+        at = (y, slice(None), slice(None), slice(None), lane(2, 0, 640))
+        acc[at] = (acc[at].astype(f32) + sibbuf[at].astype(f32)).astype(bf)
+    start_halves(2)
+    for_sibling(1)
+    for_own(0)
+    pass_on(2)
+    for_own(1)
+    for n in (3, 4):
+        loads[n].wait()
+    input_product(0)
+    pass_on(0)
+    take(2, 0)
+    input_product(1)
+    pass_on(1)
+    take(0, 0)
+    input_product(2)
+    take(2, 1)
+    take(1, 0)
+    input_product(3)
+    take(0, 1)
+    for n in (5, 6, 7, 8):
+        loads[n].wait()
+    input_rows(0)
+    take(1, 1)
+    input_rows(1)
+    take(2, 2)
+    input_rows(2)
+    take(0, 2)
+    input_rows(3)
+    stores = [cp(out, igrad_hbm, 9)]
+    take(1, 2)
     top, bottom = last[0:8, :], last[8:16, :]
     low[...] = jnp.where(core == 0, bottom, top)
     swap = pltpu.make_async_remote_copy(
@@ -354,42 +436,71 @@
     mine = jnp.where(core == 0, top, bottom)
     swap.wait()
     theirs = fin[...]
-    out_ref[:, :HALFW] = jnp.where(core == 0, mine, theirs)
-    out_ref[:, HALFW:] = jnp.where(core == 0, theirs, mine)
-    for cp in sends + gives:
-        cp.wait_send()
-
-
-def scatter(g):
-    bf = jnp.bfloat16
+    total = jnp.zeros((8, 1), f32)
+    for c in (0, 1):
+        own = jnp.where(core == c, mine, theirs)
+        o_in[:, c * 1024 : c * 1024 + 1024] = own[:, :1024]
+        o_out[:, c * 512 : c * 512 + 512] = own[:, 1024:1536]
+        rows = w_rows[:, c * 1024 : c * 1024 + 1024].astype(f32)
+        total = total + jnp.sum(rows * own[:, :1024], axis=-1, keepdims=True)
+        if c == 0:
+            rest = own[:, 1536:]
+    total = total / small[:, 31:32]
+    lanes = lax.broadcasted_iota(jnp.int32, (8, 128), 1)
+    o_small[...] = jnp.where(lanes == 31, total, rest)
+    for c in sends:
+        c.wait_send()
+    for c in stores:
+        c.wait()
+
+
+def back(early, ln, dpre, w, frames, cot, inv, mean, gains, w_rows, small):
+    bf, f32 = jnp.bfloat16, jnp.float32
+    vm = pl.BlockSpec(memory_space=pltpu.VMEM)
+    hbm = pl.BlockSpec(memory_space=pltpu.HBM)
+    V = pltpu.VMEM
     return pl.pallas_call(
-        scatter_kernel,
-        out_shape=jax.ShapeDtypeStruct((8, WIDE), jnp.float32),
-        in_specs=[pl.BlockSpec(memory_space=pltpu.HBM)],
-        out_specs=pl.BlockSpec(memory_space=pltpu.VMEM),
+        back_kernel,
+        out_shape=(
+            jax.ShapeDtypeStruct((8, 2048), f32),
+            jax.ShapeDtypeStruct((8, 1024), f32),
+            jax.ShapeDtypeStruct((8, 128), f32),
+            jax.ShapeDtypeStruct((768, 1024), bf),
+        ),
+        in_specs=[hbm] * 8 + [vm] * 3,
+        out_specs=(vm, vm, vm, hbm),
         scratch_shapes=[
-            pltpu.VMEM((4, 4, 4, 16, HALFW), bf),
-            pltpu.VMEM((4, 4, 4, 16, HALFW), bf),
-            pltpu.VMEM((4, 4, 16, HALFW), bf),
-            pltpu.VMEM((4, 16, HALFW), bf),
-            pltpu.VMEM((16, HALFW), bf),
-            pltpu.VMEM((2, 4, 4, 16, HALFW), bf),
-            pltpu.VMEM((2, 4, 16, HALFW), bf),
-            pltpu.VMEM((2, 16, HALFW), bf),
-            pltpu.VMEM((16, HALFW), jnp.float32),
-            pltpu.VMEM((8, HALFW), jnp.float32),
-            pltpu.VMEM((8, HALFW), jnp.float32),
+            V((4, 4, 4, 16, HALFW), bf),
+            V((4, 4, 4, 16, HALFW), bf),
+            V((4, 4, 4, 16, 1024), bf),
+            V((4, 4, 16, HALFW), bf),
+            V((2, 4, 4, 16, HALFW), bf),
+            V((3, 4, 16, HALFW), bf),
+            V((3, 16, HALFW), bf),
+            V((16, HALFW), f32),
+            V((8, HALFW), f32),
+            V((8, HALFW), f32),
+            V((768, 1024), bf),
+            V((1024, 768), bf),
+            V((768, 2048), bf),
+            V((1024, 2048), bf),
+            V((768, 1024), bf),
+            V((768, 1024), bf),
+            V((768, 128), f32),
+            V((768, 128), f32),
+            V((768, 1024), f32),
+            V((768, 1024), bf),
+            pltpu.SemaphoreType.DMA((10,)),
             pltpu.SemaphoreType.DMA((3,)),
             pltpu.SemaphoreType.DMA((3,)),
-            pltpu.SemaphoreType.DMA((3,)),
-            pltpu.SemaphoreType.DMA((3, 3, 4)),
-            pltpu.SemaphoreType.DMA((3, 3, 4)),
+            pltpu.SemaphoreType.DMA((3, 3, 5)),
+            pltpu.SemaphoreType.DMA((3, 3, 5)),
             pltpu.SemaphoreType.DMA((2,)),
         ],
         compiler_params=pltpu.CompilerParams(
-            collective_id=1, has_side_effects=True, vmem_limit_bytes=48 << 20),
-        name="scatter_grads",
-    )(g)
+            collective_id=1, has_side_effects=True, vmem_limit_bytes=60 << 20),
+        name="back_and_scatter",
+    )(early, ln, dpre, w, frames, cot, inv, mean, gains, w_rows, small)
 
 
 EPS = 1e-05
@@ -468,8 +579,8 @@
 
 def mid_kernel(
     ids, basis, turned, spread, back, frames, cot, hf, hc, w_hbm,
-    out_hbm, igrad_hbm, g_hbm,
-    xe, ce, w, ln, glu, sig, mixed, work, act, dm, dpre, g, spec, prod, gains, extra, inv_in, mean_in,
+    out_hbm, ln_hbm, dpre_hbm, early_hbm, inv_hbm, mean_hbm, gains,
+    xe, ce, w, ln, glu, sig, mixed, work, act, dm, dpre, g, spec, prod, extra, inv_in, mean_in,
     table, across, counts, out, sems,
 ):
     scale = 1.0 / math.sqrt(98304.0)
@@ -481,15 +592,17 @@
 
     cols = lambda lo, n: (slice(None), pl.ds(lo, n))
     loads = [
-        cp(w_hbm.at[cols(3072, 256)], w.at[cols(3072, 256)], 0),
+        cp(w_hbm.at[cols(1536, 128)], w.at[cols(3072, 128)], 0),
         cp(hf.at[pl.ds(0, 32)], xe.at[pl.ds(0, 32)], 1),
         cp(hf.at[pl.ds(32, 32)], xe.at[pl.ds(800, 32)], 2),
         cp(frames, xe.at[pl.ds(32, ROWS)], 3),
-        cp(w_hbm.at[cols(0, 2048)], w.at[cols(0, 2048)], 4),
-        cp(w_hbm.at[cols(2048, 1024)], w.at[cols(2048, 1024)], 5),
+        cp(w_hbm.at[cols(0, 1024)], w.at[cols(0, 1024)], 4),
+        cp(w_hbm.at[cols(1664, 1024)], w.at[cols(1024, 1024)], 5),
         cp(cot, ce.at[pl.ds(16, ROWS)], 6),
         cp(hc.at[pl.ds(0, 16)], ce.at[pl.ds(0, 16)], 7),
         cp(hc.at[pl.ds(16, 16)], ce.at[pl.ds(784, 16)], 8),
+        cp(w_hbm.at[cols(1024, 512)], w.at[cols(2048, 512)], 9),
+        cp(w_hbm.at[cols(2688, 512)], w.at[cols(2560, 512)], 10),
     ]
     for n, count in enumerate(colours(ids, table, across)):
         counts[n] = count
@@ -521,7 +634,13 @@
             inv_in[at, :] = jnp.broadcast_to(inv, (16, 128))
             mean_in[at, :] = jnp.broadcast_to(m, (16, 128))
 
+    stores = [
+        cp(ln.at[pl.ds(32, ROWS)], ln_hbm, 11),
+        cp(inv_in.at[pl.ds(32, ROWS)], inv_hbm, 12),
+        cp(mean_in.at[pl.ds(32, ROWS)], mean_hbm, 13),
+    ]
     loads[4].wait()
+    loads[5].wait()
 
     @pl.loop(0, 8)
     def _(i):
@@ -535,7 +654,7 @@
         glu[rows, c0] = (value * s).astype(BF)
         sig[rows, c0] = s
 
-    for n in (5, 6, 7, 8):
+    for n in (6, 7, 8, 9, 10):
         loads[n].wait()
 
     def picked(row, first, k):
@@ -656,72 +775,38 @@
         y = mm(act[16:784, :], w[:, pl.ds(pl.multiple_of(2048 + j * 256, 256), 256)])
         out[:, col] = (xe[32:800, col].astype(F32) + y).astype(BF)
         lhs = act[16:784, col].T
-        g[col, 2048:3072] = (mm(lhs, ce[16:784, :]) * scale).astype(BF)
-
-    stores = [cp(out, out_hbm, 9), cp(g.at[cols(2048, 1024)], g_hbm.at[cols(2048, 1024)], 10)]
+        r = (mm(lhs, ce[16:784, :]) * scale).astype(BF)
+        g[col, 0:512] = r[:, :512]
+        g[col, 640:1152] = r[:, 512:]
+
+    stores.append(cp(out, out_hbm, 14))
 
     @pl.loop(0, 4)
     def _(wi):
         by_class(backward, wi, counts[4 + wi], 192, 192)
 
-    @pl.loop(0, 48)
-    def _(i):
-        at = pl.ds(pl.multiple_of(i * 16, 16), 16)
-        ext = pl.ds(pl.multiple_of(i * 16 + 32, 16), 16)
-        d = mixed[at, :]
-        s = sig[ext, :]
-        ds = d * s
-        dpre[at, :1024] = ds.astype(BF)
-        dpre[at, 1024:] = (d * glu[ext, :].astype(F32) * (1.0 - s)).astype(BF)
-
-    @pl.loop(0, 4)
-    def _(j):
-        col = pl.ds(pl.multiple_of(j * 256, 256), 256)
-        lhs = ln[32:800, col].T
-        for n in range(4):
-            c = slice(n * 512, n * 512 + 512)
-            g[col, c] = (mm(lhs, dpre[:, c]) * scale).astype(BF)
-
-    stores.append(cp(g.at[cols(0, 2048)], g_hbm.at[cols(0, 2048)], 11))
     gk = jnp.dot(back[...], prod[...], precision=lax.Precision.HIGHEST, preferred_element_type=F32)
     extra[0:31, :] = gk[0:31]
-
-    @pl.loop(0, 4)
-    def _(j):
-        col = pl.ds(pl.multiple_of(j * 256, 256), 256)
-        work[0:768, col] = nt(dpre[...], w[col, 0:2048])
-
-    stores[0].wait()
-
-    @pl.loop(0, 12)
-    def _(i):
-        ats, exts, ces = strips(i, 4), strips(i, 4, 32), strips(i, 4, 16)
-        invs = [inv_in[e, 0:1] for e in exts]
-        normals = [(xe[e, :].astype(F32) - mean_in[e, 0:1]) * inv for e, inv in zip(exts, invs)]
-        us = []
-        gain = gains[0:1, :]
-        total = None
-        for at, normal in zip(ats, normals):
-            d = work[at, :]
-            dn = d * normal
-            dn = dn[:8] + dn[8:]
-            total = dn if total is None else total + dn
-            us.append(d * gain)
-        extra[48:56, :] += total
-        m1 = [row_mean(u) for u in us]
-        m2 = [row_mean(u * n) for u, n in zip(us, normals)]
-        for at, c, inv, u, n, a, b in zip(ats, ces, invs, us, normals, m1, m2):
-            out[at, :] = (ce[c, :].astype(F32) + inv * (u - a - n * b)).astype(BF)
-
-    stores.append(cp(out, igrad_hbm, 12))
     g_mid = jnp.sum(extra[40:48, :], axis=0, keepdims=True)
-    g_in = jnp.sum(extra[48:56, :], axis=0, keepdims=True)
-    extra[31:32, :] = g_in
     extra[32:33, :] = g_mid
-    g[:, 3072:3200] = (extra[...].T * scale).astype(BF)
-    g[:, 3200:3328] = jnp.zeros((D, 128), BF)
-    stores.append(cp(g.at[cols(3072, 256)], g_hbm.at[cols(3072, 256)], 13))
-    for s in stores[1:]:
+    g[:, 512:640] = (extra[...].T * scale).astype(BF)
+    g[:, 1152:1280] = jnp.zeros((D, 128), BF)
+    stores.append(cp(g, early_hbm, 15))
+
+    for q in range(4):
+        @pl.loop(q * 6, q * 6 + 6)
+        def _(i):
+            for u in range(2):
+                at = pl.ds(pl.multiple_of(i * 32 + 16 * u, 16), 16)
+                ext = pl.ds(pl.multiple_of(i * 32 + 16 * u + 32, 16), 16)
+                d = mixed[at, :]
+                s = sig[ext, :]
+                dpre[at, :1024] = (d * s).astype(BF)
+                dpre[at, 1024:] = (d * glu[ext, :].astype(F32) * (1.0 - s)).astype(BF)
+
+        part = pl.ds(q * 192, 192)
+        stores.append(cp(dpre.at[part], dpre_hbm.at[part], 16 + q))
+    for s in stores:
         s.wait()
 
 
@@ -734,18 +819,22 @@
         out_shape=(
             jax.ShapeDtypeStruct((ROWS, D), BF),
             jax.ShapeDtypeStruct((ROWS, D), BF),
-            jax.ShapeDtypeStruct((D, WIDE), BF),
+            jax.ShapeDtypeStruct((ROWS, 2 * D), BF),
+            jax.ShapeDtypeStruct((D, 1280), BF),
+            jax.ShapeDtypeStruct((ROWS, 128), F32),
+            jax.ShapeDtypeStruct((ROWS, 128), F32),
+            jax.ShapeDtypeStruct((16, D), F32),
         ),
         in_specs=[vm, vm, vm, vm, vm, hbm, hbm, hbm, hbm, hbm],
-        out_specs=(hbm, hbm, hbm),
+        out_specs=(hbm,) * 6 + (vm,),
         scratch_shapes=[
-            V((832, D), BF), V((800, D), BF), V((D, WIDE), BF),
+            V((832, D), BF), V((800, D), BF), V((D, 3200), BF),
             V((832, D), BF), V((848, D), BF), V((832, D), F32),
             V((800, D), F32), V((800, D), F32), V((800, D), BF), V((832, D), BF),
-            V((768, 2 * D), BF), V((D, WIDE), BF), V((NFFT, D), F32), V((NFFT, D), F32),
-            V((16, D), F32), V((128, D), F32), V((832, 128), F32), V((832, 128), F32),
+            V((768, 2 * D), BF), V((D, 1280), BF), V((NFFT, D), F32), V((NFFT, D), F32),
+            V((128, D), F32), V((832, 128), F32), V((832, 128), F32),
             V((12, 8, NFFT), F32), V((8, NFFT, 128), F32), pltpu.SMEM((8,), jnp.int32), V((ROWS, D), BF),
-            pltpu.SemaphoreType.DMA((14,)),
+            pltpu.SemaphoreType.DMA((20,)),
         ],
         compiler_params=pltpu.CompilerParams(vmem_limit_bytes=60 << 20),
         name="block_pass",
@@ -754,12 +843,14 @@
 
 def shards(frames, cotangent, segments, w_in, w_out, kernel, gain_in, gain_mid):
     small = jnp.concatenate(
-        [kernel.astype(F32), gain_in.astype(F32)[:, None], gain_mid.astype(F32)[:, None], jnp.zeros((8, 223), F32)], axis=1)
-    full, f_halo, c_halo, ids = gather(w_in, w_out, small, segments.reshape(6, 128), frames[0], cotangent[0])
-    block_out, input_grad, g = mid(
-        ids, tables(), frames[0], cotangent[0], f_halo, c_halo, full.reshape(D, WIDE))
-    r = scatter(g.reshape(4, 4, 4, 16, WIDE))
-    return (block_out[None], input_grad[None], r[:, :2048], r[:, 2048:3072], r[:, 3072:3103], r[:, 3103], r[:, 3104])
+        [kernel.astype(F32), gain_in.astype(F32)[:, None], gain_mid.astype(F32)[:, None], jnp.zeros((8, 95), F32)], axis=1)
+    x, cot = frames[0], cotangent[0]
+    full, f_halo, c_halo, ids = gather(w_in, w_out, small, segments.reshape(6, 128), x, cot)
+    full = full.reshape(D, WIDE)
+    block_out, ln, dpre, early, inv, mean, gains = mid(ids, tables(), x, cot, f_halo, c_halo, full)
+    g_in, g_out, g_small, input_grad = back(
+        early.reshape(4, 4, 4, 16, 1280), ln, dpre, full, x, cot, inv, mean, gains, w_in, small)
+    return (block_out[None], input_grad[None], g_in, g_out, g_small[:, :31], g_small[:, 31], g_small[:, 32])
 
 
 def solution(mesh):

time: 147 us -> 139 us (0.946)
  Pallas kernels: 134 us -> 127 us
  local copies, waits for them, and re-layouts: 8.96 us -> 6.26 us
    pallas_call x1, Pallas kernels: 52.1 us -> 42 us  [mid(): pl.pallas_call(mid_kernel, out_shape=(jax.ShapeDtypeStruct((ROWS, D), BF)...]
    pallas_call x1, Pallas kernels: 41.6 us -> 46.6 us  [back(): pl.pallas_call(back_kernel, out_shape=(jax.ShapeDtypeStruct((8, 2048), f3...]
    unnamed x14 -> x10, local copies, waits for them, and re-layouts: 6.15 us -> 4.55 us
where the time goes in v4:
time: 139 us; the launch traced here: 138 us
  Pallas kernels  127 us (91%)
  local copies, waits for them, and re-layouts  6.26 us (5%)
  other arithmetic  3.96 us (3%)
    pallas_call x1, Pallas kernels, back(): pl.pallas_call(back_kernel, out_shape=(jax.ShapeDtypeStruct((8, 2048), f3...  46.6 us
    pallas_call x1, Pallas kernels, mid(): pl.pallas_call(mid_kernel, out_shape=(jax.ShapeDtypeStruct((ROWS, D), BF)...  42 us
    pallas_call x1, Pallas kernels, gather(): pl.pallas_call(gather_kernel, out_shape=(jax.ShapeDtypeStruct((4, 4, 4, 1...  38.9 us
    unnamed x10, local copies, waits for them, and re-layouts  4.55 us

profile of v4, /device:TPU:1, one launch (start us, length us, event | category | flops | bytes accessed | tf_op | source)
XLA Modules:
  0.0 138.3 jit_solution(8103677460143004771)
XLA Ops:
  0.6 0.7 bitcast_convert_fusion.1
  1.3 0.7 bitcast_convert_fusion
  1.9 0.1 pad.3.clone
  2.0 0.1 copy.22
  2.1 0.1 copy.21
  2.2 1.3 reduce
  3.5 0.7 convert_element_type.2
  4.2 0.7 maximum_maximum_fusion.small_ref.small
  4.8 38.9 %gather_weights.1 = (bf16[4,4,4,16,3328]{4,3,2,1,0:T(8,128)(2,1)}, bf16[64,1024]{1,0:T(8,128)(2,1)}, bf16[32,1024]{1,0:T(8,128)(2,1)}, f32[8,128]{1,0:T(8,128)}) custom-call(bf16[8,2048]{1,0:T(8,128)(2,1)} %w_rows.1, bf16[8,1024]{1,0:T(8,128)(2,1)} %w_out_ref.1, f32[8,128]{1,0:T(8,128)} %maximum_maximum_fusion.small_ref.small, s32[6,128]{1,0:T(8,128)} %bitcast.25, ...), custom_call_target="tpu_custom_call" | custom-call | tf_op jit(solution)/shard_map/gather_weights/pallas_call | solution.py:184
  43.7 42.0 %block_pass.1 = (bf16[768,1024]{1,0:T(8,128)(2,1)}, bf16[768,1024]{1,0:T(8,128)(2,1)}, bf16[768,2048]{1,0:T(8,128)(2,1)}, bf16[1024,1280]{1,0:T(8,128)(2,1)}, f3...) custom-call(f32[8,128]{1,0:T(8,128)} %get-tuple-element.22.ids, f32[256,256]{1,0:T(8,128)} %constant.10.clone.basis, ...), custom_call_target="tpu_custom_call" | custom-call | tf_op jit(solution)/shard_map/block_pass/pallas_call | solution.py:817
  85.7 46.6 %back_and_scatter.1 = (f32[8,2048]{1,0:T(8,128)}, f32[8,1024]{1,0:T(8,128)}, f32[8,128]{1,0:T(8,128)}, bf16[768,1024]{1,0:T(8,128)(2,1)}) custom-call(bf16[4,4,4,16,1280]{4,3,2,1,0:T(8,128)(2,1)} %bitcast.22, bf16[768,1024]{1,0:T(8,128)(2,1)} %get-tuple-element.28.ln_hbm, bf16[768,2048]{1,0:T(8,128)(2,1)} %get-tuple-element.29.dpre_hbm, ...), custom_call_target="tpu_custom_call" | custom-call | tf_op jit(solution)/shard_map/back_and_scatter/pallas_call | solution.py:462
  132.3 1.5 %slice_reduce_fusion = (f32[8]{0:T(128)}, f32[8]{0:T(128)}) fusion(f32[8,128]{1,0:T(8,128)} %get-tuple-element.36), kind=kLoop, calls=%fused_computation.1 | loop fusion | bytes 128 | tf_op jit(solution)/shard_map/slice | solution.py:853
  133.8 0.0 copy-start
  133.8 0.0 copy-start.2
  133.8 0.0 copy-start.1
  133.8 2.7 %copy.27 = bf16[1,768,1024]{2,1,0:T(8,128)(2,1)} copy(bf16[1,768,1024]{2,1,0:T(8,128)(2,1)} %bitcast.23) | data formatting | bytes 3145728
  136.5 0.0 copy-done
  136.5 0.6 copy.28
  137.1 0.0 copy-done.2
  137.1 0.6 copy.29
  137.7 0.0 copy-done.1
  137.8 0.6 copy.30
  (1 shorter events, 0.0 us)
Async XLA Ops:
  133.8 2.7 %copy-start = (f32[8,2048]{1,0:T(8,128)S(1)}, f32[8,2048]{1,0:T(8,128)}, u32[]{:S(2)}) copy-start(f32[8,2048]{1,0:T(8,128)} %get-tuple-element.48) | copy-start | bytes 196612
  133.8 3.3 %copy-start.2 = (f32[8,1024]{1,0:T(8,128)S(1)}, f32[8,1024]{1,0:T(8,128)}, u32[]{:S(2)}) copy-start(f32[8,1024]{1,0:T(8,128)} %get-tuple-element.49) | copy-start | bytes 98308
  133.8 4.0 %copy-start.1 = (f32[8,128]{1,0:T(8,128)S(1)}, f32[8,128]{1,0:T(8,128)}, u32[]{:S(2)}) copy-start(f32[8,128]{1,0:T(8,128)} %get-tuple-element.36) | copy-start | bytes 12292

commit v5 on v4

--- a/solution.py
+++ b/solution.py
@@ -11,8 +11,9 @@
 MESH = pl.DeviceIdType.MESH
 HALFW = 1664
 WIDE = 2 * HALFW
-PARTS = ((0, 512, 256), (512, 512, 256), (1024, 640, 384))
-ORDERS = (("z", "x", "y"), ("x", "y", "z"), ("y", "z", "x"))
+PARTS = ((0, 384), (384, 384), (768, 256), (1024, 128), (1152, 256), (1408, 256))
+FIRST, SECOND = (0, 1, 2), (3, 4, 5)
+ORDERS = (("z", "x", "y"), ("x", "y", "z"), ("y", "z", "x")) * 2
 HALO = 32
 
 
@@ -32,10 +33,17 @@
 
 
 def greet(targets):
-    barrier = pltpu.get_barrier_semaphore()
     for t in targets:
-        pl.semaphore_signal(barrier, inc=1, device_id=t, device_id_type=MESH)
-    pl.semaphore_wait(barrier, len(targets))
+        pl.semaphore_signal(pltpu.get_barrier_semaphore(), inc=1, device_id=t, device_id_type=MESH)
+
+
+def greeted(targets):
+    pl.semaphore_wait(pltpu.get_barrier_semaphore(), len(targets))
+
+
+def half_of(index, which):
+    at = [isinstance(i, slice) for i in index].index(True)
+    return index[:at] + (pl.ds(2 * which, 2),) + index[at + 1 :]
 
 
 def block_index(coords, full, axis, value):
@@ -51,23 +59,30 @@
 
 
 def gather_kernel(
-    w_in_ref, w_out_ref, small_ref, seg_ref, frames_ref, cot_ref,
+    w_in_ref, w_out_ref, kern_ref, gain_ref, seg_ref, frames_ref, cot_ref,
     out_ref, hf_ref, hc_ref, ids_ref,
     buf, shard, sib, segs, sib_sem, halo_send, halo_recv, a_send, a_recv, s_send, s_recv, out_sem,
 ):
     me, core = place()
+    f32, bf = jnp.float32, jnp.bfloat16
     sibling = dev(me, 1 - core)
     seq = lax.axis_index("seq")
     right = (lax.axis_index("dp"), (seq + 1) % 8)
     left = (lax.axis_index("dp"), (seq + 7) % 8)
     cross = dev(moved(me, "z", 2 * core - 1), 1 - core)
-    targets = [dev(moved(me, a, b), core) for a in "yxz" for b in (1, -1, 2)]
+    targets = [dev(moved(me, a, b), core) for a in "yxz" for b in (1, -1, 2)] + [sibling, cross]
+    greet(targets)
     for c in (0, 1):
         at = c * HALFW
-        shard[:, at : at + 1024] = w_in_ref[:, c * 1024 : c * 1024 + 1024].astype(jnp.float32)
-        shard[:, at + 1024 : at + 1536] = w_out_ref[:, c * 512 : c * 512 + 512].astype(jnp.float32)
-        shard[:, at + 1536 : at + HALFW] = small_ref[...] if c == 0 else jnp.zeros((8, 128), jnp.float32)
-    greet(targets + [sibling, cross])
+        shard[:, at : at + 1024] = w_in_ref[:, c * 1024 : c * 1024 + 1024].astype(f32)
+        shard[:, at + 1024 : at + 1536] = w_out_ref[:, c * 512 : c * 512 + 512].astype(f32)
+        shard[:, at + 1536 : at + HALFW] = jnp.zeros((8, 128), f32)
+    shard[:, 1536 : 1536 + 31] = kern_ref[...].astype(f32)
+    eye = lax.broadcasted_iota(jnp.int32, (8, 8), 0) == lax.broadcasted_iota(jnp.int32, (8, 8), 1)
+    for n in (0, 1):
+        row = jnp.broadcast_to(gain_ref[n : n + 1, :], (8, 8))
+        shard[:, 1567 + n : 1568 + n] = jnp.sum(jnp.where(eye, row, 0.0), axis=1, keepdims=True)
+    greeted(targets)
 
     first = pltpu.make_async_remote_copy(
         src_ref=shard, dst_ref=sib, send_sem=sib_sem.at[0], recv_sem=sib_sem.at[1],
@@ -90,23 +105,20 @@
     low = jnp.where(core == 0, mine[:, :HALFW], other[:, HALFW:])
     high = jnp.where(core == 0, other[:, :HALFW], mine[:, HALFW:])
     buf[me["y"], me["x"], me["z"], :, pl.ds(pl.multiple_of(core * HALFW, 128), HALFW)] = jnp.concatenate(
-        [low, high], axis=0).astype(jnp.bfloat16)
-    for cp in halos:
-        cp.start()
-
-    def cols(p, lo, width, c=core):
-        return pl.ds(pl.multiple_of(c * HALFW + PARTS[p][0] + lo, 128), width)
-
-    def send(p, ph, which, idx, lo, width, by):
+        [low, high], axis=0).astype(bf)
+
+    def cols(p, c=core):
+        return pl.ds(pl.multiple_of(c * HALFW + PARTS[p][0], 128), PARTS[p][1])
+
+    def send(p, ph, which, idx, by):
         axis = ORDERS[p][ph]
-        ref = buf.at[idx + (slice(None), cols(p, lo, width))]
+        ref = buf.at[idx + (slice(None), cols(p))]
         return pltpu.make_async_remote_copy(
             src_ref=ref, dst_ref=ref, send_sem=a_send.at[p, ph, which], recv_sem=a_recv.at[p, ph, which],
             device_id=dev(moved(me, axis, by), core), device_id_type=MESH)
 
     def to_sibling(p, which, idx, c=core):
-        start, width, _ = PARTS[p]
-        ref = buf.at[idx + (slice(None), cols(p, 0, width, c))]
+        ref = buf.at[idx + (slice(None), cols(p, c))]
         return pltpu.make_async_remote_copy(
             src_ref=ref, dst_ref=ref, send_sem=s_send.at[p, which], recv_sem=s_recv.at[p, which],
             device_id=sibling, device_id_type=MESH)
@@ -115,69 +127,83 @@
         axis = ORDERS[p][ph]
         return block_index(me, ORDERS[p][:ph], axis, (me[axis] + by + 4) % 4)
 
-    sends = []
+    sends, outs = [], []
 
     def go(cp):
         cp.start()
         sends.append(cp)
 
-    for ph in range(2):
-        for p in range(3):
-            width = PARTS[p][1]
-            if ph > 0:
-                for which, by in ((0, -1), (1, 1), (2, 2)):
-                    send(p, 0, which, block(p, 0, by), 0, width, by).wait_recv()
-            for which, by in ((0, 1), (1, -1), (2, 2)):
-                go(send(p, ph, which, block(p, ph, 0), 0, width, by))
-    for p in range(3):
-        width = PARTS[p][1]
-        for which, by in ((0, -1), (1, 1), (2, 2)):
-            send(p, 1, which, block(p, 1, by), 0, width, by).wait_recv()
-        own = block(p, 2, 0)
-        for which, by in ((0, 1), (1, -1)):
-            go(send(p, 2, which, own, 0, width, by))
-        go(to_sibling(p, 0, own))
-    for p in range(3):
-        _, width, half = PARTS[p]
-        for which, by, lo, w in ((0, -1, 0, half), (1, 1, half, width - half)):
+    def start(p, ph):
+        if ph > 0:
+            for which, by in ((0, -1), (1, 1), (2, 2)):
+                send(p, ph - 1, which, block(p, ph - 1, by), by).wait_recv()
+        own = block(p, ph, 0)
+        for which, by in ((0, 1), (1, -1), (2, 2))[: 3 if ph < 2 else 2]:
+            go(send(p, ph, which, own, by))
+        if ph == 2:
+            go(to_sibling(p, 0, own))
+
+    def pass_on(p):
+        for which, by in ((0, -1), (1, 1)):
             idx = block(p, 2, by)
-            send(p, 2, which, idx, 0, width, -by).wait_recv()
-            go(send(p, 2, which + 2, idx, lo, w, -by))
+            send(p, 2, which, idx, -by).wait_recv()
+            go(send(p, 2, which + 2, half_of(idx, which), -by))
             go(to_sibling(p, 1 + which, idx))
-    outs = []
 
     def flush(p, c, n):
-        at = (slice(None),) * 4 + (cols(p, 0, PARTS[p][1], c),)
+        at = (slice(None),) * 4 + (cols(p, c),)
         cp = pltpu.make_async_copy(buf.at[at], out_ref.at[at], out_sem.at[p, n])
         cp.start()
         outs.append(cp)
 
-    for p in range(3):
-        _, width, half = PARTS[p]
-        opp = block(p, 2, 2)
-        send(p, 2, 2, opp, 0, half, 1).wait_recv()
-        send(p, 2, 3, opp, half, width - half, -1).wait_recv()
-        cp = to_sibling(p, 3, opp)
-        cp.start()
-        sends.append(cp)
+    def finish(p):
+        idx = block(p, 2, 2)
+        for which in (0, 1):
+            send(p, 2, 2 + which, half_of(idx, which), 1).wait_recv()
+        go(to_sibling(p, 3, idx))
         flush(p, core, 0)
+
+    def from_sibling(p):
+        for which, by in ((0, 0), (1, -1), (2, 1), (3, 2)):
+            to_sibling(p, which, block(p, 2, by), 1 - core).wait_recv()
+        flush(p, 1 - core, 1)
+
+    for ph in (0, 1):
+        for p in FIRST + SECOND:
+            start(p, ph)
+            if ph == 0 and p == 2:
+                for cp in halos:
+                    cp.start()
+    for p in FIRST:
+        start(p, 2)
+    for p in FIRST:
+        pass_on(p)
+    for p in SECOND:
+        start(p, 2)
+    for p in FIRST:
+        finish(p)
     for cp in halos:
         cp.wait()
     own = seg_ref[...]
-    before = jnp.where(seq == 0, jnp.broadcast_to(own[0:1, 0:1] - 1, (1, 128)), segs[0, 5:6, :])
-    after = jnp.where(seq == 7, jnp.broadcast_to(own[5:6, 127:128] + 1, (1, 128)), segs[1, 0:1, :])
-    ids_ref[...] = jnp.concatenate([before, own, after], axis=0).astype(jnp.float32)
-    for p in range(3):
-        for which, by in ((0, 0), (1, -1), (2, 1), (3, 2)):
-            to_sibling(p, which, block(p, 2, by), 1 - core).wait_recv()
-        flush(p, 1 - core, 1)
+    before = jnp.where(seq == 0, jnp.broadcast_to(own[:, 0:1] - 1, (1, 128)), segs[0, :, 640:768])
+    after = jnp.where(seq == 7, jnp.broadcast_to(own[:, 767:768] + 1, (1, 128)), segs[1, :, 0:128])
+    ids_ref[...] = jnp.concatenate(
+        [before] + [own[:, n * 128 : n * 128 + 128] for n in range(6)] + [after], axis=0).astype(f32)
+    for p in SECOND:
+        pass_on(p)
+    for p in FIRST:
+        from_sibling(p)
+    for p in SECOND:
+        finish(p)
+    for p in SECOND:
+        from_sibling(p)
     for cp in sends:
         cp.wait_send()
     for cp in outs:
         cp.wait()
 
 
-def gather(w_in, w_out, small, seg, frames, cot):
+def gather(w_in, w_out, kern, gain, seg, frames, cot):
     bf = jnp.bfloat16
     vm = pl.BlockSpec(memory_space=pltpu.VMEM)
     hbm = pl.BlockSpec(memory_space=pltpu.HBM)
@@ -189,33 +215,33 @@
             jax.ShapeDtypeStruct((32, 1024), bf),
             jax.ShapeDtypeStruct((8, 128), jnp.float32),
         ),
-        in_specs=[vm, vm, vm, vm, hbm, hbm],
+        in_specs=[vm, vm, vm, vm, vm, hbm, hbm],
         out_specs=(hbm, vm, vm, vm),
         scratch_shapes=[
             pltpu.VMEM((4, 4, 4, 16, WIDE), bf),
             pltpu.VMEM((8, WIDE), jnp.float32),
             pltpu.VMEM((8, WIDE), jnp.float32),
-            pltpu.VMEM((2, 6, 128), jnp.int32),
+            pltpu.VMEM((2, 1, 768), jnp.int32),
             pltpu.SemaphoreType.DMA((2,)),
             pltpu.SemaphoreType.DMA((3, 2)),
             pltpu.SemaphoreType.DMA((3, 2)),
-            pltpu.SemaphoreType.DMA((3, 3, 4)),
-            pltpu.SemaphoreType.DMA((3, 3, 4)),
-            pltpu.SemaphoreType.DMA((3, 4)),
-            pltpu.SemaphoreType.DMA((3, 4)),
-            pltpu.SemaphoreType.DMA((3, 2)),
+            pltpu.SemaphoreType.DMA((6, 3, 4)),
+            pltpu.SemaphoreType.DMA((6, 3, 4)),
+            pltpu.SemaphoreType.DMA((6, 4)),
+            pltpu.SemaphoreType.DMA((6, 4)),
+            pltpu.SemaphoreType.DMA((6, 2)),
         ],
         compiler_params=pltpu.CompilerParams(
             collective_id=0, has_side_effects=True, vmem_limit_bytes=60 << 20),
         name="gather_weights",
-    )(w_in, w_out, small, seg, frames, cot)
+    )(w_in, w_out, kern, gain, seg, frames, cot)
 
 
 def back_kernel(
-    early, ln_hbm, dpre_hbm, w_hbm, frames, cot, inv_hbm, mean_hbm, gains, w_rows, small,
-    o_in, o_out, o_small, igrad_hbm,
+    early, ln_hbm, dpre_hbm, w_hbm, frames, cot, inv_hbm, mean_hbm, gains, w_rows, gain,
+    o_in, o_out, o_kern, o_vec, out,
     acc, sibbuf, gsend, h0, f0, f1, f2, last, low, fin,
-    ln, turned, dpre, w, xe, ce, inv_in, mean_in, work, out,
+    ln, turned, dpre, w, xe, ce, inv_in, mean_in, work,
     load_sem, d_send, d_recv, a_send, a_recv, e_sem,
 ):
     scale = 1.0 / math.sqrt(98304.0)
@@ -232,13 +258,15 @@
     def early_cols(c):
         return full4 + (pl.ds(pl.multiple_of(c * 640, 128), 640),)
 
-    def lane(p, lo, w):
-        return pl.ds(PARTS[p][0] + lo, w)
+    def lanes(p):
+        return pl.ds(*PARTS[p])
+
+    later = pl.ds(1024, 640)
 
     loads = [
         cp(ln_hbm, ln, 0),
         cp(dpre_hbm, dpre, 1),
-        cp(early.at[early_cols(core)], acc.at[full4 + (lane(2, 0, 640),)], 2),
+        cp(early.at[early_cols(core)], acc.at[full4 + (later,)], 2),
         cp(w_hbm.at[:, pl.ds(0, 1024)], w.at[:, pl.ds(0, 1024)], 3),
         cp(w_hbm.at[:, pl.ds(HALFW, 1024)], w.at[:, pl.ds(1024, 1024)], 4),
         cp(frames, xe, 5),
@@ -246,13 +274,13 @@
         cp(inv_hbm, inv_in, 7),
         cp(mean_hbm, mean_in, 8),
     ]
-    targets = [dev(moved(me, a, b), core) for a in "yxz" for b in (1, -1, 2)]
-    greet(targets + [sibling])
+    targets = [dev(moved(me, a, b), core) for a in "yxz" for b in (1, -1, 2)] + [sibling]
+    greet(targets)
 
     def give(p):
-        src = early.at[early_cols(1 - core)] if p == 2 else gsend.at[full4 + (lane(p, 0, 512),)]
+        src = early.at[early_cols(1 - core)] if p == 3 else gsend.at[full4 + (lanes(p),)]
         return pltpu.make_async_remote_copy(
-            src_ref=src, dst_ref=sibbuf.at[full4 + (lane(p, 0, PARTS[p][1]),)],
+            src_ref=src, dst_ref=sibbuf.at[full4 + (later if p == 3 else lanes(p),)],
             send_sem=d_send.at[p], recv_sem=d_recv.at[p], device_id=sibling, device_id_type=MESH)
 
     sends = []
@@ -268,28 +296,22 @@
         axis = axis_of(p, ph)
         return block_index(me, ORDERS[p][: 2 - ph], axis, (me[axis] + by + 4) % 4)
 
-    def landing(p, ph, which, lo, w):
-        ref = (f0, f1, f2)[ph]
-        return ref.at[(which,) + (slice(None),) * (2 - ph) + (slice(None), lane(p, lo, w))]
-
     def send_half(p, which):
-        _, width, half = PARTS[p]
-        lo, w, by = ((0, half, 1), (half, width - half, -1))[which]
         return pltpu.make_async_remote_copy(
-            src_ref=acc.at[block(p, 0, 2) + (slice(None), lane(p, lo, w))],
-            dst_ref=h0.at[(slice(None),) * 3 + (lane(p, lo, w),)],
+            src_ref=acc.at[half_of(block(p, 0, 2), which) + (slice(None), lanes(p))],
+            dst_ref=h0.at[pl.ds(2 * which, 2), :, :, lanes(p)],
             send_sem=a_send.at[p, 0, which], recv_sem=a_recv.at[p, 0, which],
-            device_id=dev(moved(me, axis_of(p, 0), by), core), device_id_type=MESH)
+            device_id=dev(moved(me, axis_of(p, 0), (1, -1)[which]), core), device_id_type=MESH)
 
     def send_full(p, ph, which):
-        width = PARTS[p][1]
         by = (1, -1, 2)[which]
+        dst = (f0, f1, f2)[ph].at[(which,) + (slice(None),) * (3 - ph) + (lanes(p),)]
         return pltpu.make_async_remote_copy(
-            src_ref=acc.at[block(p, ph, by) + (slice(None), lane(p, 0, width))], dst_ref=landing(p, ph, which, 0, width),
+            src_ref=acc.at[block(p, ph, by) + (slice(None), lanes(p))], dst_ref=dst,
             send_sem=a_send.at[p, ph, 2 + which], recv_sem=a_recv.at[p, ph, 2 + which],
             device_id=dev(moved(me, axis_of(p, ph), by), core), device_id_type=MESH)
 
-    def over(p, ph, value, body):
+    def over(p, ph, value, body, span=(0, 4)):
         axis, full = axis_of(p, ph), ORDERS[p][: 2 - ph]
         names = [a for a in "yxz" if a in full]
 
@@ -303,7 +325,7 @@
             return tuple(by_name[a] if a in by_name else me[a] for a in "yxz")
 
         if len(names) == 2:
-            @pl.loop(0, 4)
+            @pl.loop(*span)
             def _(k):
                 body(at(k), (k, slice(None)))
         else:
@@ -314,25 +336,22 @@
             go(send_half(p, which))
 
     def pass_on(p):
-        start, width, half = PARTS[p]
         axis = axis_of(p, 0)
-        for which, by, lo, w in ((0, 1, 0, half), (1, -1, half, width - half)):
+        for which, by in ((0, 1), (1, -1)):
             send_half(p, which).wait_recv()
-            sl = pl.ds(start + lo, w)
-
-            def body(at, dig, sl=sl):
-                at = at + (slice(None), sl)
-                acc[at] = (acc[at].astype(f32) + h0[dig + (slice(None), sl)].astype(f32)).astype(bf)
-            over(p, 0, (me[axis] + by + 4) % 4, body)
+
+            def body(at, dig):
+                at = at + (slice(None), lanes(p))
+                acc[at] = (acc[at].astype(f32) + h0[dig + (slice(None), lanes(p))].astype(f32)).astype(bf)
+            over(p, 0, (me[axis] + by + 4) % 4, body, (2 * which, 2 * which + 2))
             go(send_full(p, 0, which))
 
     def take(p, ph):
-        start, width, _ = PARTS[p]
         count = 2 if ph == 0 else 3
         ref = (f0, f1, f2)[ph]
         for which in range(count):
             send_full(p, ph, which).wait_recv()
-        sl = pl.ds(start, width)
+        sl = lanes(p)
 
         def body(at, dig):
             at = at + (slice(None), sl)
@@ -349,24 +368,25 @@
                 go(send_full(p, ph + 1, which))
 
     def product(p, half, store):
+        at, width = PARTS[p]
+
         @pl.loop(0, 4)
         def _(y):
             lhs = turned[pl.ds(pl.multiple_of(y * 256, 256), 256), :]
-            rhs = dpre[:, pl.ds(pl.multiple_of(half * 1024 + p * 512, 512), 512)]
+            rhs = dpre[:, pl.ds(pl.multiple_of(half * 1024 + at, 128), width)]
             r = jnp.dot(lhs, rhs, preferred_element_type=f32) * scale
-            store(y, r.reshape(4, 4, 16, 512))
+            store(y, r.reshape(4, 4, 16, width))
 
     def for_sibling(p):
         def store(y, r):
-            gsend[y, :, :, :, lane(p, 0, 512)] = r.astype(bf)
+            gsend[y, :, :, :, lanes(p)] = r.astype(bf)
         product(p, 1 - core, store)
-        go(give(p))
 
     def for_own(p):
         give(p).wait_recv()
 
         def store(y, r):
-            acc[y, :, :, :, lane(p, 0, 512)] = (r + sibbuf[y, :, :, :, lane(p, 0, 512)].astype(f32)).astype(bf)
+            acc[y, :, :, :, lanes(p)] = (r + sibbuf[y, :, :, :, lanes(p)].astype(f32)).astype(bf)
         product(p, core, store)
         start_halves(p)
 
@@ -387,52 +407,66 @@
             for at, inv, u, n, a, b in zip(ats, invs, us, normals, m1, m2):
                 out[at, :] = (ce[at, :].astype(f32) + inv * (u - a - n * b)).astype(bf)
 
-    go(give(2))
     loads[0].wait()
     turned[...] = ln[...].T
     loads[1].wait()
     for_sibling(0)
+    greeted(targets)
+    go(give(3))
+    go(give(0))
+    for_sibling(1)
+    go(give(1))
     loads[2].wait()
-    give(2).wait_recv()
+    give(3).wait_recv()
 
     @pl.loop(0, 4)
     def _(y):
-        at = (y, slice(None), slice(None), slice(None), lane(2, 0, 640))
+        at = (y, slice(None), slice(None), slice(None), later)
         acc[at] = (acc[at].astype(f32) + sibbuf[at].astype(f32)).astype(bf)
-    start_halves(2)
-    for_sibling(1)
+    for p in SECOND:
+        start_halves(p)
+    for_sibling(2)
+    go(give(2))
     for_own(0)
-    pass_on(2)
+    for p in SECOND:
+        pass_on(p)
     for_own(1)
+    for_own(2)
+    pass_on(0)
     for n in (3, 4):
         loads[n].wait()
     input_product(0)
-    pass_on(0)
-    take(2, 0)
+    pass_on(1)
+    pass_on(2)
+    for p in SECOND:
+        take(p, 0)
     input_product(1)
-    pass_on(1)
     take(0, 0)
     input_product(2)
-    take(2, 1)
+    for p in SECOND:
+        take(p, 1)
     take(1, 0)
+    take(2, 0)
     input_product(3)
-    take(0, 1)
     for n in (5, 6, 7, 8):
         loads[n].wait()
+    take(0, 1)
+    for p in SECOND:
+        take(p, 2)
     input_rows(0)
     take(1, 1)
+    take(2, 1)
     input_rows(1)
+    take(0, 2)
+    input_rows(2)
+    take(1, 2)
     take(2, 2)
-    input_rows(2)
-    take(0, 2)
-    input_rows(3)
-    stores = [cp(out, igrad_hbm, 9)]
-    take(1, 2)
     top, bottom = last[0:8, :], last[8:16, :]
     low[...] = jnp.where(core == 0, bottom, top)
     swap = pltpu.make_async_remote_copy(
         src_ref=low, dst_ref=fin, send_sem=e_sem.at[0], recv_sem=e_sem.at[1], device_id=sibling, device_id_type=MESH)
     swap.start()
+    input_rows(3)
     mine = jnp.where(core == 0, top, bottom)
     swap.wait()
     theirs = fin[...]
@@ -445,16 +479,18 @@
         total = total + jnp.sum(rows * own[:, :1024], axis=-1, keepdims=True)
         if c == 0:
             rest = own[:, 1536:]
-    total = total / small[:, 31:32]
-    lanes = lax.broadcasted_iota(jnp.int32, (8, 128), 1)
-    o_small[...] = jnp.where(lanes == 31, total, rest)
+    eye = lax.broadcasted_iota(jnp.int32, (8, 8), 0) == lax.broadcasted_iota(jnp.int32, (8, 8), 1)
+    column = jnp.sum(jnp.where(eye, jnp.broadcast_to(gain[0:1, :], (8, 8)), 0.0), axis=1, keepdims=True)
+    o_kern[...] = rest[:, 0:31]
+    pair = []
+    for v in (total / column, rest[:, 32:33]):
+        pair.append(jnp.sum(jnp.where(eye, jnp.broadcast_to(v, (8, 8)), 0.0), axis=0, keepdims=True))
+    o_vec[...] = jnp.concatenate(pair, axis=0)
     for c in sends:
         c.wait_send()
-    for c in stores:
-        c.wait()
-
-
-def back(early, ln, dpre, w, frames, cot, inv, mean, gains, w_rows, small):
+
+
+def back(early, ln, dpre, w, frames, cot, inv, mean, gains, w_rows, gain):
     bf, f32 = jnp.bfloat16, jnp.float32
     vm = pl.BlockSpec(memory_space=pltpu.VMEM)
     hbm = pl.BlockSpec(memory_space=pltpu.HBM)
@@ -464,11 +500,12 @@
         out_shape=(
             jax.ShapeDtypeStruct((8, 2048), f32),
             jax.ShapeDtypeStruct((8, 1024), f32),
-            jax.ShapeDtypeStruct((8, 128), f32),
+            jax.ShapeDtypeStruct((8, 31), f32),
+            jax.ShapeDtypeStruct((2, 8), f32),
             jax.ShapeDtypeStruct((768, 1024), bf),
         ),
         in_specs=[hbm] * 8 + [vm] * 3,
-        out_specs=(vm, vm, vm, hbm),
+        out_specs=(vm, vm, vm, vm, vm),
         scratch_shapes=[
             V((4, 4, 4, 16, HALFW), bf),
             V((4, 4, 4, 16, HALFW), bf),
@@ -489,18 +526,17 @@
             V((768, 128), f32),
             V((768, 128), f32),
             V((768, 1024), f32),
-            V((768, 1024), bf),
             pltpu.SemaphoreType.DMA((10,)),
-            pltpu.SemaphoreType.DMA((3,)),
-            pltpu.SemaphoreType.DMA((3,)),
-            pltpu.SemaphoreType.DMA((3, 3, 5)),
-            pltpu.SemaphoreType.DMA((3, 3, 5)),
+            pltpu.SemaphoreType.DMA((4,)),
+            pltpu.SemaphoreType.DMA((4,)),
+            pltpu.SemaphoreType.DMA((6, 3, 5)),
+            pltpu.SemaphoreType.DMA((6, 3, 5)),
             pltpu.SemaphoreType.DMA((2,)),
         ],
         compiler_params=pltpu.CompilerParams(
             collective_id=1, has_side_effects=True, vmem_limit_bytes=60 << 20),
         name="back_and_scatter",
-    )(early, ln, dpre, w, frames, cot, inv, mean, gains, w_rows, small)
+    )(early, ln, dpre, w, frames, cot, inv, mean, gains, w_rows, gain)
 
 
 EPS = 1e-05
@@ -842,15 +878,14 @@
 
 
 def shards(frames, cotangent, segments, w_in, w_out, kernel, gain_in, gain_mid):
-    small = jnp.concatenate(
-        [kernel.astype(F32), gain_in.astype(F32)[:, None], gain_mid.astype(F32)[:, None], jnp.zeros((8, 95), F32)], axis=1)
+    gain = jnp.stack([gain_in, gain_mid]).astype(F32)
     x, cot = frames[0], cotangent[0]
-    full, f_halo, c_halo, ids = gather(w_in, w_out, small, segments.reshape(6, 128), x, cot)
+    full, f_halo, c_halo, ids = gather(w_in, w_out, kernel, gain, segments, x, cot)
     full = full.reshape(D, WIDE)
     block_out, ln, dpre, early, inv, mean, gains = mid(ids, tables(), x, cot, f_halo, c_halo, full)
-    g_in, g_out, g_small, input_grad = back(
-        early.reshape(4, 4, 4, 16, 1280), ln, dpre, full, x, cot, inv, mean, gains, w_in, small)
-    return (block_out[None], input_grad[None], g_in, g_out, g_small[:, :31], g_small[:, 31], g_small[:, 32])
+    g_in, g_out, g_kern, g_vec, input_grad = back(
+        early.reshape(4, 4, 4, 16, 1280), ln, dpre, full, x, cot, inv, mean, gains, w_in, gain)
+    return (block_out[None], input_grad[None], g_in, g_out, g_kern, g_vec[0], g_vec[1])
 
 
 def solution(mesh):

time: 139 us -> 131 us (0.942)
  Pallas kernels: 127 us -> 123 us
  other arithmetic: 3.96 us -> 1.24 us
    pallas_call x1, Pallas kernels: 46.6 us -> 40.8 us  [back(): pl.pallas_call(back_kernel, out_shape=(jax.ShapeDtypeStruct((8, 2048), f3...]
    slice x1 -> x0, local copies, waits for them, and re-layouts: 1.47 us -> none  [shards(): g_small[:, 32]]
where the time goes in v5:
time: 131 us
  Pallas kernels  123 us (94%)
  local copies, waits for them, and re-layouts  5.82 us (4%)
    pallas_call x1, Pallas kernels, mid(): pl.pallas_call(mid_kernel, out_shape=(jax.ShapeDtypeStruct((ROWS, D), BF)...  43.2 us
    pallas_call x1, Pallas kernels, back(): pl.pallas_call(back_kernel, out_shape=(jax.ShapeDtypeStruct((8, 2048), f3...  40.8 us
    pallas_call x1, Pallas kernels, gather(): pl.pallas_call(gather_kernel, out_shape=(jax.ShapeDtypeStruct((4, 4, 4, 1...  38.8 us
    unnamed x10, local copies, waits for them, and re-layouts  4.55 us

profile of v5, /device:TPU:1, one launch (start us, length us, event | category | flops | bytes accessed | tf_op | source)
XLA Modules:
  0.0 130.5 jit_solution(6158531553322937764)
XLA Ops:
  0.6 1.2 maximum_convert_fusion.gain_ref.gain
  1.9 38.8 %gather_weights.1 = (bf16[4,4,4,16,3328]{4,3,2,1,0:T(8,128)(2,1)}, bf16[64,1024]{1,0:T(8,128)(2,1)}, bf16[32,1024]{1,0:T(8,128)(2,1)}, f32[8,128]{1,0:T(8,128)}) custom-call(bf16[8,2048]{1,0:T(8,128)(2,1)} %w_rows.1, bf16[8,1024]{1,0:T(8,128)(2,1)} %w_out_ref.1, bf16[8,31]{1,0:T(8,128)(2,1)} %kern_ref.1, f32[2,8]{1,0:T(2,128)} %maximum_convert_fusion.gain_ref.gain, ...), custom_call_target="tpu_custom_call" | custom-call | tf_op jit(solution)/shard_map/gather_weights/pallas_call | solution.py:210
  40.7 43.2 %block_pass.1 = (bf16[768,1024]{1,0:T(8,128)(2,1)}, bf16[768,1024]{1,0:T(8,128)(2,1)}, bf16[768,2048]{1,0:T(8,128)(2,1)}, bf16[1024,1280]{1,0:T(8,128)(2,1)}, f3...) custom-call(f32[8,128]{1,0:T(8,128)} %get-tuple-element.23.ids, f32[256,256]{1,0:T(8,128)} %constant.8.clone.basis, ...), custom_call_target="tpu_custom_call" | custom-call | tf_op jit(solution)/shard_map/block_pass/pallas_call | solution.py:853
  83.9 40.8 %back_and_scatter.1 = (f32[8,2048]{1,0:T(8,128)}, f32[8,1024]{1,0:T(8,128)}, f32[8,31]{1,0:T(8,128)}, f32[2,8]{1,0:T(2,128)}, bf16[768,1024]{1,0:T(8,128)(2,1)}) custom-call(bf16[4,4,4,16,1280]{4,3,2,1,0:T(8,128)(2,1)} %bitcast.20, bf16[768,1024]{1,0:T(8,128)(2,1)} %get-tuple-element.29.ln_hbm, bf16[768,2048]{1,0:T(8,128)(2,1)} %get-tuple-element.30.dpre_hbm, ...), custom_call_target="tpu_custom_call" | custom-call | tf_op jit(solution)/shard_map/back_and_scatter/pallas_call | solution.py:498
  124.7 1.3 slice_bitcast_fusion
  126.0 0.0 copy-start
  126.0 0.0 copy-start.1
  126.0 0.0 copy-start.2
  126.0 2.7 %copy.23 = bf16[1,768,1024]{2,1,0:T(8,128)(2,1)} copy(bf16[1,768,1024]{2,1,0:T(8,128)(2,1)} %bitcast.21) | data formatting | bytes 3145728
  128.7 0.0 copy-done
  128.7 0.6 copy.24
  129.3 0.0 copy-done.1
  129.3 0.6 copy.25
  129.9 0.0 copy-done.2
  129.9 0.6 copy.26
Async XLA Ops:
  126.0 2.7 %copy-start = (f32[8,2048]{1,0:T(8,128)S(1)}, f32[8,2048]{1,0:T(8,128)}, u32[]{:S(2)}) copy-start(f32[8,2048]{1,0:T(8,128)} %get-tuple-element.50) | copy-start | bytes 196612
  126.0 3.3 %copy-start.1 = (f32[8,1024]{1,0:T(8,128)S(1)}, f32[8,1024]{1,0:T(8,128)}, u32[]{:S(2)}) copy-start(f32[8,1024]{1,0:T(8,128)} %get-tuple-element.51) | copy-start | bytes 98308
  126.0 4.0 %copy-start.2 = (f32[8,31]{1,0:T(8,128)S(1)}, f32[8,31]{1,0:T(8,128)}, u32[]{:S(2)}) copy-start(f32[8,31]{1,0:T(8,128)} %get-tuple-element.52) | copy-start | bytes 2980

commit v6 on v5

--- a/solution.py
+++ b/solution.py
@@ -11,6 +11,7 @@
 MESH = pl.DeviceIdType.MESH
 HALFW = 1664
 WIDE = 2 * HALFW
+OUT_PARTS = ((0, 384), (384, 384), (768, 384), (1152, 128), (1280, 128), (1408, 256))
 PARTS = ((0, 384), (384, 384), (768, 256), (1024, 128), (1152, 256), (1408, 256))
 FIRST, SECOND = (0, 1, 2), (3, 4, 5)
 ORDERS = (("z", "x", "y"), ("x", "y", "z"), ("y", "z", "x")) * 2
@@ -59,9 +60,9 @@
 
 
 def gather_kernel(
-    w_in_ref, w_out_ref, kern_ref, gain_ref, seg_ref, frames_ref, cot_ref,
-    out_ref, hf_ref, hc_ref, ids_ref,
-    buf, shard, sib, segs, sib_sem, halo_send, halo_recv, a_send, a_recv, s_send, s_recv, out_sem,
+    w_in_ref, w_out_ref, kern_ref, gain_ref, seg_ref, spread, frames_ref, cot_ref,
+    out_ref, hc_ref, ln_hbm, glu_hbm, sig_hbm, inv_hbm, mean_hbm, gains, spec, table, across, counts,
+    buf, shard, sib, segs, xe, hat, ln, glu, sig, inv_in, mean_in, load_sem, store_sem, sib_sem, halo_send, halo_recv, a_send, a_recv, s_send, s_recv, out_sem,
 ):
     me, core = place()
     f32, bf = jnp.float32, jnp.bfloat16
@@ -72,16 +73,19 @@
     cross = dev(moved(me, "z", 2 * core - 1), 1 - core)
     targets = [dev(moved(me, a, b), core) for a in "yxz" for b in (1, -1, 2)] + [sibling, cross]
     greet(targets)
+    rows = frames_ref.shape[0]
+    load = pltpu.make_async_copy(frames_ref, xe.at[pl.ds(HALO, rows)], load_sem)
+    load.start()
     for c in (0, 1):
         at = c * HALFW
         shard[:, at : at + 1024] = w_in_ref[:, c * 1024 : c * 1024 + 1024].astype(f32)
-        shard[:, at + 1024 : at + 1536] = w_out_ref[:, c * 512 : c * 512 + 512].astype(f32)
-        shard[:, at + 1536 : at + HALFW] = jnp.zeros((8, 128), f32)
-    shard[:, 1536 : 1536 + 31] = kern_ref[...].astype(f32)
+        shard[:, at + 1024 : at + 1152] = jnp.zeros((8, 128), f32)
+        shard[:, at + 1152 : at + HALFW] = w_out_ref[:, c * 512 : c * 512 + 512].astype(f32)
+    shard[:, 1024 : 1024 + 31] = kern_ref[...].astype(f32)
     eye = lax.broadcasted_iota(jnp.int32, (8, 8), 0) == lax.broadcasted_iota(jnp.int32, (8, 8), 1)
     for n in (0, 1):
         row = jnp.broadcast_to(gain_ref[n : n + 1, :], (8, 8))
-        shard[:, 1567 + n : 1568 + n] = jnp.sum(jnp.where(eye, row, 0.0), axis=1, keepdims=True)
+        shard[:, 1055 + n : 1056 + n] = jnp.sum(jnp.where(eye, row, 0.0), axis=1, keepdims=True)
     greeted(targets)
 
     first = pltpu.make_async_remote_copy(
@@ -89,9 +93,8 @@
         device_id=sibling, device_id_type=MESH)
     first.start()
     halos = []
-    rows = frames_ref.shape[0]
-    for n, (src, dst, h) in enumerate(((frames_ref, hf_ref, HALO), (cot_ref, hc_ref, 16))):
-        for m, (at, to, who) in enumerate(((rows - h, 0, right), (0, h, left))):
+    for n, (src, dst, h, end) in enumerate(((frames_ref, xe, HALO, HALO + rows), (cot_ref, hc_ref, 16, 16))):
+        for m, (at, to, who) in enumerate(((rows - h, 0, right), (0, end, left))):
             halos.append(pltpu.make_async_remote_copy(
                 src_ref=src.at[pl.ds(at, h)], dst_ref=dst.at[pl.ds(to, h)],
                 send_sem=halo_send.at[n, m], recv_sem=halo_recv.at[n, m],
@@ -108,7 +111,7 @@
         [low, high], axis=0).astype(bf)
 
     def cols(p, c=core):
-        return pl.ds(pl.multiple_of(c * HALFW + PARTS[p][0], 128), PARTS[p][1])
+        return pl.ds(pl.multiple_of(c * HALFW + OUT_PARTS[p][0], 128), OUT_PARTS[p][1])
 
     def send(p, ph, which, idx, by):
         axis = ORDERS[p][ph]
@@ -168,42 +171,102 @@
             to_sibling(p, which, block(p, 2, by), 1 - core).wait_recv()
         flush(p, 1 - core, 1)
 
-    for ph in (0, 1):
-        for p in FIRST + SECOND:
-            start(p, ph)
-            if ph == 0 and p == 2:
-                for cp in halos:
-                    cp.start()
+    def strips(i, n):
+        return [pl.ds(pl.multiple_of(i * (16 * n) + 16 * u, 16), 16) for u in range(n)]
+
+    def normalise(lo, hi):
+        @pl.loop(lo, hi)
+        def _(i):
+            ats = strips(i, 4)
+            xs = [xe[at, :].astype(f32) for at in ats]
+            means = [row_mean(x) for x in xs]
+            cens = [x - m for x, m in zip(xs, means)]
+            invs = [lax.rsqrt(row_mean(c * c) + EPS) for c in cens]
+            for at, c, inv, m in zip(ats, cens, invs, means):
+                hat[at, :] = c * inv
+                inv_in[at, :] = jnp.broadcast_to(inv, (16, 128))
+                mean_in[at, :] = jnp.broadcast_to(m, (16, 128))
+
+    def keep(src, dst, n):
+        cp = pltpu.make_async_copy(src, dst, store_sem.at[n])
+        cp.start()
+        outs.append(cp)
+
+    for p in FIRST + SECOND:
+        start(p, 0)
+    for cp in halos:
+        cp.start()
+    load.wait()
+    for cp in halos:
+        cp.wait()
+    normalise(0, 4)
+    for p in FIRST + SECOND:
+        start(p, 1)
+    normalise(4, 10)
     for p in FIRST:
         start(p, 2)
+    normalise(10, 13)
+    inner = pl.ds(HALO, rows)
+    keep(inv_in.at[inner], inv_hbm, 0)
+    keep(mean_in.at[inner], mean_hbm, 1)
+    own = seg_ref[...]
+    before = jnp.where(seq == 0, jnp.broadcast_to(own[:, 0:1] - 1, (1, 128)), segs[0, :, 640:768])
+    after = jnp.where(seq == 7, jnp.broadcast_to(own[:, 767:768] + 1, (1, 128)), segs[1, :, 0:128])
+    ids = jnp.concatenate(
+        [before] + [own[:, n * 128 : n * 128 + 128] for n in range(6)] + [after], axis=0).astype(f32)
+    colours(ids, table, across, counts)
     for p in FIRST:
         pass_on(p)
     for p in SECOND:
         start(p, 2)
     for p in FIRST:
         finish(p)
-    for cp in halos:
-        cp.wait()
-    own = seg_ref[...]
-    before = jnp.where(seq == 0, jnp.broadcast_to(own[:, 0:1] - 1, (1, 128)), segs[0, :, 640:768])
-    after = jnp.where(seq == 7, jnp.broadcast_to(own[:, 767:768] + 1, (1, 128)), segs[1, :, 0:128])
-    ids_ref[...] = jnp.concatenate(
-        [before] + [own[:, n * 128 : n * 128 + 128] for n in range(6)] + [after], axis=0).astype(f32)
     for p in SECOND:
         pass_on(p)
     for p in FIRST:
         from_sibling(p)
+    taps = buf[:, :, :, :, 1024:1152].reshape(1024, 128).astype(f32).T
+    gains[0:8, :] = jnp.broadcast_to(taps[31:32, :], (8, 1024))
+    gains[8:16, :] = jnp.broadcast_to(taps[32:33, :], (8, 1024))
+
+    @pl.loop(0, 13)
+    def _(i):
+        for at in strips(i, 4):
+            ln[at, :] = (hat[at, :] * gains[0:1, :]).astype(bf)
+    keep(ln.at[inner], ln_hbm, 2)
+
+    def project(j):
+        col = slice(j * 256, j * 256 + 256)
+        w0 = buf[:, :, :, :, j * 256 : j * 256 + 256].reshape(1024, 256)
+        w1 = buf[:, :, :, :, HALFW + j * 256 : HALFW + j * 256 + 256].reshape(1024, 256)
+
+        @pl.loop(0, 2)
+        def _(r):
+            at = pl.ds(pl.multiple_of(r * 416, 16), 416)
+            lhs = ln[at, :]
+            value = mm(lhs, w0)
+            s = sigmoid(mm(lhs, w1))
+            glu[at, col] = (value * s).astype(bf)
+            sig[at, col] = s
+        keep(glu.at[:, col], glu_hbm.at[:, col], 3 + 2 * j)
+        keep(sig.at[inner, col], sig_hbm.at[:, col], 4 + 2 * j)
+
+    project(0)
     for p in SECOND:
         finish(p)
+    project(1)
+    project(2)
     for p in SECOND:
         from_sibling(p)
+    spec[...] = jnp.dot(spread[...], taps, precision=lax.Precision.HIGHEST, preferred_element_type=f32)
+    project(3)
     for cp in sends:
         cp.wait_send()
     for cp in outs:
         cp.wait()
 
 
-def gather(w_in, w_out, kern, gain, seg, frames, cot):
+def gather(w_in, w_out, kern, gain, seg, spread, frames, cot):
     bf = jnp.bfloat16
     vm = pl.BlockSpec(memory_space=pltpu.VMEM)
     hbm = pl.BlockSpec(memory_space=pltpu.HBM)
@@ -211,17 +274,34 @@
         gather_kernel,
         out_shape=(
             jax.ShapeDtypeStruct((4, 4, 4, 16, WIDE), bf),
-            jax.ShapeDtypeStruct((2 * HALO, 1024), bf),
             jax.ShapeDtypeStruct((32, 1024), bf),
-            jax.ShapeDtypeStruct((8, 128), jnp.float32),
+            jax.ShapeDtypeStruct((768, 1024), bf),
+            jax.ShapeDtypeStruct((832, 1024), bf),
+            jax.ShapeDtypeStruct((768, 1024), jnp.float32),
+            jax.ShapeDtypeStruct((768, 128), jnp.float32),
+            jax.ShapeDtypeStruct((768, 128), jnp.float32),
+            jax.ShapeDtypeStruct((16, 1024), jnp.float32),
+            jax.ShapeDtypeStruct((NFFT, 1024), jnp.float32),
+            jax.ShapeDtypeStruct((12, 8, NFFT), jnp.float32),
+            jax.ShapeDtypeStruct((8, NFFT, 128), jnp.float32),
+            jax.ShapeDtypeStruct((8, 128), jnp.int32),
         ),
-        in_specs=[vm, vm, vm, vm, vm, hbm, hbm],
-        out_specs=(hbm, vm, vm, vm),
+        in_specs=[vm, vm, vm, vm, vm, vm, hbm, hbm],
+        out_specs=(hbm, vm, hbm, hbm, hbm, hbm, hbm, vm, vm, vm, vm, vm),
         scratch_shapes=[
             pltpu.VMEM((4, 4, 4, 16, WIDE), bf),
             pltpu.VMEM((8, WIDE), jnp.float32),
             pltpu.VMEM((8, WIDE), jnp.float32),
             pltpu.VMEM((2, 1, 768), jnp.int32),
+            pltpu.VMEM((832, 1024), bf),
+            pltpu.VMEM((832, 1024), jnp.float32),
+            pltpu.VMEM((832, 1024), bf),
+            pltpu.VMEM((832, 1024), bf),
+            pltpu.VMEM((832, 1024), jnp.float32),
+            pltpu.VMEM((832, 128), jnp.float32),
+            pltpu.VMEM((832, 128), jnp.float32),
+            pltpu.SemaphoreType.DMA,
+            pltpu.SemaphoreType.DMA((11,)),
             pltpu.SemaphoreType.DMA((2,)),
             pltpu.SemaphoreType.DMA((3, 2)),
             pltpu.SemaphoreType.DMA((3, 2)),
@@ -234,7 +314,7 @@
         compiler_params=pltpu.CompilerParams(
             collective_id=0, has_side_effects=True, vmem_limit_bytes=60 << 20),
         name="gather_weights",
-    )(w_in, w_out, kern, gain, seg, frames, cot)
+    )(w_in, w_out, kern, gain, seg, spread, frames, cot)
 
 
 def back_kernel(
@@ -474,11 +554,11 @@
     for c in (0, 1):
         own = jnp.where(core == c, mine, theirs)
         o_in[:, c * 1024 : c * 1024 + 1024] = own[:, :1024]
-        o_out[:, c * 512 : c * 512 + 512] = own[:, 1024:1536]
+        o_out[:, c * 512 : c * 512 + 512] = own[:, 1152:1664]
         rows = w_rows[:, c * 1024 : c * 1024 + 1024].astype(f32)
         total = total + jnp.sum(rows * own[:, :1024], axis=-1, keepdims=True)
         if c == 0:
-            rest = own[:, 1536:]
+            rest = own[:, 1024:1152]
     eye = lax.broadcasted_iota(jnp.int32, (8, 8), 0) == lax.broadcasted_iota(jnp.int32, (8, 8), 1)
     column = jnp.sum(jnp.where(eye, jnp.broadcast_to(gain[0:1, :], (8, 8)), 0.0), axis=1, keepdims=True)
     o_kern[...] = rest[:, 0:31]
@@ -584,10 +664,9 @@
 FWD_AT, BWD_AT = (0, 208, 416, 592), (16, 208, 400, 592)
 
 
-def colours(ids, table, across):
+def colours(ids, table, across, counts):
     lane = lax.broadcasted_iota(jnp.int32, (1, 128), 1)
     wide = lax.broadcasted_iota(jnp.int32, (1, NFFT), 1)
-    counts = []
     for n, at in enumerate(FWD_AT + BWD_AT):
         length = 240 if n < 4 else 224
         r, o = divmod(at + 96, 128)
@@ -600,7 +679,7 @@
 
         own = jnp.concatenate([piece(r), piece(r + 1)], axis=1)
         step = jnp.where(wide < length - HALF, pltpu.roll(own, NFFT - HALF, 1) - own, 0.0)
-        count = jnp.max(step) + 1.0
+        count = jnp.max(step, axis=1, keepdims=True) + 1.0
         own = own + 1.0
         own = own - count * jnp.floor((own + 0.5) / count)
         own = jnp.where(wide < length, own, -1.0)
@@ -609,15 +688,13 @@
         across[n] = jnp.broadcast_to(rows.T[:, 0:1], (NFFT, 128))
         if n >= 4:
             table[n + 4] = jnp.where((wide >= 16) & (wide < 208), rows, -1.0)
-        counts.append(count.astype(jnp.int32))
-    return counts
+        counts[n : n + 1, :] = jnp.broadcast_to(count, (1, 128)).astype(jnp.int32)
 
 
 def mid_kernel(
-    ids, basis, turned, spread, back, frames, cot, hf, hc, w_hbm,
-    out_hbm, ln_hbm, dpre_hbm, early_hbm, inv_hbm, mean_hbm, gains,
-    xe, ce, w, ln, glu, sig, mixed, work, act, dm, dpre, g, spec, prod, extra, inv_in, mean_in,
-    table, across, counts, out, sems,
+    counts, gains, basis, turned, back, frames, cot, hc, w_hbm, glu_hbm, sig_hbm, spec_hbm, table_hbm, across_hbm,
+    out_hbm, dpre_hbm, early_hbm,
+    xe, ce, w, glu, sig, mixed, work, act, dm, dpre, g, spec, prod, extra, table, across, out, sems,
 ):
     scale = 1.0 / math.sqrt(98304.0)
 
@@ -628,70 +705,28 @@
 
     cols = lambda lo, n: (slice(None), pl.ds(lo, n))
     loads = [
-        cp(w_hbm.at[cols(1536, 128)], w.at[cols(3072, 128)], 0),
-        cp(hf.at[pl.ds(0, 32)], xe.at[pl.ds(0, 32)], 1),
-        cp(hf.at[pl.ds(32, 32)], xe.at[pl.ds(800, 32)], 2),
-        cp(frames, xe.at[pl.ds(32, ROWS)], 3),
-        cp(w_hbm.at[cols(0, 1024)], w.at[cols(0, 1024)], 4),
-        cp(w_hbm.at[cols(1664, 1024)], w.at[cols(1024, 1024)], 5),
-        cp(cot, ce.at[pl.ds(16, ROWS)], 6),
-        cp(hc.at[pl.ds(0, 16)], ce.at[pl.ds(0, 16)], 7),
-        cp(hc.at[pl.ds(16, 16)], ce.at[pl.ds(784, 16)], 8),
-        cp(w_hbm.at[cols(1024, 512)], w.at[cols(2048, 512)], 9),
-        cp(w_hbm.at[cols(2688, 512)], w.at[cols(2560, 512)], 10),
+        cp(table_hbm, table, 0),
+        cp(across_hbm, across, 1),
+        cp(spec_hbm, spec, 2),
+        cp(glu_hbm, glu.at[pl.ds(0, 832)], 3),
+        cp(cot, ce.at[pl.ds(16, ROWS)], 4),
+        cp(hc.at[pl.ds(0, 16)], ce.at[pl.ds(0, 16)], 5),
+        cp(hc.at[pl.ds(16, 16)], ce.at[pl.ds(784, 16)], 6),
+        cp(w_hbm.at[cols(1152, 512)], w.at[cols(0, 512)], 7),
+        cp(w_hbm.at[cols(2816, 512)], w.at[cols(512, 512)], 8),
+        cp(frames, xe, 9),
+        cp(sig_hbm, sig, 10),
     ]
-    for n, count in enumerate(colours(ids, table, across)):
-        counts[n] = count
-    loads[0].wait()
-    taps = w[:, 3072:3200].astype(F32).T
-    gains[0:8, :] = jnp.broadcast_to(taps[31:32, :], (8, D))
-    gains[8:16, :] = jnp.broadcast_to(taps[32:33, :], (8, D))
-    spec[...] = jnp.dot(spread[...], taps, precision=lax.Precision.HIGHEST, preferred_element_type=F32)
     glu[pl.ds(832, 16), :] = jnp.zeros((16, D), BF)
     dm[pl.ds(800, 32), :] = jnp.zeros((32, D), BF)
     prod[...] = jnp.zeros((NFFT, D), F32)
     extra[...] = jnp.zeros((128, D), F32)
-    for n in (1, 2, 3):
+    stores = []
+    for n in range(4):
         loads[n].wait()
 
     def strips(i, n, off=0):
         return [pl.ds(pl.multiple_of(i * (16 * n) + off + 16 * u, 16), 16) for u in range(n)]
-
-    @pl.loop(0, 13)
-    def _(i):
-        ats = strips(i, 4)
-        gain = gains[0:1, :]
-        xs = [xe[at, :].astype(F32) for at in ats]
-        means = [row_mean(x) for x in xs]
-        cens = [x - m for x, m in zip(xs, means)]
-        invs = [lax.rsqrt(row_mean(c * c) + EPS) for c in cens]
-        for at, c, inv, m in zip(ats, cens, invs, means):
-            ln[at, :] = (c * inv * gain).astype(BF)
-            inv_in[at, :] = jnp.broadcast_to(inv, (16, 128))
-            mean_in[at, :] = jnp.broadcast_to(m, (16, 128))
-
-    stores = [
-        cp(ln.at[pl.ds(32, ROWS)], ln_hbm, 11),
-        cp(inv_in.at[pl.ds(32, ROWS)], inv_hbm, 12),
-        cp(mean_in.at[pl.ds(32, ROWS)], mean_hbm, 13),
-    ]
-    loads[4].wait()
-    loads[5].wait()
-
-    @pl.loop(0, 8)
-    def _(i):
-        j, r = i // 2, i % 2
-        rows = pl.ds(pl.multiple_of(r * 416, 16), 416)
-        c0 = pl.ds(pl.multiple_of(j * 256, 256), 256)
-        c1 = pl.ds(pl.multiple_of(j * 256 + 1024, 256), 256)
-        lhs = ln[rows, :]
-        value = mm(lhs, w[:, c0])
-        s = sigmoid(mm(lhs, w[:, c1]))
-        glu[rows, c0] = (value * s).astype(BF)
-        sig[rows, c0] = s
-
-    for n in (6, 7, 8, 9, 10):
-        loads[n].wait()
 
     def picked(row, first, k):
         return jnp.concatenate(
@@ -770,12 +805,15 @@
 
     @pl.loop(0, 4)
     def _(wi):
-        by_class(forward, wi, counts[wi], 208, 208)
+        by_class(forward, wi, counts[wi, 0], 208, 208)
+
+    for n in range(4, 11):
+        loads[n].wait()
 
     @pl.loop(0, 4)
     def _(j):
         col = pl.ds(pl.multiple_of(j * 256, 256), 256)
-        work[:, col] = nt(ce[...], w[col, 2048:3072])
+        work[:, col] = nt(ce[...], w[col, :])
 
     def mid_rows(ats, central):
         gain = gains[8:9, :]
@@ -808,26 +846,26 @@
     @pl.loop(0, 4)
     def _(j):
         col = pl.ds(pl.multiple_of(j * 256, 256), 256)
-        y = mm(act[16:784, :], w[:, pl.ds(pl.multiple_of(2048 + j * 256, 256), 256)])
-        out[:, col] = (xe[32:800, col].astype(F32) + y).astype(BF)
+        y = mm(act[16:784, :], w[:, col])
+        out[:, col] = (xe[:, col].astype(F32) + y).astype(BF)
         lhs = act[16:784, col].T
         r = (mm(lhs, ce[16:784, :]) * scale).astype(BF)
-        g[col, 0:512] = r[:, :512]
-        g[col, 640:1152] = r[:, 512:]
-
-    stores.append(cp(out, out_hbm, 14))
+        g[col, 128:640] = r[:, :512]
+        g[col, 768:1280] = r[:, 512:]
+
+    stores.append(cp(out, out_hbm, 11))
 
     @pl.loop(0, 4)
     def _(wi):
-        by_class(backward, wi, counts[4 + wi], 192, 192)
+        by_class(backward, wi, counts[4 + wi, 0], 192, 192)
 
     gk = jnp.dot(back[...], prod[...], precision=lax.Precision.HIGHEST, preferred_element_type=F32)
     extra[0:31, :] = gk[0:31]
     g_mid = jnp.sum(extra[40:48, :], axis=0, keepdims=True)
     extra[32:33, :] = g_mid
-    g[:, 512:640] = (extra[...].T * scale).astype(BF)
-    g[:, 1152:1280] = jnp.zeros((D, 128), BF)
-    stores.append(cp(g, early_hbm, 15))
+    g[:, 0:128] = (extra[...].T * scale).astype(BF)
+    g[:, 640:768] = jnp.zeros((D, 128), BF)
+    stores.append(cp(g, early_hbm, 12))
 
     for q in range(4):
         @pl.loop(q * 6, q * 6 + 6)
@@ -836,17 +874,17 @@
                 at = pl.ds(pl.multiple_of(i * 32 + 16 * u, 16), 16)
                 ext = pl.ds(pl.multiple_of(i * 32 + 16 * u + 32, 16), 16)
                 d = mixed[at, :]
-                s = sig[ext, :]
+                s = sig[at, :]
                 dpre[at, :1024] = (d * s).astype(BF)
                 dpre[at, 1024:] = (d * glu[ext, :].astype(F32) * (1.0 - s)).astype(BF)
 
         part = pl.ds(q * 192, 192)
-        stores.append(cp(dpre.at[part], dpre_hbm.at[part], 16 + q))
+        stores.append(cp(dpre.at[part], dpre_hbm.at[part], 13 + q))
     for s in stores:
         s.wait()
 
 
-def mid(ids, consts, frames, cot, hf, hc, w):
+def mid(counts, gains, consts, *rest):
     vm = pl.BlockSpec(memory_space=pltpu.VMEM)
     hbm = pl.BlockSpec(memory_space=pltpu.HBM)
     V = pltpu.VMEM
@@ -854,35 +892,33 @@
         mid_kernel,
         out_shape=(
             jax.ShapeDtypeStruct((ROWS, D), BF),
-            jax.ShapeDtypeStruct((ROWS, D), BF),
             jax.ShapeDtypeStruct((ROWS, 2 * D), BF),
             jax.ShapeDtypeStruct((D, 1280), BF),
-            jax.ShapeDtypeStruct((ROWS, 128), F32),
-            jax.ShapeDtypeStruct((ROWS, 128), F32),
-            jax.ShapeDtypeStruct((16, D), F32),
         ),
-        in_specs=[vm, vm, vm, vm, vm, hbm, hbm, hbm, hbm, hbm],
-        out_specs=(hbm,) * 6 + (vm,),
+        in_specs=[pl.BlockSpec(memory_space=pltpu.SMEM), vm, vm, vm, vm] + [hbm] * 9,
+        out_specs=(hbm,) * 3,
         scratch_shapes=[
-            V((832, D), BF), V((800, D), BF), V((D, 3200), BF),
-            V((832, D), BF), V((848, D), BF), V((832, D), F32),
+            V((768, D), BF), V((800, D), BF), V((D, D), BF),
+            V((848, D), BF), V((768, D), F32),
             V((800, D), F32), V((800, D), F32), V((800, D), BF), V((832, D), BF),
             V((768, 2 * D), BF), V((D, 1280), BF), V((NFFT, D), F32), V((NFFT, D), F32),
-            V((128, D), F32), V((832, 128), F32), V((832, 128), F32),
-            V((12, 8, NFFT), F32), V((8, NFFT, 128), F32), pltpu.SMEM((8,), jnp.int32), V((ROWS, D), BF),
-            pltpu.SemaphoreType.DMA((20,)),
+            V((128, D), F32), V((12, 8, NFFT), F32), V((8, NFFT, 128), F32), V((ROWS, D), BF),
+            pltpu.SemaphoreType.DMA((17,)),
         ],
         compiler_params=pltpu.CompilerParams(vmem_limit_bytes=60 << 20),
         name="block_pass",
-    )(ids, *consts, frames, cot, hf, hc, w)
+    )(counts, gains, *consts, *rest)
 
 
 def shards(frames, cotangent, segments, w_in, w_out, kernel, gain_in, gain_mid):
     gain = jnp.stack([gain_in, gain_mid]).astype(F32)
     x, cot = frames[0], cotangent[0]
-    full, f_halo, c_halo, ids = gather(w_in, w_out, kernel, gain, segments, x, cot)
+    basis, turned, spread, back_table = tables()
+    full, c_halo, ln, glu, sig, inv, mean, gains, spec, table, across, counts = gather(
+        w_in, w_out, kernel, gain, segments, spread, x, cot)
     full = full.reshape(D, WIDE)
-    block_out, ln, dpre, early, inv, mean, gains = mid(ids, tables(), x, cot, f_halo, c_halo, full)
+    block_out, dpre, early = mid(
+        counts, gains, (basis, turned, back_table), x, cot, c_halo, full, glu, sig, spec, table, across)
     g_in, g_out, g_kern, g_vec, input_grad = back(
         early.reshape(4, 4, 4, 16, 1280), ln, dpre, full, x, cot, inv, mean, gains, w_in, gain)
     return (block_out[None], input_grad[None], g_in, g_out, g_kern, g_vec[0], g_vec[1])

time: 131 us -> 129 us (0.985)
  Pallas kernels: 123 us -> 121 us
    pallas_call x1, Pallas kernels: 43.2 us -> 34.5 us  [mid(): pl.pallas_call(mid_kernel, out_shape=(jax.ShapeDtypeStruct((ROWS, D), BF)...]
    pallas_call x1, Pallas kernels: 38.8 us -> 44.9 us  [gather(): pl.pallas_call(gather_kernel, out_shape=(jax.ShapeDtypeStruct((4, 4, 4, 1...]
where the time goes in v6:
time: 129 us
  Pallas kernels  121 us (94%)
  local copies, waits for them, and re-layouts  5.8 us (4%)
    pallas_call x1, Pallas kernels, gather(): pl.pallas_call(gather_kernel, out_shape=(jax.ShapeDtypeStruct((4, 4, 4, 1...  44.9 us
    pallas_call x1, Pallas kernels, back(): pl.pallas_call(back_kernel, out_shape=(jax.ShapeDtypeStruct((8, 2048), f3...  41.9 us
    pallas_call x1, Pallas kernels, mid(): pl.pallas_call(mid_kernel, out_shape=(jax.ShapeDtypeStruct((ROWS, D), BF)...  34.5 us
    unnamed x10, local copies, waits for them, and re-layouts  4.55 us

profile of v6, /device:TPU:1, one launch (start us, length us, event | category | flops | bytes accessed | tf_op | source)
XLA Modules:
  0.0 129.1 jit_solution(3469540338165415646)
XLA Ops:
  0.6 1.2 maximum_convert_fusion.gain_ref.gain
  1.9 44.9 %gather_weights.1 = (bf16[4,4,4,16,3328]{4,3,2,1,0:T(8,128)(2,1)}, bf16[32,1024]{1,0:T(8,128)(2,1)}, bf16[768,1024]{1,0:T(8,128)(2,1)}, bf16[832,1024]{1,0:T(8,1...) custom-call(bf16[8,2048]{1,0:T(8,128)(2,1)} %w_rows.1, ...), custom_call_target="tpu_custom_call" | custom-call | tf_op jit(solution)/shard_map/gather_weights/pallas_call | solution.py:273
  46.8 34.5 %block_pass.1 = (bf16[768,1024]{1,0:T(8,128)(2,1)}, bf16[768,2048]{1,0:T(8,128)(2,1)}, bf16[1024,1280]{1,0:T(8,128)(2,1)}) custom-call(s32[8,128]{1,0:T(8,128)} %get-tuple-element.27.counts, f32[16,1024]{1,0:T(8,128)} %get-tuple-element.28.gains, f32[256,256]{1,0:T(8,128)} %constant.8.clone.basis, f32[256,256]{1,0:T(8,128)} %constant.9.clone.turned, ...), custom_call_target="tpu_custom_call" | custom-call | tf_op jit(solution)/shard_map/block_pass/pallas_call | solution.py:891
  81.4 41.9 %back_and_scatter.1 = (f32[8,2048]{1,0:T(8,128)}, f32[8,1024]{1,0:T(8,128)}, f32[8,31]{1,0:T(8,128)}, f32[2,8]{1,0:T(2,128)}, bf16[768,1024]{1,0:T(8,128)(2,1)}) custom-call(bf16[4,4,4,16,1280]{4,3,2,1,0:T(8,128)(2,1)} %bitcast.20, bf16[768,1024]{1,0:T(8,128)(2,1)} %get-tuple-element.38.ln_hbm, bf16[768,2048]{1,0:T(8,128)(2,1)} %get-tuple-element.39.dpre_hbm, ...), custom_call_target="tpu_custom_call" | custom-call | tf_op jit(solution)/shard_map/back_and_scatter/pallas_call | solution.py:578
  123.3 1.3 slice_bitcast_fusion
  124.6 0.0 copy-start
  124.6 0.0 copy-start.1
  124.6 0.0 copy-start.2
  124.6 2.7 %copy.23 = bf16[1,768,1024]{2,1,0:T(8,128)(2,1)} copy(bf16[1,768,1024]{2,1,0:T(8,128)(2,1)} %bitcast.21) | data formatting | bytes 3145728
  127.3 0.0 copy-done
  127.3 0.6 copy.24
  127.9 0.0 copy-done.1
  127.9 0.6 copy.25
  128.5 0.0 copy-done.2
  128.5 0.6 copy.26
Async XLA Ops:
  124.6 2.7 %copy-start = (f32[8,2048]{1,0:T(8,128)S(1)}, f32[8,2048]{1,0:T(8,128)}, u32[]{:S(2)}) copy-start(f32[8,2048]{1,0:T(8,128)} %get-tuple-element.58) | copy-start | bytes 196612
  124.6 3.3 %copy-start.1 = (f32[8,1024]{1,0:T(8,128)S(1)}, f32[8,1024]{1,0:T(8,128)}, u32[]{:S(2)}) copy-start(f32[8,1024]{1,0:T(8,128)} %get-tuple-element.59) | copy-start | bytes 98308
  124.6 4.0 %copy-start.2 = (f32[8,31]{1,0:T(8,128)S(1)}, f32[8,31]{1,0:T(8,128)}, u32[]{:S(2)}) copy-start(f32[8,31]{1,0:T(8,128)} %get-tuple-element.60) | copy-start | bytes 2980

commit v7 on v6

--- a/solution.py
+++ b/solution.py
@@ -197,15 +197,16 @@
     for cp in halos:
         cp.start()
     load.wait()
+    normalise(1, 4)
+    for p in FIRST + SECOND:
+        start(p, 1)
+    normalise(4, 12)
+    for p in FIRST:
+        start(p, 2)
     for cp in halos:
         cp.wait()
-    normalise(0, 4)
-    for p in FIRST + SECOND:
-        start(p, 1)
-    normalise(4, 10)
-    for p in FIRST:
-        start(p, 2)
-    normalise(10, 13)
+    for n in (0, 12):
+        normalise(n, n + 1)
     inner = pl.ds(HALO, rows)
     keep(inv_in.at[inner], inv_hbm, 0)
     keep(mean_in.at[inner], mean_hbm, 1)
@@ -221,8 +222,6 @@
         start(p, 2)
     for p in FIRST:
         finish(p)
-    for p in SECOND:
-        pass_on(p)
     for p in FIRST:
         from_sibling(p)
     taps = buf[:, :, :, :, 1024:1152].reshape(1024, 128).astype(f32).T
@@ -251,14 +250,16 @@
         keep(glu.at[:, col], glu_hbm.at[:, col], 3 + 2 * j)
         keep(sig.at[inner, col], sig_hbm.at[:, col], 4 + 2 * j)
 
+    for p in SECOND:
+        pass_on(p)
     project(0)
+    project(1)
     for p in SECOND:
         finish(p)
-    project(1)
     project(2)
+    spec[...] = jnp.dot(spread[...], taps, precision=lax.Precision.HIGHEST, preferred_element_type=f32)
     for p in SECOND:
         from_sibling(p)
-    spec[...] = jnp.dot(spread[...], taps, precision=lax.Precision.HIGHEST, preferred_element_type=f32)
     project(3)
     for cp in sends:
         cp.wait_send()
@@ -783,7 +784,7 @@
             else:
                 mixed[pl.ds(base, 192), col] = y
 
-    def by_class(run, wi, count, length, step):
+    def by_class(run, wi, count):
         zero = jnp.int32(0)
 
         @pl.when(count <= 2)
@@ -796,16 +797,15 @@
 
         @pl.when(count > 3)
         def _():
-            base = pl.multiple_of(jnp.minimum(wi * step, 592), 16)
-            mixed[pl.ds(base, length), :] = jnp.zeros((length, D), F32)
-
-            @pl.loop(0, (count + 3) // 4)
+            run(wi, zero, 4, False)
+
+            @pl.loop(0, (count - 3) // 2)
             def _(n):
-                run(wi, n * 4, 4, True)
+                run(wi, 4 + n * 2, 2, True)
 
     @pl.loop(0, 4)
     def _(wi):
-        by_class(forward, wi, counts[wi, 0], 208, 208)
+        by_class(forward, wi, counts[wi, 0])
 
     for n in range(4, 11):
         loads[n].wait()
@@ -839,9 +839,9 @@
 
     mid_rows([pl.ds(0, 16), pl.ds(784, 16)], False)
 
-    @pl.loop(0, 24)
+    @pl.loop(0, 12)
     def _(i):
-        mid_rows(strips(i, 2, 16), True)
+        mid_rows(strips(i, 4, 16), True)
 
     @pl.loop(0, 4)
     def _(j):
@@ -857,7 +857,7 @@
 
     @pl.loop(0, 4)
     def _(wi):
-        by_class(backward, wi, counts[4 + wi, 0], 192, 192)
+        by_class(backward, wi, counts[4 + wi, 0])
 
     gk = jnp.dot(back[...], prod[...], precision=lax.Precision.HIGHEST, preferred_element_type=F32)
     extra[0:31, :] = gk[0:31]

time: 129 us -> 123 us (0.953)
  Pallas kernels: 121 us -> 115 us
    pallas_call x1, Pallas kernels: 44.9 us -> 41.2 us  [gather(): pl.pallas_call(gather_kernel, out_shape=(jax.ShapeDtypeStruct((4, 4, 4, 1...]
    pallas_call x1, Pallas kernels: 34.5 us -> 31 us  [mid(): pl.pallas_call(mid_kernel, out_shape=(jax.ShapeDtypeStruct((ROWS, D), BF)...]
where the time goes in v7:
time: 123 us
  Pallas kernels  115 us (93%)
  local copies, waits for them, and re-layouts  5.8 us (5%)
  other arithmetic  1.24 us (1%)
    pallas_call x1, Pallas kernels, back(): pl.pallas_call(back_kernel, out_shape=(jax.ShapeDtypeStruct((8, 2048), f3...  42.7 us
    pallas_call x1, Pallas kernels, gather(): pl.pallas_call(gather_kernel, out_shape=(jax.ShapeDtypeStruct((4, 4, 4, 1...  41.2 us
    pallas_call x1, Pallas kernels, mid(): pl.pallas_call(mid_kernel, out_shape=(jax.ShapeDtypeStruct((ROWS, D), BF)...  31 us
    unnamed x10, local copies, waits for them, and re-layouts  4.55 us

profile of v7, /device:TPU:1, one launch (start us, length us, event | category | flops | bytes accessed | tf_op | source)
XLA Modules:
  0.0 122.7 jit_solution(12764500413692514370)
XLA Ops:
  0.6 1.2 %maximum_convert_fusion.gain_ref.gain = f32[2,8]{1,0:T(2,128)} fusion(bf16[1,8]{1,0:T(2,128)(2,1)} %bitcast.22, bf16[1,8]{1,0:T(2,128)(2,1)} %bitcast.23), kind=kLoop, calls=%fused_computation | loop fusion | flops 64 | bytes 96 | tf_op jit(solution)/shard_map/convert_element_type | solution.py:914
  1.9 41.2 %gather_weights.1 = (bf16[4,4,4,16,3328]{4,3,2,1,0:T(8,128)(2,1)}, bf16[32,1024]{1,0:T(8,128)(2,1)}, bf16[768,1024]{1,0:T(8,128)(2,1)}, bf16[832,1024]{1,0:T(8,1...) custom-call(bf16[8,2048]{1,0:T(8,128)(2,1)} %w_rows.1, ...), custom_call_target="tpu_custom_call" | custom-call | tf_op jit(solution)/shard_map/gather_weights/pallas_call | solution.py:274
  43.1 31.0 %block_pass.1 = (bf16[768,1024]{1,0:T(8,128)(2,1)}, bf16[768,2048]{1,0:T(8,128)(2,1)}, bf16[1024,1280]{1,0:T(8,128)(2,1)}) custom-call(s32[8,128]{1,0:T(8,128)} %get-tuple-element.27.counts, f32[16,1024]{1,0:T(8,128)} %get-tuple-element.28.gains, f32[256,256]{1,0:T(8,128)} %constant.8.clone.basis, f32[256,256]{1,0:T(8,128)} %constant.9.clone.turned, ...), custom_call_target="tpu_custom_call" | custom-call | tf_op jit(solution)/shard_map/block_pass/pallas_call | solution.py:891
  74.1 42.7 %back_and_scatter.1 = (f32[8,2048]{1,0:T(8,128)}, f32[8,1024]{1,0:T(8,128)}, f32[8,31]{1,0:T(8,128)}, f32[2,8]{1,0:T(2,128)}, bf16[768,1024]{1,0:T(8,128)(2,1)}) custom-call(bf16[4,4,4,16,1280]{4,3,2,1,0:T(8,128)(2,1)} %bitcast.20, bf16[768,1024]{1,0:T(8,128)(2,1)} %get-tuple-element.38.ln_hbm, bf16[768,2048]{1,0:T(8,128)(2,1)} %get-tuple-element.39.dpre_hbm, ...), custom_call_target="tpu_custom_call" | custom-call | tf_op jit(solution)/shard_map/back_and_scatter/pallas_call | solution.py:579
  116.9 1.3 %slice_bitcast_fusion = (f32[8]{0:T(128)}, f32[8]{0:T(128)}) fusion(f32[2,8]{1,0:T(2,128)} %get-tuple-element.46), kind=kLoop, calls=%fused_computation.1 | loop fusion | bytes 128 | tf_op jit(solution)/shard_map/squeeze | solution.py:924
  118.1 0.0 copy-start
  118.1 0.0 copy-start.1
  118.1 0.0 copy-start.2
  118.1 2.7 %copy.23 = bf16[1,768,1024]{2,1,0:T(8,128)(2,1)} copy(bf16[1,768,1024]{2,1,0:T(8,128)(2,1)} %bitcast.21) | data formatting | bytes 3145728
  120.8 0.0 copy-done
  120.8 0.6 copy.24
  121.5 0.0 copy-done.1
  121.5 0.6 copy.25
  122.1 0.0 copy-done.2
  122.1 0.6 copy.26
Async XLA Ops:
  118.1 2.7 %copy-start = (f32[8,2048]{1,0:T(8,128)S(1)}, f32[8,2048]{1,0:T(8,128)}, u32[]{:S(2)}) copy-start(f32[8,2048]{1,0:T(8,128)} %get-tuple-element.58) | copy-start | bytes 196612
  118.1 3.3 %copy-start.1 = (f32[8,1024]{1,0:T(8,128)S(1)}, f32[8,1024]{1,0:T(8,128)}, u32[]{:S(2)}) copy-start(f32[8,1024]{1,0:T(8,128)} %get-tuple-element.59) | copy-start | bytes 98308
  118.1 4.0 %copy-start.2 = (f32[8,31]{1,0:T(8,128)S(1)}, f32[8,31]{1,0:T(8,128)}, u32[]{:S(2)}) copy-start(f32[8,31]{1,0:T(8,128)} %get-tuple-element.60) | copy-start | bytes 2980

commit v8 on v7

--- a/solution.py
+++ b/solution.py
@@ -239,12 +239,13 @@
         w0 = buf[:, :, :, :, j * 256 : j * 256 + 256].reshape(1024, 256)
         w1 = buf[:, :, :, :, HALFW + j * 256 : HALFW + j * 256 + 256].reshape(1024, 256)
 
-        @pl.loop(0, 2)
-        def _(r):
-            at = pl.ds(pl.multiple_of(r * 416, 16), 416)
-            lhs = ln[at, :]
-            value = mm(lhs, w0)
-            s = sigmoid(mm(lhs, w1))
+        pairs = []
+        for r in (0, 1):
+            lhs = ln[r * 416 : r * 416 + 416, :]
+            pairs.append((mm(lhs, w0), mm(lhs, w1)))
+        for r, (value, gate) in enumerate(pairs):
+            at = slice(r * 416, r * 416 + 416)
+            s = sigmoid(gate)
             glu[at, col] = (value * s).astype(bf)
             sig[at, col] = s
         keep(glu.at[:, col], glu_hbm.at[:, col], 3 + 2 * j)
@@ -448,12 +449,17 @@
             for which in range(3):
                 go(send_full(p, ph + 1, which))
 
-    def product(p, half, store):
+    def product(p, half, store, fresh=False):
         at, width = PARTS[p]
 
         @pl.loop(0, 4)
         def _(y):
-            lhs = turned[pl.ds(pl.multiple_of(y * 256, 256), 256), :]
+            some = pl.ds(pl.multiple_of(y * 256, 256), 256)
+            if fresh:
+                lhs = ln[:, some].T
+                turned[some, :] = lhs
+            else:
+                lhs = turned[some, :]
             rhs = dpre[:, pl.ds(pl.multiple_of(half * 1024 + at, 128), width)]
             r = jnp.dot(lhs, rhs, preferred_element_type=f32) * scale
             store(y, r.reshape(4, 4, 16, width))
@@ -461,7 +467,7 @@
     def for_sibling(p):
         def store(y, r):
             gsend[y, :, :, :, lanes(p)] = r.astype(bf)
-        product(p, 1 - core, store)
+        product(p, 1 - core, store, fresh=p == 0)
 
     def for_own(p):
         give(p).wait_recv()
@@ -489,7 +495,6 @@
                 out[at, :] = (ce[at, :].astype(f32) + inv * (u - a - n * b)).astype(bf)
 
     loads[0].wait()
-    turned[...] = ln[...].T
     loads[1].wait()
     for_sibling(0)
     greeted(targets)
@@ -740,33 +745,58 @@
         return jnp.concatenate(
             [jnp.where(own == (first + c).astype(F32), turned[lo:hi, :], 0.0) for c in range(k)], axis=1).astype(BF)
 
+    def staged(spectrum, filtered, put):
+        x = [spectrum(0)]
+        y = None
+        for j in range(4):
+            if j < 3:
+                x.append(spectrum(j + 1))
+            new = filtered(j, x[j])
+            if y is not None:
+                put(j - 1, y)
+            y = new
+        put(3, y)
+
     def forward(wi, first, k, add):
         base = pl.multiple_of(jnp.minimum(wi * 208, 592), 16)
         to = picked(wi, first, k)
         fro = placed(wi, first, k, 16, 224)
-        for j in range(4):
+
+        def spectrum(j):
+            return mm(to, glu[pl.ds(base, 256), j * 256 : j * 256 + 256])
+
+        def filtered(j, x):
             col = slice(j * 256, j * 256 + 256)
-            x = mm(to, glu[pl.ds(base, 256), col])
             hr, hi = spec[:128, col], spec[128:, col]
             ys = []
             for c in range(k):
                 xr, xi = x[256 * c : 256 * c + 128], x[256 * c + 128 : 256 * c + 256]
                 ys += [(xr * hr - xi * hi).astype(BF), (xr * hi + xi * hr).astype(BF)]
-            y = mm(fro, jnp.concatenate(ys, axis=0))
+            return jnp.concatenate(ys, axis=0)
+
+        def put(j, y):
+            col = slice(j * 256, j * 256 + 256)
+            y = mm(fro, y)
             if add:
                 mixed[pl.ds(base, 208), col] += y
             else:
                 mixed[pl.ds(base, 208), col] = y
+
+        staged(spectrum, filtered, put)
 
     def backward(wi, first, k, add):
         base = pl.multiple_of(wi * 192, 16)
         to = picked(4 + wi, first, k)
         mid_to = picked(8 + wi, first, k)
         fro = placed(4 + wi, first, k, 16, 208)
-        for j in range(4):
+
+        def spectrum(j):
             col = slice(j * 256, j * 256 + 256)
-            d = mm(to, dm[pl.ds(base, 256), col])
-            q = mm(mid_to, glu[pl.ds(base + 16, 256), col])
+            return mm(to, dm[pl.ds(base, 256), col]), mm(mid_to, glu[pl.ds(base + 16, 256), col])
+
+        def filtered(j, pair):
+            d, q = pair
+            col = slice(j * 256, j * 256 + 256)
             hr, hi = spec[:128, col], spec[128:, col]
             ys = []
             pr, pi = prod[:128, col], prod[128:, col]
@@ -778,11 +808,17 @@
                 pi = pi + (qi * dr - qr * di)
             prod[:128, col] = pr
             prod[128:, col] = pi
-            y = mm(fro, jnp.concatenate(ys, axis=0))
+            return jnp.concatenate(ys, axis=0)
+
+        def put(j, y):
+            col = slice(j * 256, j * 256 + 256)
+            y = mm(fro, y)
             if add:
                 mixed[pl.ds(base, 192), col] += y
             else:
                 mixed[pl.ds(base, 192), col] = y
+
+        staged(spectrum, filtered, put)
 
     def by_class(run, wi, count):
         zero = jnp.int32(0)

time: 123 us -> 120 us (0.976)
  Pallas kernels: 115 us -> 112 us
    pallas_call x1, Pallas kernels: 31 us -> 28.3 us  [mid(): pl.pallas_call(mid_kernel, out_shape=(jax.ShapeDtypeStruct((ROWS, D), BF)...]
where the time goes in v8:
time: 120 us
  Pallas kernels  112 us (93%)
  local copies, waits for them, and re-layouts  5.8 us (5%)
  other arithmetic  1.24 us (1%)
    pallas_call x1, Pallas kernels, back(): pl.pallas_call(back_kernel, out_shape=(jax.ShapeDtypeStruct((8, 2048), f3...  42.9 us
    pallas_call x1, Pallas kernels, gather(): pl.pallas_call(gather_kernel, out_shape=(jax.ShapeDtypeStruct((4, 4, 4, 1...  40.6 us
    pallas_call x1, Pallas kernels, mid(): pl.pallas_call(mid_kernel, out_shape=(jax.ShapeDtypeStruct((ROWS, D), BF)...  28.3 us
    unnamed x10, local copies, waits for them, and re-layouts  4.55 us

profile of v8, /device:TPU:1, one launch (start us, length us, event | category | flops | bytes accessed | tf_op | source)
XLA Modules:
  0.0 119.6 jit_solution(16239490817855998918)
XLA Ops:
  0.6 1.2 %maximum_convert_fusion.gain_ref.gain = f32[2,8]{1,0:T(2,128)} fusion(bf16[1,8]{1,0:T(2,128)(2,1)} %bitcast.22, bf16[1,8]{1,0:T(2,128)(2,1)} %bitcast.23), kind=kLoop, calls=%fused_computation | loop fusion | flops 64 | bytes 96 | tf_op jit(solution)/shard_map/convert_element_type | solution.py:950
  1.9 40.6 %gather_weights.1 = (bf16[4,4,4,16,3328]{4,3,2,1,0:T(8,128)(2,1)}, bf16[32,1024]{1,0:T(8,128)(2,1)}, bf16[768,1024]{1,0:T(8,128)(2,1)}, bf16[832,1024]{1,0:T(8,1...) custom-call(bf16[8,2048]{1,0:T(8,128)(2,1)} %w_rows.1, ...), custom_call_target="tpu_custom_call" | custom-call | tf_op jit(solution)/shard_map/gather_weights/pallas_call | solution.py:275
  42.5 28.3 %block_pass.1 = (bf16[768,1024]{1,0:T(8,128)(2,1)}, bf16[768,2048]{1,0:T(8,128)(2,1)}, bf16[1024,1280]{1,0:T(8,128)(2,1)}) custom-call(s32[8,128]{1,0:T(8,128)} %get-tuple-element.27.counts, f32[16,1024]{1,0:T(8,128)} %get-tuple-element.28.gains, f32[256,256]{1,0:T(8,128)} %constant.8.clone.basis, f32[256,256]{1,0:T(8,128)} %constant.9.clone.turned, ...), custom_call_target="tpu_custom_call" | custom-call | tf_op jit(solution)/shard_map/block_pass/pallas_call | solution.py:927
  70.9 42.9 %back_and_scatter.1 = (f32[8,2048]{1,0:T(8,128)}, f32[8,1024]{1,0:T(8,128)}, f32[8,31]{1,0:T(8,128)}, f32[2,8]{1,0:T(2,128)}, bf16[768,1024]{1,0:T(8,128)(2,1)}) custom-call(bf16[4,4,4,16,1280]{4,3,2,1,0:T(8,128)(2,1)} %bitcast.20, bf16[768,1024]{1,0:T(8,128)(2,1)} %get-tuple-element.38.ln_hbm, bf16[768,2048]{1,0:T(8,128)(2,1)} %get-tuple-element.39.dpre_hbm, ...), custom_call_target="tpu_custom_call" | custom-call | tf_op jit(solution)/shard_map/back_and_scatter/pallas_call | solution.py:584
  113.8 1.3 %slice_bitcast_fusion = (f32[8]{0:T(128)}, f32[8]{0:T(128)}) fusion(f32[2,8]{1,0:T(2,128)} %get-tuple-element.46), kind=kLoop, calls=%fused_computation.1 | loop fusion | bytes 128 | tf_op jit(solution)/shard_map/squeeze | solution.py:960
  115.1 0.0 copy-start
  115.1 0.0 copy-start.1
  115.1 0.0 copy-start.2
  115.1 2.7 %copy.23 = bf16[1,768,1024]{2,1,0:T(8,128)(2,1)} copy(bf16[1,768,1024]{2,1,0:T(8,128)(2,1)} %bitcast.21) | data formatting | bytes 3145728
  117.8 0.0 copy-done
  117.8 0.6 copy.24
  118.4 0.0 copy-done.1
  118.4 0.6 copy.25
  119.0 0.0 copy-done.2
  119.0 0.6 copy.26
Async XLA Ops:
  115.1 2.7 %copy-start = (f32[8,2048]{1,0:T(8,128)S(1)}, f32[8,2048]{1,0:T(8,128)}, u32[]{:S(2)}) copy-start(f32[8,2048]{1,0:T(8,128)} %get-tuple-element.58) | copy-start | bytes 196612
  115.1 3.3 %copy-start.1 = (f32[8,1024]{1,0:T(8,128)S(1)}, f32[8,1024]{1,0:T(8,128)}, u32[]{:S(2)}) copy-start(f32[8,1024]{1,0:T(8,128)} %get-tuple-element.59) | copy-start | bytes 98308
  115.1 4.0 %copy-start.2 = (f32[8,31]{1,0:T(8,128)S(1)}, f32[8,31]{1,0:T(8,128)}, u32[]{:S(2)}) copy-start(f32[8,31]{1,0:T(8,128)} %get-tuple-element.60) | copy-start | bytes 2980

commit v9 on v8

--- a/solution.py
+++ b/solution.py
@@ -496,9 +496,9 @@
 
     loads[0].wait()
     loads[1].wait()
-    for_sibling(0)
     greeted(targets)
     go(give(3))
+    for_sibling(0)
     go(give(0))
     for_sibling(1)
     go(give(1))

time: 120 us -> 116 us (0.967)
  Pallas kernels: 112 us -> 108 us
    pallas_call x1, Pallas kernels: 42.9 us -> 38.8 us  [back(): pl.pallas_call(back_kernel, out_shape=(jax.ShapeDtypeStruct((8, 2048), f3...]
where the time goes in v9:
time: 116 us
  Pallas kernels  108 us (93%)
  local copies, waits for them, and re-layouts  5.8 us (5%)
  other arithmetic  1.24 us (1%)
    pallas_call x1, Pallas kernels, gather(): pl.pallas_call(gather_kernel, out_shape=(jax.ShapeDtypeStruct((4, 4, 4, 1...  40.6 us
    pallas_call x1, Pallas kernels, back(): pl.pallas_call(back_kernel, out_shape=(jax.ShapeDtypeStruct((8, 2048), f3...  38.8 us
    pallas_call x1, Pallas kernels, mid(): pl.pallas_call(mid_kernel, out_shape=(jax.ShapeDtypeStruct((ROWS, D), BF)...  28.3 us
    unnamed x10, local copies, waits for them, and re-layouts  4.55 us

profile of v9, /device:TPU:1, one launch (start us, length us, event | category | flops | bytes accessed | tf_op | source)
XLA Modules:
  0.0 115.5 jit_solution(6470342161748891302)
XLA Ops:
  0.6 1.2 %maximum_convert_fusion.gain_ref.gain = f32[2,8]{1,0:T(2,128)} fusion(bf16[1,8]{1,0:T(2,128)(2,1)} %bitcast.22, bf16[1,8]{1,0:T(2,128)(2,1)} %bitcast.23), kind=kLoop, calls=%fused_computation | loop fusion | flops 64 | bytes 96 | tf_op jit(solution)/shard_map/convert_element_type | solution.py:950
  1.9 40.6 %gather_weights.1 = (bf16[4,4,4,16,3328]{4,3,2,1,0:T(8,128)(2,1)}, bf16[32,1024]{1,0:T(8,128)(2,1)}, bf16[768,1024]{1,0:T(8,128)(2,1)}, bf16[832,1024]{1,0:T(8,1...) custom-call(bf16[8,2048]{1,0:T(8,128)(2,1)} %w_rows.1, ...), custom_call_target="tpu_custom_call" | custom-call | tf_op jit(solution)/shard_map/gather_weights/pallas_call | solution.py:275
  42.5 28.3 %block_pass.1 = (bf16[768,1024]{1,0:T(8,128)(2,1)}, bf16[768,2048]{1,0:T(8,128)(2,1)}, bf16[1024,1280]{1,0:T(8,128)(2,1)}) custom-call(s32[8,128]{1,0:T(8,128)} %get-tuple-element.27.counts, f32[16,1024]{1,0:T(8,128)} %get-tuple-element.28.gains, f32[256,256]{1,0:T(8,128)} %constant.8.clone.basis, f32[256,256]{1,0:T(8,128)} %constant.9.clone.turned, ...), custom_call_target="tpu_custom_call" | custom-call | tf_op jit(solution)/shard_map/block_pass/pallas_call | solution.py:927
  70.9 38.8 %back_and_scatter.1 = (f32[8,2048]{1,0:T(8,128)}, f32[8,1024]{1,0:T(8,128)}, f32[8,31]{1,0:T(8,128)}, f32[2,8]{1,0:T(2,128)}, bf16[768,1024]{1,0:T(8,128)(2,1)}) custom-call(bf16[4,4,4,16,1280]{4,3,2,1,0:T(8,128)(2,1)} %bitcast.20, bf16[768,1024]{1,0:T(8,128)(2,1)} %get-tuple-element.38.ln_hbm, bf16[768,2048]{1,0:T(8,128)(2,1)} %get-tuple-element.39.dpre_hbm, ...), custom_call_target="tpu_custom_call" | custom-call | tf_op jit(solution)/shard_map/back_and_scatter/pallas_call | solution.py:584
  109.7 1.3 %slice_bitcast_fusion = (f32[8]{0:T(128)}, f32[8]{0:T(128)}) fusion(f32[2,8]{1,0:T(2,128)} %get-tuple-element.46), kind=kLoop, calls=%fused_computation.1 | loop fusion | bytes 128 | tf_op jit(solution)/shard_map/squeeze | solution.py:960
  111.0 0.0 copy-start
  111.0 0.0 copy-start.1
  111.0 0.0 copy-start.2
  111.0 2.7 %copy.23 = bf16[1,768,1024]{2,1,0:T(8,128)(2,1)} copy(bf16[1,768,1024]{2,1,0:T(8,128)(2,1)} %bitcast.21) | data formatting | bytes 3145728
  113.7 0.0 copy-done
  113.7 0.6 copy.24
  114.3 0.0 copy-done.1
  114.3 0.6 copy.25
  114.9 0.0 copy-done.2
  114.9 0.6 copy.26
Async XLA Ops:
  111.0 2.7 %copy-start = (f32[8,2048]{1,0:T(8,128)S(1)}, f32[8,2048]{1,0:T(8,128)}, u32[]{:S(2)}) copy-start(f32[8,2048]{1,0:T(8,128)} %get-tuple-element.58) | copy-start | bytes 196612
  111.0 3.3 %copy-start.1 = (f32[8,1024]{1,0:T(8,128)S(1)}, f32[8,1024]{1,0:T(8,128)}, u32[]{:S(2)}) copy-start(f32[8,1024]{1,0:T(8,128)} %get-tuple-element.59) | copy-start | bytes 98308
  111.0 4.0 %copy-start.2 = (f32[8,31]{1,0:T(8,128)S(1)}, f32[8,31]{1,0:T(8,128)}, u32[]{:S(2)}) copy-start(f32[8,31]{1,0:T(8,128)} %get-tuple-element.60) | copy-start | bytes 2980
